TPU v7x, 256 devices: a whole 4x4x8 slice. The times are simulated.
256 devices in a mesh: seq: 16 (over x_hi, y, core), grp: 16 (over x_lo, z).
Axes of the slice: x: 4 (x_hi: 2, x_lo: 2; x = x_hi * 2 + x_lo), y: 4, z: 8, core: 2. Of those that a mesh axis runs over, the one named last changes fastest.
Arguments:
- gate_in: bfloat16 [8192, 8192], P('seq', 'grp'), may hold values from 0.5 to 1.5
- key_in: bfloat16 [8192, 8192], P('seq', 'grp'), may hold values from -12 to 12, as said below
- value_in: bfloat16 [8192, 8192], P('seq', 'grp'), may hold values from 0.5 to 1.5
- filt_in: bfloat16 [8192, 8192], P('seq', 'grp'), may hold values from -1 to 1
- skip_gain: float32 [8192], P('grp'), may hold values from -3 to 3
- running_gram: float32 [8192, 8192], P('seq', 'grp'), may hold values from -2 to 2
Outputs:
- gram: float32 [8192, 8192], P('seq', 'grp')
Inputs may be any that keep to these rules, and one draw needn't show every extreme that they name: `key_in`: each row (token) is a value shared by all channels of that token plus independent per-channel parts.
All inputs are finite; a program needn't handle non-finite values.
Results may differ from a plain program's by a relative error of at most 0.0012.
Values may be sent and summed in bfloat16 or wider, within the bound.
No kernel may reach another device: no remote copies, remote signals or barrier semaphores. Data moves between devices by JAX's collectives and lax.ppermute only.
A program may use at most 128 MiB of HBM per device.

v0:
```python
import math

import jax
import jax.numpy as jnp
from jax import lax
from jax.sharding import PartitionSpec as P


def angle_table(rows, cols, modulus):
    left = jnp.arange(rows, dtype=jnp.int32)
    right = jnp.arange(cols, dtype=jnp.int32)
    turned = left[:, None] * right[None, :] % modulus
    angle = turned.astype(jnp.float32) * (2.0 * math.pi / modulus)
    return (jnp.cos(angle), jnp.sin(angle))


def spectrum(signal, tables):
    c_one, s_one, t_cos, t_sin, c_blk, s_blk = tables
    chans, length = signal.shape
    grid = signal.reshape(chans, length // 128, 128)
    s_re = jnp.einsum("ka,cab->ckb", c_one, grid, preferred_element_type=jnp.float32)
    s_im = -jnp.einsum("ka,cab->ckb", s_one, grid, preferred_element_type=jnp.float32)
    t_re = (s_re * t_cos + s_im * t_sin).astype(jnp.bfloat16)
    t_im = (s_im * t_cos - s_re * t_sin).astype(jnp.bfloat16)
    x_re = jnp.dot(t_re, c_blk, preferred_element_type=jnp.float32) + jnp.dot(
        t_im, s_blk, preferred_element_type=jnp.float32
    )
    x_im = jnp.dot(t_im, c_blk, preferred_element_type=jnp.float32) - jnp.dot(
        t_re, s_blk, preferred_element_type=jnp.float32
    )
    return (x_re, x_im)


def inverse(p_re, p_im, tables):
    c_one, s_one, t_cos, t_sin, c_blk, s_blk = tables
    chans = p_re.shape[0]
    width = p_re.shape[1]
    q_re = jnp.dot(p_re, c_blk, preferred_element_type=jnp.float32) - jnp.dot(
        p_im, s_blk, preferred_element_type=jnp.float32
    )
    q_im = jnp.dot(p_im, c_blk, preferred_element_type=jnp.float32) + jnp.dot(
        p_re, s_blk, preferred_element_type=jnp.float32
    )
    r_re = (q_re * t_cos - q_im * t_sin).astype(jnp.bfloat16)
    r_im = (q_im * t_cos + q_re * t_sin).astype(jnp.bfloat16)
    result = jnp.einsum("ka,ckb->cab", c_one, r_re, preferred_element_type=jnp.float32)
    result = result - jnp.einsum("ka,ckb->cab", s_one, r_im, preferred_element_type=jnp.float32)
    return (result * (1.0 / (width * 128))).reshape(chans, width * 64)


def local(gate_in, key_in, value_in, filt_in, skip_gain, running_gram):
    mixed = (key_in.astype(jnp.float32) * value_in.astype(jnp.float32)).astype(jnp.bfloat16).T
    seq_index = lax.axis_index("seq")
    owned, owned_filt, owned_gate = (
        lax.all_to_all(mixed, "seq", split_axis=0, concat_axis=1, tiled=True),
        lax.all_to_all(filt_in.T, "seq", split_axis=0, concat_axis=1, tiled=True),
        lax.all_to_all(gate_in.T, "seq", split_axis=0, concat_axis=1, tiled=True),
    )
    chans, length = owned.shape
    half = length // 128
    c_one, s_one = angle_table(2 * half, half, 2 * half)
    t_cos, t_sin = angle_table(2 * half, 128, 2 * length)
    c_blk, s_blk = angle_table(128, 128, 128)
    tables = (
        c_one.astype(jnp.bfloat16),
        s_one.astype(jnp.bfloat16),
        t_cos,
        t_sin,
        c_blk.astype(jnp.bfloat16),
        s_blk.astype(jnp.bfloat16),
    )
    skips = lax.dynamic_slice_in_dim(skip_gain, seq_index * chans, chans, 0)
    u_re, u_im = spectrum(owned, tables)
    f_re, f_im = spectrum(owned_filt, tables)
    p_re = (u_re * f_re - u_im * f_im).astype(jnp.bfloat16)
    p_im = (u_re * f_im + u_im * f_re).astype(jnp.bfloat16)
    conv = inverse(p_re, p_im, tables)
    mixed_out = (conv + skips[:, None] * owned.astype(jnp.float32)).astype(jnp.bfloat16)
    gated_own = (owned_gate.astype(jnp.float32) * mixed_out.astype(jnp.float32)).astype(
        jnp.bfloat16
    )
    home = lax.all_to_all(gated_own, "seq", split_axis=1, concat_axis=0, tiled=True)
    every = lax.all_gather(home, "grp", axis=0, tiled=True)
    partial_sum = (
        lax.dot_general(every, home, (((1,), (1,)), ((), ())), preferred_element_type=jnp.float32)
        / length
    )
    tile = lax.psum_scatter(partial_sum, "seq", scatter_dimension=0, tiled=True)
    return running_gram + tile


def solution(mesh):
    in_specs = (
        P("seq", "grp"),
        P("seq", "grp"),
        P("seq", "grp"),
        P("seq", "grp"),
        P("grp"),
        P("seq", "grp"),
    )
    out_specs = P("seq", "grp")
    return jax.shard_map(local, mesh=mesh, in_specs=in_specs, out_specs=out_specs, check_vma=False)
```

profile of v0, /device:TPU:1, one launch (start us, length us, event | category | flops | bytes accessed | tf_op | source)
XLA Modules:
  0.0 359.2 jit_solution(13219544227760748040)
XLA Ops:
  6.5 1.3 copy.23
  7.8 1.3 copy.24
  9.1 0.9 multiply_convert_fusion
  10.0 8.6 %all-to-all-start.1 = ((bf16[16,32,512]{2,1,0:T(8,128)(2,1)}), bf16[16,32,512]{2,1,0:T(8,128)(2,1)S(1)}, u32[]{:S(2)}, u32[]{:S(2)}) async-start(bf16[16,32,512]{2,1,0:T(8,128)(2,1)} %bitcast.4), calls=%async_computation.1 | async-start | bytes 1048576 | tf_op jit(solution)/shard_map/all_to_all | solution.py:55
  18.6 1.0 copy.30
  19.6 10.3 %all-to-all-done.1 = bf16[16,32,512]{2,1,0:T(8,128)(2,1)S(1)} async-done(((bf16[16,32,512]{2,1,0:T(8,128)(2,1)}), bf16[16,32,512]{2,1,0:T(8,128)(2,1)S(1)}, u32[]{:S(2)}, u32[]{:S(2)}) %all-to-all-start.1) | async-done | bytes 524320 | tf_op jit(solution)/shard_map/all_to_all | solution.py:55
  29.9 4.5 %all-to-all-start.2 = ((bf16[16,32,512]{2,1,0:T(8,128)(2,1)}), bf16[16,32,512]{2,1,0:T(8,128)(2,1)S(1)}, u32[]{:S(2)}, u32[]{:S(2)}) async-start(bf16[16,32,512]{2,1,0:T(8,128)(2,1)} %bitcast.13), calls=%async_computation.2 | async-start | bytes 1048576 | tf_op jit(solution)/shard_map/all_to_all | solution.py:56
  34.9 1.0 copy.22
  35.9 0.8 dynamic_slice.3
  37.3 8.5 %all-to-all-done.2 = bf16[16,32,512]{2,1,0:T(8,128)(2,1)S(1)} async-done(((bf16[16,32,512]{2,1,0:T(8,128)(2,1)}), bf16[16,32,512]{2,1,0:T(8,128)(2,1)S(1)}, u32[]{:S(2)}, u32[]{:S(2)}) %all-to-all-start.2) | async-done | bytes 524320 | tf_op jit(solution)/shard_map/all_to_all | solution.py:56
  45.8 4.5 %all-to-all-start = ((bf16[16,32,512]{2,1,0:T(8,128)(2,1)}), bf16[16,32,512]{2,1,0:T(8,128)(2,1)S(1)}, u32[]{:S(2)}, u32[]{:S(2)}) async-start(bf16[16,32,512]{2,1,0:T(8,128)(2,1)} %bitcast.1), calls=%async_computation | async-start | bytes 1048576 | tf_op jit(solution)/shard_map/all_to_all | solution.py:57
  51.8 1.0 fusion.7
  52.8 0.7 fusion.41
  53.4 0.7 fusion.45
  54.1 0.7 convolution_subtract_fusion.1
  54.8 0.7 convolution_add_fusion.1
  56.0 0.9 fusion.1
  57.0 0.7 fusion.47
  57.7 0.7 fusion.43
  58.3 0.7 convolution_add_fusion.2
  59.0 1.2 subtract_convert_fusion.1
  60.2 0.7 fusion.39
  60.9 0.7 fusion.37
  61.6 0.7 convolution_subtract_fusion
  62.4 0.7 convolution_add_fusion
  63.7 0.9 fusion.5
  64.8 0.7 fusion.9
  65.5 18.5 %all_to_all.61 = bf16[32,16,512]{2,0,1:T(8,128)(2,1)} all-to-all(bf16[32,16,512]{2,0,1:T(8,128)(2,1)S(1)} %fusion.9), channel_id=1, replica_groups=mesh['seq'=16,'grp'=16] {'seq'}, dimensions={1} | all-to-all | bytes 1048576 | tf_op jit(solution)/shard_map/all_to_all | solution.py:82
  84.1 100.3 %all-gather.2.cloned.1.call-done = bf16[8192,512]{1,0:T(8,128)(2,1)} async-done(((bf16[512,512]{1,0:T(8,128)(2,1)}), bf16[8192,512]{1,0:T(8,128)(2,1)}) %all-gather.2.cloned.1.call-update) | async-done | bytes 8388624 | tf_op jit(solution)/shard_map/all_gather | solution.py:83
  184.4 13.7 %convolution_multiply_fusion = f32[8192,512]{1,0:T(8,128)} fusion(bf16[8192,512]{1,0:T(8,128)(2,1)} %all-gather.2.cloned.1.call-done, bf16[512,512]{1,0:T(8,128)(2,1)} %bitcast.94), kind=kOutput, calls=%fused_computation | convolution fusion | flops 4299161600 | bytes 25690112 | tf_op jit(solution)/shard_map/dot_general | solution.py:85
  198.2 151.8 %reduce-scatter.2.cloned.1.call-done = f32[512,512]{1,0:T(8,128)} async-done(((f32[8192,512]{1,0:T(8,128)}), f32[512,512]{1,0:T(8,128)}) %reduce-scatter.2.cloned.1.call-update) | async-done | bytes 1048592 | tf_op jit(solution)/shard_map/reduce_scatter | solution.py:88
  349.9 2.4 add.123
  (22 shorter events, 4.0 us)
Async XLA Ops:
  7.8 10.8 %copy-start.1 = (bf16[512,512]{1,0:T(8,128)(2,1)S(1)}, bf16[512,512]{1,0:T(8,128)(2,1)}, u32[]{:S(2)}) copy-start(bf16[512,512]{1,0:T(8,128)(2,1)} %param.9) | copy-start | bytes 1572868
  10.0 24.9 %copy-start.2 = (bf16[512,512]{1,0:T(8,128)(2,1)S(1)}, bf16[512,512]{1,0:T(8,128)(2,1)}, u32[]{:S(2)}) copy-start(bf16[512,512]{1,0:T(8,128)(2,1)} %param.6) | copy-start | bytes 1572868
  10.0 19.9 %all-to-all-start.1 = ((bf16[16,32,512]{2,1,0:T(8,128)(2,1)}), bf16[16,32,512]{2,1,0:T(8,128)(2,1)S(1)}, u32[]{:S(2)}, u32[]{:S(2)}) async-start(bf16[16,32,512]{2,1,0:T(8,128)(2,1)} %bitcast.4), calls=%async_computation.1 | async-start | bytes 1048576 | tf_op jit(solution)/shard_map/all_to_all | solution.py:55
  29.9 15.9 %all-to-all-start.2 = ((bf16[16,32,512]{2,1,0:T(8,128)(2,1)}), bf16[16,32,512]{2,1,0:T(8,128)(2,1)S(1)}, u32[]{:S(2)}, u32[]{:S(2)}) async-start(bf16[16,32,512]{2,1,0:T(8,128)(2,1)} %bitcast.13), calls=%async_computation.2 | async-start | bytes 1048576 | tf_op jit(solution)/shard_map/all_to_all | solution.py:56
  45.8 19.0 %all-to-all-start = ((bf16[16,32,512]{2,1,0:T(8,128)(2,1)}), bf16[16,32,512]{2,1,0:T(8,128)(2,1)S(1)}, u32[]{:S(2)}, u32[]{:S(2)}) async-start(bf16[16,32,512]{2,1,0:T(8,128)(2,1)} %bitcast.1), calls=%async_computation | async-start | bytes 1048576 | tf_op jit(solution)/shard_map/all_to_all | solution.py:57
  50.4 134.0 %all-gather.2.cloned.1.call-start = ((), (), s32[]{:S(2)}) async-start(), calls=%async_computation.5 | async-start | bytes 8912896 | tf_op jit(solution)/shard_map/all_gather | solution.py:83
  84.0 265.9 %reduce-scatter.2.cloned.1.call-start = ((), (), s32[]{:S(2)}) async-start(), calls=%async_computation.6 | async-start | bytes 17825792 | tf_op jit(solution)/shard_map/reduce_scatter | solution.py:88
  198.1 151.8 %copy-start = (f32[512,512]{1,0:T(8,128)S(1)}, f32[512,512]{1,0:T(8,128)}, u32[]{:S(2)}) copy-start(f32[512,512]{1,0:T(8,128)} %param.11) | copy-start | bytes 3145732
Sparse Core Ops, SparseCore 0:
  84.1 100.2 all-gather.1
  198.3 151.6 reduce-scatter.1
where the time goes:
time: 360 us; the launch traced here: 359 us
  waiting for transfers between devices  271 us (75%)
  matrix products  27.1 us (8%)
  blocking collectives  18.5 us (5%)
  starting transfers between devices  17.9 us (5%)
  between operations  13.6 us (4%)
  local copies, waits for them, and re-layouts  6.9 us (2%)
  other arithmetic  4.29 us (1%)
    reduce_scatter x1, waiting for transfers between devices, local(): tile = lax.psum_scatter(partial_sum, 'seq', scatter_dimension=0, tiled=True)  152 us
    all_gather x1, waiting for transfers between devices, local(): every = lax.all_gather(home, 'grp', axis=0, tiled=True)  100 us
    all_to_all x1, blocking collectives, local(): lax.all_to_all(gated_own, 'seq', split_axis=1, concat_axis=0, tiled=True)  18.5 us
    dot_general x1, matrix products, local(): lax.dot_general(every, home, (((1,), (1,)), ((), ())), preferred_element_...  13.7 us
    all_to_all x1, waiting for transfers between devices, local(): lax.all_to_all(mixed, 'seq', split_axis=0, concat_axis=1, tiled=True)  10.3 us
    all_to_all x1, starting transfers between devices, local(): lax.all_to_all(mixed, 'seq', split_axis=0, concat_axis=1, tiled=True)  8.58 us
    all_to_all x1, waiting for transfers between devices, local(): lax.all_to_all(filt_in.T, 'seq', split_axis=0, concat_axis=1, tiled=True)  8.52 us
  transfers between devices with their start and end apart: 5, of which 4 were waited for; matrix products, arithmetic and copies ran while one was open for 5% of the time, Pallas kernels for 0%

commit v1 on v0

v1 whole, which is shorter than its diff:
```python
import functools
import math

import jax
import jax.numpy as jnp
import numpy as np
from jax import lax
from jax.experimental import pallas as pl
from jax.experimental.pallas import tpu as pltpu
from jax.sharding import PartitionSpec as P

BF = jnp.bfloat16
F32 = jnp.float32
MESH = ("seq", "grp")
VMEM = pl.BlockSpec(memory_space=pltpu.VMEM)
SMEM = pl.BlockSpec(memory_space=pltpu.SMEM)
MIB = 1024 * 1024


def coords(seq, grp):
    return 2 * (seq // 8) + grp // 8, (seq // 2) % 4, seq % 2, grp % 8


def device(x, y, core, z):
    return (8 * (x // 2) + 2 * y + core) * 16 + 8 * (x % 2) + z


def move(array, target):
    pairs = []
    for seq in range(16):
        for grp in range(16):
            pairs.append((16 * seq + grp, device(*target(*coords(seq, grp)))))
    return lax.ppermute(array, MESH, pairs)


def along_x(array, step):
    return move(array, lambda x, y, c, z: ((x + step) % 4, y, c, z))


def along_y(array, step):
    return move(array, lambda x, y, c, z: (x, (y + step) % 4, c, z))


def along_z(array, step):
    return move(array, lambda x, y, c, z: (x, y, c, (z + step) % 8))


def other_core(array):
    return move(array, lambda x, y, c, z: (x, y, 1 - c, z))


def other_x_lo(array):
    return move(array, lambda x, y, c, z: (x ^ 1, y, c, z))


def to_rows(array, first):
    def target(x, y, c, z):
        h, p = x // 2, x % 2
        return 2 * p + (h if first else 1 - h), z // 2, c, 2 * ((y - z // 2) % 4) + (z + h) % 2

    return move(array, target)


def phase(*arrays):
    return lax.optimization_barrier(arrays)


def angles(rows, cols, modulus):
    turned = (np.arange(rows)[:, None] * np.arange(cols)[None, :]) % modulus
    angle = turned.astype(np.float32) * np.float32(2.0 * math.pi / modulus)
    return np.cos(angle), np.sin(angle)


def tables():
    c_one, s_one = angles(128, 64, 128)
    order = np.array([4 * s + q for q in range(4) for s in range(16)])
    c_one, s_one = c_one[:, order], s_one[:, order]
    t_cos, t_sin = angles(128, 128, 16384)
    c_blk, s_blk = angles(128, 128, 128)
    first = np.concatenate([c_one, s_one], 0)
    last = np.concatenate([c_one.T, -s_one.T], 1) / 16384.0
    fwd = np.block([[c_blk, -s_blk], [s_blk, c_blk]])
    bwd = np.block([[c_blk, s_blk], [-s_blk, c_blk]])
    as_bf = [jnp.asarray(t, dtype=F32).astype(BF) for t in (first, last, fwd, bwd)]
    return (*as_bf, jnp.asarray(t_cos, dtype=F32), jnp.asarray(t_sin, dtype=F32))


def prepare_kernel(gate, key, value, filt, out):
    row = lax.broadcasted_iota(jnp.int32, (128, 128), 0)
    col = lax.broadcasted_iota(jnp.int32, (128, 128), 1)
    eye = (row == col).astype(BF)
    mixed = (key[...].astype(F32) * value[...].astype(F32)).astype(BF)
    for place, block in enumerate((mixed, filt[...], gate[...])):
        turned = lax.dot_general(
            eye, block, (((1,), (1,)), ((), ())), preferred_element_type=F32
        ).astype(BF)
        for j in range(4):
            out[j, 32 * place : 32 * place + 32, :] = turned[32 * j : 32 * j + 32, :]


def prepare(gate, key, value, filt):
    block = pl.BlockSpec((512, 128), lambda i: (0, i))
    return pl.pallas_call(
        prepare_kernel,
        grid=(4,),
        in_specs=[block] * 4,
        out_specs=pl.BlockSpec((4, 96, 512), lambda i: (i, 0, 0)),
        out_shape=jax.ShapeDtypeStruct((16, 96, 512), BF),
        name="prepare",
    )(gate, key, value, filt)


GROUP = 8


def conv_kernel(
    where, skip, data, first, last, fwd, bwd, t_cos, t_sin, keep_same, keep_other, send, grid, done
):
    for arr in range(3):
        for half in range(2):
            lo = 32 * arr + 16 * half
            block = data[:, lo : lo + 16, :].astype(F32)
            block = jnp.swapaxes(block, 0, 1).astype(BF)
            for i in range(16):
                for q in range(4):
                    grid[16 * q : 16 * q + 16, (lo + i) * 128 : (lo + i + 1) * 128] = block[
                        i, :, 128 * q : 128 * q + 128
                    ]
    tc = t_cos[...]
    ts = t_sin[...]

    def group(g, carry):
        lanes = pl.ds(pl.multiple_of(g * (GROUP * 128), GROUP * 128), GROUP * 128)
        f_lanes = pl.ds(pl.multiple_of(4096 + g * (GROUP * 128), GROUP * 128), GROUP * 128)
        g_lanes = pl.ds(pl.multiple_of(8192 + g * (GROUP * 128), GROUP * 128), GROUP * 128)
        spectra = []
        for where_lanes in (lanes, f_lanes):
            s = jnp.dot(first[...], grid[:, where_lanes], preferred_element_type=F32)
            rows = []
            for i in range(GROUP):
                s_re = s[:128, 128 * i : 128 * i + 128]
                s_im = -s[128:, 128 * i : 128 * i + 128]
                t_re = (s_re * tc + s_im * ts).astype(BF)
                t_im = (s_im * tc - s_re * ts).astype(BF)
                rows.append(jnp.concatenate([t_re, t_im], 1))
            spectra.append(
                jnp.dot(jnp.concatenate(rows, 0), fwd[...], preferred_element_type=F32)
            )
        u, f = spectra
        u_re, u_im, f_re, f_im = u[:, :128], u[:, 128:], f[:, :128], f[:, 128:]
        p_re = (u_re * f_re - u_im * f_im).astype(BF)
        p_im = (u_re * f_im + u_im * f_re).astype(BF)
        qq = jnp.dot(
            jnp.concatenate([p_re, p_im], 1), bwd[...], preferred_element_type=F32
        )
        cols = []
        for i in range(GROUP):
            q_re = qq[128 * i : 128 * i + 128, :128]
            q_im = qq[128 * i : 128 * i + 128, 128:]
            r_re = (q_re * tc - q_im * ts).astype(BF)
            r_im = (q_im * tc + q_re * ts).astype(BF)
            cols.append(jnp.concatenate([r_re, r_im], 0))
        conv = jnp.dot(last[...], jnp.concatenate(cols, 1), preferred_element_type=F32)
        signal = grid[:, lanes].astype(F32)
        gates = grid[:, g_lanes].astype(F32)
        for i in range(GROUP):
            part = slice(128 * i, 128 * i + 128)
            mixed_out = conv[:, part] + skip[g * GROUP + i] * signal[:, part]
            gated = gates[:, part] * mixed_out.astype(BF).astype(F32)
            done[g * GROUP + i] = gated
        return carry

    lax.fori_loop(0, 32 // GROUP, group, 0)
    core = where[2]
    x_lo = where[0] % 2

    def quarter(lo, part):
        rows = pl.ds(pl.multiple_of(part * 16, 16), 16)
        return jnp.swapaxes(done[lo : lo + 16, rows, :], 0, 1).astype(BF)

    for lo in (0, 16):
        keep_same[:, lo : lo + 16, :] = quarter(lo, 2 * x_lo + core)
        keep_other[:, lo : lo + 16, :] = quarter(lo, 2 * (1 - x_lo) + core)
        send[0, :, lo : lo + 16, :] = quarter(lo, 2 * x_lo + 1 - core)
        send[1, :, lo : lo + 16, :] = quarter(lo, 2 * (1 - x_lo) + 1 - core)


def convolve(where, skips, data):
    piece = jax.ShapeDtypeStruct((16, 32, 128), BF)
    return pl.pallas_call(
        conv_kernel,
        in_specs=[SMEM, SMEM] + [VMEM] * 7,
        out_specs=[VMEM] * 3,
        out_shape=[piece, piece, jax.ShapeDtypeStruct((2, 16, 32, 128), BF)],
        scratch_shapes=[pltpu.VMEM((64, 96 * 128), BF), pltpu.VMEM((32, 64, 128), F32)],
        compiler_params=pltpu.CompilerParams(vmem_limit_bytes=14 * MIB),
        cost_estimate=pl.CostEstimate(
            flops=4 * 10**9, bytes_accessed=3 * 10**6, transcendentals=0
        ),
        name="convolve",
    )(where, skips, data, *tables())


def columns_kernel(where, *refs):
    y, core, first_x, second_x = where[1], where[2], where[4], where[5]
    own, below, above, far_low, far_high, right = refs
    for j, from_x in enumerate((first_x, second_x)):
        for step in (0, -1, 1, 2):
            from_y = (y + step + 4) % 4
            base = 32 * (8 * (from_x // 2) + 2 * from_y)
            for rel in range(2):
                row = pl.ds(pl.multiple_of(base + 32 * ((core + rel) % 2), 32), 32)
                if step == 2:
                    piece = (far_low, far_high)[rel].at[j, 0]
                else:
                    piece = {0: own, -1: below, 1: above}[step].at[j, rel]
                for a in range(16):
                    right[row, 128 * a : 128 * a + 128] = piece[a]


def columns(where, *shards):
    return pl.pallas_call(
        columns_kernel,
        in_specs=[SMEM] + [VMEM] * len(shards),
        out_specs=VMEM,
        out_shape=jax.ShapeDtypeStruct((512, 2048), BF),
        compiler_params=pltpu.CompilerParams(vmem_limit_bytes=12 * MIB),
        cost_estimate=pl.CostEstimate(flops=0, bytes_accessed=4 * 10**6, transcendentals=0),
        name="columns",
    )(where, *shards)


def gram_kernel(steps, n_right, where, *refs):
    rows = 64 * len(steps)
    rights, shard_refs = refs[:n_right], refs[n_right:-3]
    keep, send, left = refs[-3:]
    x, core, z = where[0], where[2], where[3]
    shards = []
    for ref in shard_refs:
        shards += [(ref, j) for j in range(2)] if ref.shape[0] == 2 else [(ref, 0)]
    for n, (ref, j) in enumerate(shards):
        h = (x + n) % 2
        source = (z + steps[n // 2] + 8) % 8
        slot = (source + h + core) % 2
        for rel in range(2):
            row = rows * slot + 64 * (n // 2) + 32 * ((core + rel) % 2)
            row = pl.multiple_of(row, 32)
            for a in range(16):
                left[pl.ds(row, 32), 128 * a : 128 * a + 128] = ref[j, rel, a]
    for half, right in enumerate(rights):
        for sub in range(2):
            lanes = slice(256 * sub, 256 * sub + 256)
            part = lax.dot_general(
                left[...],
                right[lanes, :],
                (((1,), (1,)), ((), ())),
                preferred_element_type=F32,
            )
            keep[half, :, lanes] = part[:rows]
            send[half, :, lanes] = part[rows:]


def gram_part(steps, where, rights, shards):
    rows = 64 * len(steps)
    tile = jax.ShapeDtypeStruct((len(rights), rows, 512), F32)
    return pl.pallas_call(
        functools.partial(gram_kernel, steps, len(rights)),
        in_specs=[SMEM] + [VMEM] * (len(rights) + len(shards)),
        out_specs=[VMEM] * 2,
        out_shape=[tile, tile],
        scratch_shapes=[pltpu.VMEM((2 * rows, 2048), BF)],
        compiler_params=pltpu.CompilerParams(vmem_limit_bytes=14 * MIB),
        cost_estimate=pl.CostEstimate(
            flops=4 * rows * len(rights) * 512 * 2048,
            bytes_accessed=4 * 10**6,
            transcendentals=0,
        ),
        name="gram_part",
    )(where, *rights, *shards)


def finish_kernel(chunks, where, running, *refs):
    out = refs[-1]
    y, core, z = where[1], where[2], where[3]
    for n, steps in enumerate(chunks):
        keep, got, theirs = refs[3 * n : 3 * n + 3]
        for k, step in enumerate(steps):
            source = (z + step + 8) % 8
            h = (source + core) % 2
            from_y = (y + source // 2) % 4
            rows = pl.ds(pl.multiple_of(64 * (4 * h + from_y), 64), 64)
            here = slice(64 * k, 64 * k + 64)
            total = keep[0, here, :] + got[0, here, :] + theirs[here, :]
            out[rows, :] = running[rows, :] + total * (1.0 / 8192.0)


def finish(chunks, where, running, *parts):
    specs = [SMEM, VMEM]
    for steps in chunks:
        half = pl.BlockSpec((1, 64 * len(steps), 512), lambda i: (0, 0, 0))
        specs += [half, half, pl.BlockSpec((64 * len(steps), 512), lambda i: (0, 0))]
    return pl.pallas_call(
        functools.partial(finish_kernel, chunks),
        grid=(1,),
        in_specs=specs,
        out_specs=VMEM,
        out_shape=jax.ShapeDtypeStruct((512, 512), F32),
        compiler_params=pltpu.CompilerParams(vmem_limit_bytes=12 * MIB),
        cost_estimate=pl.CostEstimate(flops=10**6, bytes_accessed=5 * 10**6, transcendentals=0),
        name="finish",
    )(where, running, *parts)


STEPS = (0, -1, 1, -2, 2, -3, 3, 4)
CHUNKS = (STEPS[:5], STEPS[5:])


def local(gate_in, key_in, value_in, filt_in, skip_gain, running_gram):
    seq, grp = lax.axis_index("seq"), lax.axis_index("grp")
    x, y, core, z = coords(seq, grp)
    where = jnp.stack([x, y, core, z, x, x]).astype(jnp.int32)
    across = jnp.stack([x, y, core, z, x, (x + 2) % 4]).astype(jnp.int32)
    beside = jnp.stack([x, y, core, z, (x + 1) % 4, (x + 3) % 4]).astype(jnp.int32)
    skips = lax.dynamic_slice_in_dim(skip_gain, seq * 32, 32, 0)

    outgoing = prepare(gate_in, key_in, value_in, filt_in)
    data = lax.all_to_all(outgoing, "seq", split_axis=0, concat_axis=0, tiled=True)
    same, other, send = convolve(where, skips, data)

    got = other_core(send)
    same = jnp.stack([same, got[0]])
    other = jnp.stack([other, got[1]])
    crossed = (x % 2) != (x // 2)
    row_a = to_rows(jnp.where(crossed, other, same), True)
    row_b = to_rows(jnp.where(crossed, same, other), False)
    below = along_x(other, 1)
    above = along_x(other, 3)
    opposite = along_x(same, 2)

    rows, near, own = phase(
        jnp.stack([row_a, row_b]), jnp.stack([above, below]), jnp.stack([same, opposite])
    )
    ups, downs = [rows], [rows]
    for _ in range(3):
        ups.append(along_z(ups[-1], 1))
        downs.append(along_z(downs[-1], 7))
    far = along_z(ups[3][:1], 1), along_z(downs[3][1:], 7)

    near_up, near_down = along_y(near, 1), along_y(near, 3)
    near_up, near_down, own = phase(near_up, near_down, own)
    near_far = along_y(near_up[:, :1], 1), along_y(near_down[:, 1:], 3)
    own_up, own_down = along_y(own, 1), along_y(own, 3)
    *near_far, own_up, own_down = phase(*near_far, own_up, own_down)
    own_far = along_y(own_up[:, :1], 1), along_y(own_down[:, 1:], 3)
    right = columns(beside, near, near_up, near_down, *near_far)
    own_right = columns(across, own, own_up, own_down, *own_far)

    early = [rows, ups[1], downs[1], ups[2], downs[2]]
    keep, send = gram_part(CHUNKS[0], where, [right], early)
    theirs_a = other_x_lo(keep[0] + other_core(send)[0])
    keep_a, send_a = gram_part(CHUNKS[0], where, [own_right], early)
    got_a = other_core(send_a)

    *far, theirs_a = phase(*far, theirs_a)
    late = [ups[3], downs[3], *far]
    keep_b, send_b = gram_part(CHUNKS[1], where, [own_right, right], late)
    got_b = other_core(send_b)
    theirs_b = other_x_lo(keep_b[1] + got_b[1])
    return finish(
        CHUNKS, where, running_gram, keep_a, got_a, theirs_a, keep_b, got_b, theirs_b
    )


def solution(mesh):
    in_specs = (
        P("seq", "grp"),
        P("seq", "grp"),
        P("seq", "grp"),
        P("seq", "grp"),
        P("grp"),
        P("seq", "grp"),
    )
    out_specs = P("seq", "grp")
    return jax.shard_map(local, mesh=mesh, in_specs=in_specs, out_specs=out_specs, check_vma=False)
```

time: 360 us -> 176 us (0.49)
  waiting for transfers between devices: 271 us -> 92.9 us
  matrix products: 27.1 us -> 0 us
  Pallas kernels: 0 us -> 25.5 us
  starting transfers between devices: 17.9 us -> 43.4 us
  blocking collectives: 18.5 us -> 0 us
  between operations: 13.6 us -> 0.29 us
  local copies, waits for them, and re-layouts: 6.9 us -> 12.1 us
    reduce_scatter x1 -> x0, waiting for transfers between devices: 152 us -> none  [local(): tile = lax.psum_scatter(partial_sum, 'seq', scatter_dimension=0, tiled=True)]
    all_gather x1 -> x0, waiting for transfers between devices: 100 us -> none  [local(): every = lax.all_gather(home, 'grp', axis=0, tiled=True)]
    ppermute x0 -> x27, waiting for transfers between devices: none -> 70.9 us  [move(): return lax.ppermute(array, MESH, pairs)]
    ppermute x0 -> x27, starting transfers between devices: none -> 34.8 us  [move(): return lax.ppermute(array, MESH, pairs)]
    dot_general x19 -> x0, matrix products: 27.1 us -> none  [the longest x1 13.7 us: local(): lax.dot_general(every, home, (((1,), (1,)), ((), ())), preferred_element_...]
    pallas_call x0 -> x8, Pallas kernels: none -> 25.5 us  [the longest x3 10.1 us: gram_part(): pl.pallas_call(functools.partial(gram_kernel, steps, len(rights)), in_spe...]
    all_to_all x1 -> x0, blocking collectives: 18.5 us -> none  [local(): lax.all_to_all(gated_own, 'seq', split_axis=1, concat_axis=0, tiled=True)]
    all_to_all x3 -> x1, starting transfers between devices: 17.6 us -> 8.59 us  [local(): lax.all_to_all(outgoing, 'seq', split_axis=0, concat_axis=0, tiled=True)]
  transfers between devices with their start and end apart: 5 -> 28, of which waited for: 4 -> 12; matrix products, arithmetic and copies ran while one was open for 5% -> 3% of each run, Pallas kernels for 0% -> 3%
where the time goes in v1:
time: 176 us; the launch traced here: 175 us
  waiting for transfers between devices  92.9 us (53%)
  starting transfers between devices  43.4 us (25%)
  Pallas kernels  25.5 us (14%)
  local copies, waits for them, and re-layouts  12.1 us (7%)
    ppermute x27, waiting for transfers between devices, move(): return lax.ppermute(array, MESH, pairs)  70.9 us
    ppermute x27, starting transfers between devices, move(): return lax.ppermute(array, MESH, pairs)  34.8 us
    all_to_all x1, waiting for transfers between devices, local(): lax.all_to_all(outgoing, 'seq', split_axis=0, concat_axis=0, tiled=True)  22 us
    pallas_call x3, Pallas kernels, gram_part(): pl.pallas_call(functools.partial(gram_kernel, steps, len(rights)), in_spe...  10.1 us
    all_to_all x1, starting transfers between devices, local(): lax.all_to_all(outgoing, 'seq', split_axis=0, concat_axis=0, tiled=True)  8.59 us
    unnamed x44, local copies, waits for them, and re-layouts  7.13 us
    pallas_call x1, Pallas kernels, convolve(): pl.pallas_call(conv_kernel, in_specs=[SMEM, SMEM] + [VMEM] * 7, out_specs...  6.24 us
    pallas_call x1, Pallas kernels, prepare(): pl.pallas_call(prepare_kernel, grid=(4,), in_specs=[block] * 4, out_specs...  4.27 us
  transfers between devices with their start and end apart: 28, of which 12 were waited for; matrix products, arithmetic and copies ran while one was open for 3% of the time, Pallas kernels for 3%

profile of v1, /device:TPU:1, one launch (start us, length us, event | category | flops | bytes accessed | tf_op | source)
XLA Modules:
  0.0 175.4 jit_solution(6700915275761571970)
XLA Ops:
  0.0 4.3 %prepare.1 = bf16[16,96,512]{2,1,0:T(8,128)(2,1)} custom-call(bf16[512,512]{1,0:T(8,128)(2,1)} %gate.1, bf16[512,512]{1,0:T(8,128)(2,1)} %key.1, bf16[512,512]{1,0:T(8,128)(2,1)} %value.1, bf16[512,512]{1,0:T(8,128)(2,1)} %filt.1), custom_call_target="tpu_custom_call" | custom-call | tf_op jit(solution)/shard_map/prepare/pallas_call | solution.py:103
  4.3 8.6 %all-to-all-start = ((bf16[16,96,512]{2,1,0:T(8,128)(2,1)}), bf16[16,96,512]{2,1,0:T(8,128)(2,1)S(1)}, u32[]{:S(2)}, u32[]{:S(2)}) async-start(bf16[16,96,512]{2,1,0:T(8,128)(2,1)} %prepare.1), calls=%async_computation | async-start | bytes 3145728 | tf_op jit(solution)/shard_map/all_to_all | solution.py:327
  13.8 22.0 %all-to-all-done.data = bf16[16,96,512]{2,1,0:T(8,128)(2,1)S(1)} async-done(((bf16[16,96,512]{2,1,0:T(8,128)(2,1)}), bf16[16,96,512]{2,1,0:T(8,128)(2,1)S(1)}, u32[]{:S(2)}, u32[]{:S(2)}) %all-to-all-start) | async-done | bytes 1572896 | tf_op jit(solution)/shard_map/all_to_all | solution.py:327
  35.8 6.2 %convolve.1 = (bf16[16,32,128]{2,1,0:T(8,128)(2,1)S(1)}, bf16[16,32,128]{2,1,0:T(8,128)(2,1)S(1)}, bf16[2,16,32,128]{3,2,1,0:T(8,128)(2,1)S(1)}) custom-call(s32[6]{0:T(128)S(1)} %stack.84.where, f32[32]{0:T(128)S(1)} %dynamic_slice.3.skip, bf16[16,96,512]{2,1,0:T(8,128)(2,1)S(1)} %all-to-all-done.data, bf16[256,64]{1,0:T(8,128)(2,1)S(1)} %copy-done.18, ...), custom_call_target="tpu_custom_call" | custom-call | flops 4000000000 | bytes 3000000 | tf_op jit(solution)/shard_map/convolve/pallas_call | solution.py:190
  43.0 1.2 collective-permute-done
  45.0 1.7 collective-permute-start.2
  46.7 3.2 %collective-permute-start.5 = (bf16[2,16,32,128]{3,2,1,0:T(8,128)(2,1)S(1)}, bf16[2,16,32,128]{3,2,1,0:T(8,128)(2,1)S(1)}, u32[]{:S(2)}, u32[]{:S(2)}) collective-permute-start(bf16[2,16,32,128]{3,2,1,0:T(8,128)(2,1)S(1)} %get-tuple-element.53), channel_id=1, source_target_pairs={{0,128},{1,129},{2,130},{3,131},{4,132},{5,133},{6,134},{7,135},{8... | collective-permute-start | bytes 786440 | tf_op jit(solution)/shard_map/ppermute | solution.py:33
  50.2 2.4 %collective-permute-start.3 = (bf16[2,16,32,128]{3,2,1,0:T(8,128)(2,1)S(1)}, bf16[2,16,32,128]{3,2,1,0:T(8,128)(2,1)S(1)}, u32[]{:S(2)}, u32[]{:S(2)}) collective-permute-start(bf16[2,16,32,128]{3,2,1,0:T(8,128)(2,1)S(1)} %get-tuple-element.52), channel_id=1, source_target_pairs={{0,136},{1,137},{2,138},{3,139},{4,140},{5,141},{6,142},{7,143},{8... | collective-permute-start | bytes 786440 | tf_op jit(solution)/shard_map/ppermute | solution.py:33
  52.6 19.7 %collective-permute-done.2 = bf16[2,16,32,128]{3,2,1,0:T(8,128)(2,1)S(1)} collective-permute-done((bf16[2,16,32,128]{3,2,1,0:T(8,128)(2,1)S(1)}, bf16[2,16,32,128]{3,2,1,0:T(8,128)(2,1)S(1)}, u32[]{:S(2)}, u32[]{:S(2)}) %collective-permute-start.2) | collective-permute-done | bytes 262176 | tf_op jit(solution)/shard_map/ppermute | solution.py:33
  72.5 8.7 %collective-permute-start.7 = (bf16[2,2,16,32,128]{4,3,2,1,0:T(8,128)(2,1)S(1)}, bf16[2,2,16,32,128]{4,3,2,1,0:T(8,128)(2,1)S(1)}, u32[]{:S(2)}, u32[]{:S(2)}) collective-permute-start(bf16[2,2,16,32,128]{4,3,2,1,0:T(8,128)(2,1)S(1)} %pad_maximum_fusion.1.refs_0_), channel_id=1, source_target_pairs={{0,96},{1,97},{2,98},{3,99},{4,100},{5,101},{6,102},{7,103},{8,104... | collective-permute-start | bytes 1572872 | tf_op jit(solution)/shard_map/ppermute | solution.py:33
  81.2 1.6 collective-permute-start.15
  82.8 8.7 %collective-permute-done.7.refs_2_ = bf16[2,2,16,32,128]{4,3,2,1,0:T(8,128)(2,1)S(1)} collective-permute-done((bf16[2,2,16,32,128]{4,3,2,1,0:T(8,128)(2,1)S(1)}, bf16[2,2,16,32,128]{4,3,2,1,0:T(8,128)(2,1)S(1)}, u32[]{:S(2)}, u32[]{:S(2)}) %collective-permute-start.7) | collective-permute-done | bytes 524320 | tf_op jit(solution)/shard_map/ppermute | solution.py:33
  91.5 3.2 %collective-permute-done.6.refs_1_ = bf16[2,2,16,32,128]{4,3,2,1,0:T(8,128)(2,1)S(1)} collective-permute-done((bf16[2,2,16,32,128]{4,3,2,1,0:T(8,128)(2,1)S(1)}, bf16[2,2,16,32,128]{4,3,2,1,0:T(8,128)(2,1)S(1)}, u32[]{:S(2)}, u32[]{:S(2)}) %collective-permute-start.6) | collective-permute-done | bytes 524320 | tf_op jit(solution)/shard_map/ppermute | solution.py:33
  96.7 1.3 collective-permute-start.16
  98.9 1.7 collective-permute-done.9.refs_4_
  100.6 13.4 %collective-permute-done.8.refs_3_ = bf16[2,1,16,32,128]{4,3,2,1,0:T(8,128)(2,1)S(1)} collective-permute-done((bf16[2,1,16,32,128]{4,3,2,1,0:T(8,128)(2,1)S(1)}, bf16[2,1,16,32,128]{4,3,2,1,0:T(8,128)(2,1)S(1)}, u32[]{:S(2)}, u32[]{:S(2)}) %collective-permute-start.8) | collective-permute-done | bytes 262176 | tf_op jit(solution)/shard_map/ppermute | solution.py:33
  119.6 3.5 %gram_part.4 = (f32[1,320,512]{2,1,0:T(8,128)S(1)}, f32[1,320,512]{2,1,0:T(8,128)S(1)}) custom-call(s32[6]{0:T(128)S(1)} %stack.84.where, bf16[512,2048]{1,0:T(8,128)(2,1)S(1)} %columns.3.refs_0_.refs_1_, bf16[2,2,16,32,128]{4,3,2,1,0:T(8,128)(2,1)S(1)} %copy-done.8, bf16[2,2,16,32,128]{4,3,2,1,0:T(8,128)(2,1)} %collective-permute-done.14.refs_2_, ...), custom_call_target="tpu_custom_call" | custom-call | flops 1342177280 | bytes 4000000 | tf_op jit(solution)/shard_map/gram_part/pallas_call | solution.py:266
  123.2 3.0 %collective-permute-start.23 = (f32[1,320,512]{2,1,0:T(8,128)S(1)}, f32[1,320,512]{2,1,0:T(8,128)S(1)}, u32[]{:S(2)}, u32[]{:S(2)}) collective-permute-start(f32[1,320,512]{2,1,0:T(8,128)S(1)} %get-tuple-element.43), channel_id=1, source_target_pairs={{0,16},{1,17},{2,18},{3,19},{4,20},{5,21},{6,22},{7,23},{8,24},{9,... | collective-permute-start | bytes 1966088 | tf_op jit(solution)/shard_map/ppermute | solution.py:33
  126.4 1.3 collective-permute-start.19
  128.9 1.7 slice.34
  131.3 1.5 collective-permute-start.12
  132.8 7.2 %collective-permute-done.21.refs_3_ = bf16[2,2,16,32,128]{4,3,2,1,0:T(8,128)(2,1)S(1)} collective-permute-done((bf16[2,2,16,32,128]{4,3,2,1,0:T(8,128)(2,1)}, bf16[2,2,16,32,128]{4,3,2,1,0:T(8,128)(2,1)S(1)}, u32[]{:S(2)}, u32[]{:S(2)}) %collective-permute-start.21) | collective-permute-done | bytes 524320 | tf_op jit(solution)/shard_map/ppermute | solution.py:33
  141.6 1.4 collective-permute-start.22
  144.6 1.6 columns.2.refs_0_
  146.2 2.7 %collective-permute-done.22.refs_5_ = bf16[1,2,16,32,128]{4,3,2,1,0:T(8,128)(2,1)} collective-permute-done((bf16[1,2,16,32,128]{4,3,2,1,0:T(8,128)(2,1)}, bf16[1,2,16,32,128]{4,3,2,1,0:T(8,128)(2,1)}, u32[]{:S(2)}, u32[]{:S(2)}) %collective-permute-start.22) | collective-permute-done | bytes 262176 | tf_op jit(solution)/shard_map/ppermute | solution.py:33
  148.9 3.8 %collective-permute-done.20.refs_4_ = bf16[1,2,16,32,128]{4,3,2,1,0:T(8,128)(2,1)} collective-permute-done((bf16[1,2,16,32,128]{4,3,2,1,0:T(8,128)(2,1)}, bf16[1,2,16,32,128]{4,3,2,1,0:T(8,128)(2,1)}, u32[]{:S(2)}, u32[]{:S(2)}) %collective-permute-start.20) | collective-permute-done | bytes 262176 | tf_op jit(solution)/shard_map/ppermute | solution.py:33
  152.8 3.1 %gram_part.5 = (f32[2,192,512]{2,1,0:T(8,128)S(1)}, f32[2,192,512]{2,1,0:T(8,128)S(1)}) custom-call(s32[6]{0:T(128)S(1)} %stack.84.where, bf16[512,2048]{1,0:T(8,128)(2,1)S(1)} %columns.2.refs_0_, bf16[512,2048]{1,0:T(8,128)(2,1)S(1)} %columns.3.refs_0_.refs_1_, bf16[2,2,16,32,128]{4,3,2,1,0:T(8,128)(2,1)S(1)} %copy-done.15, ...), custom_call_target="tpu_custom_call" | custom-call | flops 1610612736 | bytes 4000000 | tf_op jit(solution)/shard_map/gram_part/pallas_call | solution.py:266
  155.9 2.3 %collective-permute-start.25 = (f32[2,192,512]{2,1,0:T(8,128)S(1)}, f32[2,192,512]{2,1,0:T(8,128)S(1)}, u32[]{:S(2)}, u32[]{:S(2)}) collective-permute-start(f32[2,192,512]{2,1,0:T(8,128)S(1)} %get-tuple-element.48), channel_id=1, source_target_pairs={{0,16},{1,17},{2,18},{3,19},{4,20},{5,21},{6,22},{7,23},{8,24},{9,... | collective-permute-start | bytes 2359304 | tf_op jit(solution)/shard_map/ppermute | solution.py:33
  158.2 3.5 %gram_part.3 = (f32[1,320,512]{2,1,0:T(8,128)S(1)}, f32[1,320,512]{2,1,0:T(8,128)S(1)}) custom-call(s32[6]{0:T(128)S(1)} %stack.84.where, bf16[512,2048]{1,0:T(8,128)(2,1)S(1)} %columns.2.refs_0_, bf16[2,2,16,32,128]{4,3,2,1,0:T(8,128)(2,1)S(1)} %copy-done.9, bf16[2,2,16,32,128]{4,3,2,1,0:T(8,128)(2,1)} %collective-permute-done.14.refs_2_, ...), custom_call_target="tpu_custom_call" | custom-call | flops 1342177280 | bytes 4000000 | tf_op jit(solution)/shard_map/gram_part/pallas_call | solution.py:266
  161.8 2.1 %collective-permute-start.26 = (f32[192,512]{1,0:T(8,128)S(1)}, f32[192,512]{1,0:T(8,128)S(1)}, u32[]{:S(2)}, u32[]{:S(2)}) collective-permute-start(f32[192,512]{1,0:T(8,128)S(1)} %fusion), channel_id=1, source_target_pairs={{0,8},{1,9},{2,10},{3,11},{4,12},{5,13},{6,14},{7,15},{8,0},{9,1},... | collective-permute-start | bytes 1179656 | tf_op jit(solution)/shard_map/ppermute | solution.py:33
  164.0 9.1 %collective-permute-done.26.refs_5_ = f32[192,512]{1,0:T(8,128)S(1)} collective-permute-done((f32[192,512]{1,0:T(8,128)S(1)}, f32[192,512]{1,0:T(8,128)S(1)}, u32[]{:S(2)}, u32[]{:S(2)}) %collective-permute-start.26) | collective-permute-done | bytes 393248 | tf_op jit(solution)/shard_map/ppermute | solution.py:33
  173.0 2.4 %finish.1 = f32[512,512]{1,0:T(8,128)} custom-call(s32[6]{0:T(128)S(1)} %stack.84.where, f32[512,512]{1,0:T(8,128)S(1)} %copy-done.6, f32[1,320,512]{2,1,0:T(8,128)S(1)} %get-tuple-element.38.refs_0_, f32[1,320,512]{2,1,0:T(8,128)S(1)} %collective-permute-done.18.refs_1_, f32[320,512]{1,0:T(8,128)} %collective-permute-done.24.refs_2_, ...), custom_call_target="tpu_custom_call" | custom-call | flops 1000000 | bytes 5000000 | tf_op jit(solution)/shard_map/finish/pallas_call | solution.py:302
  (93 shorter events, 17.2 us)
Async XLA Ops:
  4.3 31.5 %copy-start.16 = (bf16[256,256]{1,0:T(8,128)(2,1)S(1)}, bf16[256,256]{1,0:T(8,128)(2,1)}, u32[]{:S(2)}) copy-start(bf16[256,256]{1,0:T(8,128)(2,1)} %constant.117.bwd) | copy-start | bytes 393220
  4.3 31.5 %copy-start.17 = (bf16[256,256]{1,0:T(8,128)(2,1)S(1)}, bf16[256,256]{1,0:T(8,128)(2,1)}, u32[]{:S(2)}) copy-start(bf16[256,256]{1,0:T(8,128)(2,1)} %constant.116.fwd) | copy-start | bytes 393220
  4.3 31.5 %copy-start.18 = (bf16[256,64]{1,0:T(8,128)(2,1)S(1)}, bf16[256,64]{1,0:T(8,128)(2,1)}, u32[]{:S(2)}) copy-start(bf16[256,64]{1,0:T(8,128)(2,1)} %constant.114.first) | copy-start | bytes 98308
  4.3 31.5 %copy-start.19 = (f32[128,128]{1,0:T(8,128)S(1)}, f32[128,128]{1,0:T(8,128)}, u32[]{:S(2)}) copy-start(f32[128,128]{1,0:T(8,128)} %constant.113.clone.t_sin) | copy-start | bytes 196612
  4.3 31.4 %all-to-all-start = ((bf16[16,96,512]{2,1,0:T(8,128)(2,1)}), bf16[16,96,512]{2,1,0:T(8,128)(2,1)S(1)}, u32[]{:S(2)}, u32[]{:S(2)}) async-start(bf16[16,96,512]{2,1,0:T(8,128)(2,1)} %prepare.1), calls=%async_computation | async-start | bytes 3145728 | tf_op jit(solution)/shard_map/all_to_all | solution.py:327
  42.1 2.2 %collective-permute-start = (bf16[2,16,32,128]{3,2,1,0:T(8,128)(2,1)S(1)}, bf16[2,16,32,128]{3,2,1,0:T(8,128)(2,1)S(1)}, u32[]{:S(2)}, u32[]{:S(2)}) collective-permute-start(bf16[2,16,32,128]{3,2,1,0:T(8,128)(2,1)S(1)} %get-tuple-element.28), channel_id=1, source_target_pairs={{0,16},{1,17},{2,18},{3,19},{4,20},{5,21},{6,22},{7,23},{8,24},{9,... | collective-permute-start | bytes 786440 | tf_op jit(solution)/shard_map/ppermute | solution.py:33
  44.3 8.2 %collective-permute-start.1 = (bf16[2,16,32,128]{3,2,1,0:T(8,128)(2,1)S(1)}, bf16[2,16,32,128]{3,2,1,0:T(8,128)(2,1)S(1)}, u32[]{:S(2)}, u32[]{:S(2)}) collective-permute-start(bf16[2,16,32,128]{3,2,1,0:T(8,128)(2,1)S(1)} %get-tuple-element.49), channel_id=1, source_target_pairs={{0,0},{1,1},{2,38},{3,39},{4,68},{5,69},{6,98},{7,99},{8,128},{9,1... | collective-permute-start | bytes 786440 | tf_op jit(solution)/shard_map/ppermute | solution.py:33
  45.0 27.3 %collective-permute-start.2 = (bf16[2,16,32,128]{3,2,1,0:T(8,128)(2,1)S(1)}, bf16[2,16,32,128]{3,2,1,0:T(8,128)(2,1)S(1)}, u32[]{:S(2)}, u32[]{:S(2)}) collective-permute-start(bf16[2,16,32,128]{3,2,1,0:T(8,128)(2,1)S(1)} %get-tuple-element.50), channel_id=1, source_target_pairs={{0,8},{1,9},{2,46},{3,47},{4,76},{5,77},{6,106},{7,107},{8,136},{9... | collective-permute-start | bytes 786440 | tf_op jit(solution)/shard_map/ppermute | solution.py:33
  46.7 25.7 %collective-permute-start.5 = (bf16[2,16,32,128]{3,2,1,0:T(8,128)(2,1)S(1)}, bf16[2,16,32,128]{3,2,1,0:T(8,128)(2,1)S(1)}, u32[]{:S(2)}, u32[]{:S(2)}) collective-permute-start(bf16[2,16,32,128]{3,2,1,0:T(8,128)(2,1)S(1)} %get-tuple-element.53), channel_id=1, source_target_pairs={{0,128},{1,129},{2,130},{3,131},{4,132},{5,133},{6,134},{7,135},{8... | collective-permute-start | bytes 786440 | tf_op jit(solution)/shard_map/ppermute | solution.py:33
  49.9 22.5 %collective-permute-start.4 = (bf16[2,16,32,128]{3,2,1,0:T(8,128)(2,1)S(1)}, bf16[2,16,32,128]{3,2,1,0:T(8,128)(2,1)S(1)}, u32[]{:S(2)}, u32[]{:S(2)}) collective-permute-start(bf16[2,16,32,128]{3,2,1,0:T(8,128)(2,1)S(1)} %get-tuple-element.52), channel_id=1, source_target_pairs={{0,8},{1,9},{2,10},{3,11},{4,12},{5,13},{6,14},{7,15},{8,128},{9,1... | collective-permute-start | bytes 786440 | tf_op jit(solution)/shard_map/ppermute | solution.py:33
  50.2 22.2 %collective-permute-start.3 = (bf16[2,16,32,128]{3,2,1,0:T(8,128)(2,1)S(1)}, bf16[2,16,32,128]{3,2,1,0:T(8,128)(2,1)S(1)}, u32[]{:S(2)}, u32[]{:S(2)}) collective-permute-start(bf16[2,16,32,128]{3,2,1,0:T(8,128)(2,1)S(1)} %get-tuple-element.52), channel_id=1, source_target_pairs={{0,136},{1,137},{2,138},{3,139},{4,140},{5,141},{6,142},{7,143},{8... | collective-permute-start | bytes 786440 | tf_op jit(solution)/shard_map/ppermute | solution.py:33
  72.5 19.0 %collective-permute-start.7 = (bf16[2,2,16,32,128]{4,3,2,1,0:T(8,128)(2,1)S(1)}, bf16[2,2,16,32,128]{4,3,2,1,0:T(8,128)(2,1)S(1)}, u32[]{:S(2)}, u32[]{:S(2)}) collective-permute-start(bf16[2,2,16,32,128]{4,3,2,1,0:T(8,128)(2,1)S(1)} %pad_maximum_fusion.1.refs_0_), channel_id=1, source_target_pairs={{0,96},{1,97},{2,98},{3,99},{4,100},{5,101},{6,102},{7,103},{8,104... | collective-permute-start | bytes 1572872 | tf_op jit(solution)/shard_map/ppermute | solution.py:33
  81.2 13.5 %collective-permute-start.6 = (bf16[2,2,16,32,128]{4,3,2,1,0:T(8,128)(2,1)S(1)}, bf16[2,2,16,32,128]{4,3,2,1,0:T(8,128)(2,1)S(1)}, u32[]{:S(2)}, u32[]{:S(2)}) collective-permute-start(bf16[2,2,16,32,128]{4,3,2,1,0:T(8,128)(2,1)S(1)} %pad_maximum_fusion.1.refs_0_), channel_id=1, source_target_pairs={{0,32},{1,33},{2,34},{3,35},{4,36},{5,37},{6,38},{7,39},{8,40},{9,... | collective-permute-start | bytes 1572872 | tf_op jit(solution)/shard_map/ppermute | solution.py:33
  81.2 15.4 %collective-permute-start.15 = (bf16[2,2,16,32,128]{4,3,2,1,0:T(8,128)(2,1)S(1)}, bf16[2,2,16,32,128]{4,3,2,1,0:T(8,128)(2,1)}, u32[]{:S(2)}, u32[]{:S(2)}) collective-permute-start(bf16[2,2,16,32,128]{4,3,2,1,0:T(8,128)(2,1)S(1)} %pad_maximum_fusion.refs_1_), channel_id=1, source_target_pairs={{0,7},{1,0},{2,1},{3,2},{4,3},{5,4},{6,5},{7,6},{8,15},{9,8},{10,9... | collective-permute-start | bytes 1572872 | tf_op jit(solution)/shard_map/ppermute | solution.py:33
  82.8 13.9 %collective-permute-start.14 = (bf16[2,2,16,32,128]{4,3,2,1,0:T(8,128)(2,1)S(1)}, bf16[2,2,16,32,128]{4,3,2,1,0:T(8,128)(2,1)}, u32[]{:S(2)}, u32[]{:S(2)}) collective-permute-start(bf16[2,2,16,32,128]{4,3,2,1,0:T(8,128)(2,1)S(1)} %pad_maximum_fusion.refs_1_), channel_id=1, source_target_pairs={{0,1},{1,2},{2,3},{3,4},{4,5},{5,6},{6,7},{7,0},{8,9},{9,10},{10,1... | collective-permute-start | bytes 1572872 | tf_op jit(solution)/shard_map/ppermute | solution.py:33
  94.7 5.9 %collective-permute-start.9 = (bf16[2,1,16,32,128]{4,3,2,1,0:T(8,128)(2,1)S(1)}, bf16[2,1,16,32,128]{4,3,2,1,0:T(8,128)(2,1)S(1)}, u32[]{:S(2)}, u32[]{:S(2)}) collective-permute-start(bf16[2,1,16,32,128]{4,3,2,1,0:T(8,128)(2,1)S(1)} %slice.33), channel_id=1, source_target_pairs={{0,96},{1,97},{2,98},{3,99},{4,100},{5,101},{6,102},{7,103},{8,104... | collective-permute-start | bytes 786440 | tf_op jit(solution)/shard_map/ppermute | solution.py:33
  95.1 19.7 %collective-permute-start.11 = (bf16[2,2,16,32,128]{4,3,2,1,0:T(8,128)(2,1)S(1)}, bf16[2,2,16,32,128]{4,3,2,1,0:T(8,128)(2,1)S(1)}, u32[]{:S(2)}, u32[]{:S(2)}) collective-permute-start(bf16[2,2,16,32,128]{4,3,2,1,0:T(8,128)(2,1)S(1)} %pad_maximum_fusion.2.refs_0_), channel_id=1, source_target_pairs={{0,96},{1,97},{2,98},{3,99},{4,100},{5,101},{6,102},{7,103},{8,104... | collective-permute-start | bytes 1572872 | tf_op jit(solution)/shard_map/ppermute | solution.py:33
  95.8 19.8 %collective-permute-start.10 = (bf16[2,2,16,32,128]{4,3,2,1,0:T(8,128)(2,1)S(1)}, bf16[2,2,16,32,128]{4,3,2,1,0:T(8,128)(2,1)}, u32[]{:S(2)}, u32[]{:S(2)}) collective-permute-start(bf16[2,2,16,32,128]{4,3,2,1,0:T(8,128)(2,1)S(1)} %pad_maximum_fusion.2.refs_0_), channel_id=1, source_target_pairs={{0,32},{1,33},{2,34},{3,35},{4,36},{5,37},{6,38},{7,39},{8,40},{9,... | collective-permute-start | bytes 1572872 | tf_op jit(solution)/shard_map/ppermute | solution.py:33
  96.6 23.0 %collective-permute-start.17 = (bf16[2,2,16,32,128]{4,3,2,1,0:T(8,128)(2,1)}, bf16[2,2,16,32,128]{4,3,2,1,0:T(8,128)(2,1)}, u32[]{:S(2)}, u32[]{:S(2)}) collective-permute-start(bf16[2,2,16,32,128]{4,3,2,1,0:T(8,128)(2,1)} %collective-permute-done.15.refs_3_), channel_id=1, source_target_pairs={{0,7},{1,0},{2,1},{3,2},{4,3},{5,4},{6,5},{7,6},{8,15},{9,8},{10,9... | collective-permute-start | bytes 1572872 | tf_op jit(solution)/shard_map/ppermute | solution.py:33
  96.7 22.8 %collective-permute-start.16 = (bf16[2,2,16,32,128]{4,3,2,1,0:T(8,128)(2,1)}, bf16[2,2,16,32,128]{4,3,2,1,0:T(8,128)(2,1)}, u32[]{:S(2)}, u32[]{:S(2)}) collective-permute-start(bf16[2,2,16,32,128]{4,3,2,1,0:T(8,128)(2,1)} %collective-permute-done.14.refs_2_), channel_id=1, source_target_pairs={{0,1},{1,2},{2,3},{3,4},{4,5},{5,6},{6,7},{7,0},{8,9},{9,10},{10,1... | collective-permute-start | bytes 1572872 | tf_op jit(solution)/shard_map/ppermute | solution.py:33
  100.6 13.5 %collective-permute-start.8 = (bf16[2,1,16,32,128]{4,3,2,1,0:T(8,128)(2,1)S(1)}, bf16[2,1,16,32,128]{4,3,2,1,0:T(8,128)(2,1)S(1)}, u32[]{:S(2)}, u32[]{:S(2)}) collective-permute-start(bf16[2,1,16,32,128]{4,3,2,1,0:T(8,128)(2,1)S(1)} %slice.32), channel_id=1, source_target_pairs={{0,32},{1,33},{2,34},{3,35},{4,36},{5,37},{6,38},{7,39},{8,40},{9,... | collective-permute-start | bytes 786440 | tf_op jit(solution)/shard_map/ppermute | solution.py:33
  123.2 4.7 %collective-permute-start.23 = (f32[1,320,512]{2,1,0:T(8,128)S(1)}, f32[1,320,512]{2,1,0:T(8,128)S(1)}, u32[]{:S(2)}, u32[]{:S(2)}) collective-permute-start(f32[1,320,512]{2,1,0:T(8,128)S(1)} %get-tuple-element.43), channel_id=1, source_target_pairs={{0,16},{1,17},{2,18},{3,19},{4,20},{5,21},{6,22},{7,23},{8,24},{9,... | collective-permute-start | bytes 1966088 | tf_op jit(solution)/shard_map/ppermute | solution.py:33
  126.2 13.8 %collective-permute-start.21 = (bf16[2,2,16,32,128]{4,3,2,1,0:T(8,128)(2,1)}, bf16[2,2,16,32,128]{4,3,2,1,0:T(8,128)(2,1)S(1)}, u32[]{:S(2)}, u32[]{:S(2)}) collective-permute-start(bf16[2,2,16,32,128]{4,3,2,1,0:T(8,128)(2,1)} %collective-permute-done.17.refs_5_), channel_id=1, source_target_pairs={{0,7},{1,0},{2,1},{3,2},{4,3},{5,4},{6,5},{7,6},{8,15},{9,8},{10,9... | collective-permute-start | bytes 1572872 | tf_op jit(solution)/shard_map/ppermute | solution.py:33
  126.4 16.6 %collective-permute-start.19 = (bf16[2,2,16,32,128]{4,3,2,1,0:T(8,128)(2,1)}, bf16[2,2,16,32,128]{4,3,2,1,0:T(8,128)(2,1)S(1)}, u32[]{:S(2)}, u32[]{:S(2)}) collective-permute-start(bf16[2,2,16,32,128]{4,3,2,1,0:T(8,128)(2,1)} %collective-permute-done.16.refs_4_), channel_id=1, source_target_pairs={{0,1},{1,2},{2,3},{3,4},{4,5},{5,6},{6,7},{7,0},{8,9},{9,10},{10,1... | collective-permute-start | bytes 1572872 | tf_op jit(solution)/shard_map/ppermute | solution.py:33
  128.9 23.9 %collective-permute-start.24 = (f32[320,512]{1,0:T(8,128)}, f32[320,512]{1,0:T(8,128)}, u32[]{:S(2)}, u32[]{:S(2)}) collective-permute-start(f32[320,512]{1,0:T(8,128)} %add_bitcast_fusion), channel_id=1, source_target_pairs={{0,8},{1,9},{2,10},{3,11},{4,12},{5,13},{6,14},{7,15},{8,0},{9,1},... | collective-permute-start | bytes 1966088 | tf_op jit(solution)/shard_map/ppermute | solution.py:33
  131.3 13.3 %collective-permute-start.13 = (bf16[2,1,16,32,128]{4,3,2,1,0:T(8,128)(2,1)}, bf16[2,1,16,32,128]{4,3,2,1,0:T(8,128)(2,1)S(1)}, u32[]{:S(2)}, u32[]{:S(2)}) collective-permute-start(bf16[2,1,16,32,128]{4,3,2,1,0:T(8,128)(2,1)} %slice.35), channel_id=1, source_target_pairs={{0,96},{1,97},{2,98},{3,99},{4,100},{5,101},{6,102},{7,103},{8,104... | collective-permute-start | bytes 786440 | tf_op jit(solution)/shard_map/ppermute | solution.py:33
  131.3 13.3 %collective-permute-start.12 = (bf16[2,1,16,32,128]{4,3,2,1,0:T(8,128)(2,1)}, bf16[2,1,16,32,128]{4,3,2,1,0:T(8,128)(2,1)}, u32[]{:S(2)}, u32[]{:S(2)}) collective-permute-start(bf16[2,1,16,32,128]{4,3,2,1,0:T(8,128)(2,1)} %slice.34), channel_id=1, source_target_pairs={{0,32},{1,33},{2,34},{3,35},{4,36},{5,37},{6,38},{7,39},{8,40},{9,... | collective-permute-start | bytes 786440 | tf_op jit(solution)/shard_map/ppermute | solution.py:33
  141.6 7.4 %collective-permute-start.22 = (bf16[1,2,16,32,128]{4,3,2,1,0:T(8,128)(2,1)}, bf16[1,2,16,32,128]{4,3,2,1,0:T(8,128)(2,1)}, u32[]{:S(2)}, u32[]{:S(2)}) collective-permute-start(bf16[1,2,16,32,128]{4,3,2,1,0:T(8,128)(2,1)} %slice.43), channel_id=1, source_target_pairs={{0,7},{1,0},{2,1},{3,2},{4,3},{5,4},{6,5},{7,6},{8,15},{9,8},{10,9... | collective-permute-start | bytes 786440 | tf_op jit(solution)/shard_map/ppermute | solution.py:33
  144.5 8.3 %collective-permute-start.20 = (bf16[1,2,16,32,128]{4,3,2,1,0:T(8,128)(2,1)}, bf16[1,2,16,32,128]{4,3,2,1,0:T(8,128)(2,1)}, u32[]{:S(2)}, u32[]{:S(2)}) collective-permute-start(bf16[1,2,16,32,128]{4,3,2,1,0:T(8,128)(2,1)} %slice.42), channel_id=1, source_target_pairs={{0,1},{1,2},{2,3},{3,4},{4,5},{5,6},{6,7},{7,0},{8,9},{9,10},{10,1... | collective-permute-start | bytes 786440 | tf_op jit(solution)/shard_map/ppermute | solution.py:33
  155.9 5.9 %collective-permute-start.25 = (f32[2,192,512]{2,1,0:T(8,128)S(1)}, f32[2,192,512]{2,1,0:T(8,128)S(1)}, u32[]{:S(2)}, u32[]{:S(2)}) collective-permute-start(f32[2,192,512]{2,1,0:T(8,128)S(1)} %get-tuple-element.48), channel_id=1, source_target_pairs={{0,16},{1,17},{2,18},{3,19},{4,20},{5,21},{6,22},{7,23},{8,24},{9,... | collective-permute-start | bytes 2359304 | tf_op jit(solution)/shard_map/ppermute | solution.py:33
  161.7 2.3 %collective-permute-start.18 = (f32[1,320,512]{2,1,0:T(8,128)S(1)}, f32[1,320,512]{2,1,0:T(8,128)S(1)}, u32[]{:S(2)}, u32[]{:S(2)}) collective-permute-start(f32[1,320,512]{2,1,0:T(8,128)S(1)} %get-tuple-element.39), channel_id=1, source_target_pairs={{0,16},{1,17},{2,18},{3,19},{4,20},{5,21},{6,22},{7,23},{8,24},{9,... | collective-permute-start | bytes 1966088 | tf_op jit(solution)/shard_map/ppermute | solution.py:33
  161.8 11.2 %collective-permute-start.26 = (f32[192,512]{1,0:T(8,128)S(1)}, f32[192,512]{1,0:T(8,128)S(1)}, u32[]{:S(2)}, u32[]{:S(2)}) collective-permute-start(f32[192,512]{1,0:T(8,128)S(1)} %fusion), channel_id=1, source_target_pairs={{0,8},{1,9},{2,10},{3,11},{4,12},{5,13},{6,14},{7,15},{8,0},{9,1},... | collective-permute-start | bytes 1179656 | tf_op jit(solution)/shard_map/ppermute | solution.py:33
  (18 other events, 153.1 us)

commit v2 on v1

--- a/solution.py
+++ b/solution.py
@@ -14,6 +14,7 @@
 MESH = ("seq", "grp")
 VMEM = pl.BlockSpec(memory_space=pltpu.VMEM)
 SMEM = pl.BlockSpec(memory_space=pltpu.SMEM)
+ANY = pl.BlockSpec(memory_space=pl.ANY)
 MIB = 1024 * 1024
 
 
@@ -61,8 +62,29 @@
     return move(array, target)
 
 
-def phase(*arrays):
-    return lax.optimization_barrier(arrays)
+def after_kernel(n_after, *refs):
+    sources, targets = refs[: len(refs) - n_after], refs[len(refs) - n_after :]
+    n = 0
+    for target in targets:
+        for place in range(target.shape[0]):
+            target[place] = sources[n][...]
+            n += 1
+
+
+def after(stacks, *earlier):
+    pieces = [piece for stack in stacks for piece in stack]
+    shapes = [jax.ShapeDtypeStruct((len(stack), *stack[0].shape), BF) for stack in stacks]
+    return pl.pallas_call(
+        lambda *refs: after_kernel(
+            len(stacks), *refs[: len(pieces)], *refs[len(pieces) + len(earlier) :]
+        ),
+        in_specs=[VMEM] * len(pieces) + [ANY] * len(earlier),
+        out_specs=[VMEM] * len(stacks),
+        out_shape=shapes,
+        compiler_params=pltpu.CompilerParams(vmem_limit_bytes=8 * MIB),
+        cost_estimate=pl.CostEstimate(flops=0, bytes_accessed=10**6, transcendentals=0),
+        name="after",
+    )(*pieces, *earlier)
 
 
 def angles(rows, cols, modulus):
@@ -203,7 +225,8 @@
 
 def columns_kernel(where, *refs):
     y, core, first_x, second_x = where[1], where[2], where[4], where[5]
-    own, below, above, far_low, far_high, right = refs
+    own, below, above, far_low, far_high = refs[:5]
+    right = refs[-1]
     for j, from_x in enumerate((first_x, second_x)):
         for step in (0, -1, 1, 2):
             from_y = (y + step + 4) % 4
@@ -218,21 +241,21 @@
                     right[row, 128 * a : 128 * a + 128] = piece[a]
 
 
-def columns(where, *shards):
+def columns(where, shards, *earlier):
     return pl.pallas_call(
         columns_kernel,
-        in_specs=[SMEM] + [VMEM] * len(shards),
+        in_specs=[SMEM] + [VMEM] * len(shards) + [ANY] * len(earlier),
         out_specs=VMEM,
         out_shape=jax.ShapeDtypeStruct((512, 2048), BF),
         compiler_params=pltpu.CompilerParams(vmem_limit_bytes=12 * MIB),
         cost_estimate=pl.CostEstimate(flops=0, bytes_accessed=4 * 10**6, transcendentals=0),
         name="columns",
-    )(where, *shards)
-
-
-def gram_kernel(steps, n_right, where, *refs):
+    )(where, *shards, *earlier)
+
+
+def gram_kernel(steps, n_right, n_earlier, where, *refs):
     rows = 64 * len(steps)
-    rights, shard_refs = refs[:n_right], refs[n_right:-3]
+    rights, shard_refs = refs[:n_right], refs[n_right : -3 - n_earlier]
     keep, send, left = refs[-3:]
     x, core, z = where[0], where[2], where[3]
     shards = []
@@ -260,12 +283,12 @@
             send[half, :, lanes] = part[rows:]
 
 
-def gram_part(steps, where, rights, shards):
+def gram_part(steps, where, rights, shards, *earlier):
     rows = 64 * len(steps)
     tile = jax.ShapeDtypeStruct((len(rights), rows, 512), F32)
     return pl.pallas_call(
-        functools.partial(gram_kernel, steps, len(rights)),
-        in_specs=[SMEM] + [VMEM] * (len(rights) + len(shards)),
+        functools.partial(gram_kernel, steps, len(rights), len(earlier)),
+        in_specs=[SMEM] + [VMEM] * (len(rights) + len(shards)) + [ANY] * len(earlier),
         out_specs=[VMEM] * 2,
         out_shape=[tile, tile],
         scratch_shapes=[pltpu.VMEM((2 * rows, 2048), BF)],
@@ -276,7 +299,7 @@
             transcendentals=0,
         ),
         name="gram_part",
-    )(where, *rights, *shards)
+    )(where, *rights, *shards, *earlier)
 
 
 def finish_kernel(chunks, where, running, *refs):
@@ -337,9 +360,7 @@
     above = along_x(other, 3)
     opposite = along_x(same, 2)
 
-    rows, near, own = phase(
-        jnp.stack([row_a, row_b]), jnp.stack([above, below]), jnp.stack([same, opposite])
-    )
+    rows, near = after([[row_a, row_b], [above, below]], same, opposite)
     ups, downs = [rows], [rows]
     for _ in range(3):
         ups.append(along_z(ups[-1], 1))
@@ -347,13 +368,12 @@
     far = along_z(ups[3][:1], 1), along_z(downs[3][1:], 7)
 
     near_up, near_down = along_y(near, 1), along_y(near, 3)
-    near_up, near_down, own = phase(near_up, near_down, own)
+    (own,) = after([[same, opposite]], near_up, near_down)
     near_far = along_y(near_up[:, :1], 1), along_y(near_down[:, 1:], 3)
     own_up, own_down = along_y(own, 1), along_y(own, 3)
-    *near_far, own_up, own_down = phase(*near_far, own_up, own_down)
+    right = columns(beside, [near, near_up, near_down, *near_far], own_up, own_down)
     own_far = along_y(own_up[:, :1], 1), along_y(own_down[:, 1:], 3)
-    right = columns(beside, near, near_up, near_down, *near_far)
-    own_right = columns(across, own, own_up, own_down, *own_far)
+    own_right = columns(across, [own, own_up, own_down, *own_far])
 
     early = [rows, ups[1], downs[1], ups[2], downs[2]]
     keep, send = gram_part(CHUNKS[0], where, [right], early)
@@ -361,9 +381,8 @@
     keep_a, send_a = gram_part(CHUNKS[0], where, [own_right], early)
     got_a = other_core(send_a)
 
-    *far, theirs_a = phase(*far, theirs_a)
     late = [ups[3], downs[3], *far]
-    keep_b, send_b = gram_part(CHUNKS[1], where, [own_right, right], late)
+    keep_b, send_b = gram_part(CHUNKS[1], where, [own_right, right], late, theirs_a, keep_a)
     got_b = other_core(send_b)
     theirs_b = other_x_lo(keep_b[1] + got_b[1])
     return finish(

time: 176 us -> 171 us (0.972)
  waiting for transfers between devices: 92.9 us -> 85.9 us
    ppermute x27, waiting for transfers between devices: 70.9 us -> 63.9 us  [move(): return lax.ppermute(array, MESH, pairs)]
    unnamed x44 -> x48, local copies, waits for them, and re-layouts: 7.13 us -> 8.23 us
    pallas_call x5 -> x7, Pallas kernels: 12.6 us -> 12.7 us  [the longest x3 10.2 us: gram_part(): pl.pallas_call(functools.partial(gram_kernel, steps, len(rights), len(ear...]
  transfers between devices with their start and end apart: 28 -> 28, of which waited for: 12 -> 10; matrix products, arithmetic and copies ran while one was open for 3% -> 3% of each run, Pallas kernels for 3% -> 4%
where the time goes in v2:
time: 171 us; the launch traced here: 170 us
  waiting for transfers between devices  85.9 us (50%)
  starting transfers between devices  45.1 us (26%)
  Pallas kernels  25.6 us (15%)
  local copies, waits for them, and re-layouts  12.2 us (7%)
    ppermute x27, waiting for transfers between devices, move(): return lax.ppermute(array, MESH, pairs)  63.9 us
    ppermute x27, starting transfers between devices, move(): return lax.ppermute(array, MESH, pairs)  36.5 us
    all_to_all x1, waiting for transfers between devices, local(): lax.all_to_all(outgoing, 'seq', split_axis=0, concat_axis=0, tiled=True)  22 us
    pallas_call x3, Pallas kernels, gram_part(): pl.pallas_call(functools.partial(gram_kernel, steps, len(rights), len(ear...  10.2 us
    all_to_all x1, starting transfers between devices, local(): lax.all_to_all(outgoing, 'seq', split_axis=0, concat_axis=0, tiled=True)  8.6 us
    unnamed x48, local copies, waits for them, and re-layouts  8.23 us
    pallas_call x1, Pallas kernels, convolve(): pl.pallas_call(conv_kernel, in_specs=[SMEM, SMEM] + [VMEM] * 7, out_specs...  6.26 us
    pallas_call x1, Pallas kernels, prepare(): pl.pallas_call(prepare_kernel, grid=(4,), in_specs=[block] * 4, out_specs...  4.24 us
  transfers between devices with their start and end apart: 28, of which 10 were waited for; matrix products, arithmetic and copies ran while one was open for 3% of the time, Pallas kernels for 4%

profile of v2, /device:TPU:1, one launch (start us, length us, event | category | flops | bytes accessed | tf_op | source)
XLA Modules:
  0.0 170.2 jit_solution(15378534642140608198)
XLA Ops:
  0.0 4.2 %prepare.1 = bf16[16,96,512]{2,1,0:T(8,128)(2,1)} custom-call(bf16[512,512]{1,0:T(8,128)(2,1)} %gate.1, bf16[512,512]{1,0:T(8,128)(2,1)} %key.1, bf16[512,512]{1,0:T(8,128)(2,1)} %value.1, bf16[512,512]{1,0:T(8,128)(2,1)} %filt.1), custom_call_target="tpu_custom_call" | custom-call | tf_op jit(solution)/shard_map/prepare/pallas_call | solution.py:125
  4.3 8.6 %all-to-all-start = ((bf16[16,96,512]{2,1,0:T(8,128)(2,1)}), bf16[16,96,512]{2,1,0:T(8,128)(2,1)S(1)}, u32[]{:S(2)}, u32[]{:S(2)}) async-start(bf16[16,96,512]{2,1,0:T(8,128)(2,1)} %prepare.1), calls=%async_computation | async-start | bytes 3145728 | tf_op jit(solution)/shard_map/all_to_all | solution.py:350
  13.7 22.0 %all-to-all-done.data = bf16[16,96,512]{2,1,0:T(8,128)(2,1)S(1)} async-done(((bf16[16,96,512]{2,1,0:T(8,128)(2,1)}), bf16[16,96,512]{2,1,0:T(8,128)(2,1)S(1)}, u32[]{:S(2)}, u32[]{:S(2)}) %all-to-all-start) | async-done | bytes 1572896 | tf_op jit(solution)/shard_map/all_to_all | solution.py:350
  35.8 6.3 %convolve.1 = (bf16[16,32,128]{2,1,0:T(8,128)(2,1)S(1)}, bf16[16,32,128]{2,1,0:T(8,128)(2,1)S(1)}, bf16[2,16,32,128]{3,2,1,0:T(8,128)(2,1)S(1)}) custom-call(s32[6]{0:T(128)S(1)} %stack.57.where, f32[32]{0:T(128)S(1)} %dynamic_slice.3.skip, bf16[16,96,512]{2,1,0:T(8,128)(2,1)S(1)} %all-to-all-done.data, bf16[256,64]{1,0:T(8,128)(2,1)S(1)} %copy-done.22, ...), custom_call_target="tpu_custom_call" | custom-call | flops 4000000000 | bytes 3000000 | tf_op jit(solution)/shard_map/convolve/pallas_call | solution.py:212
  43.1 1.2 collective-permute-done
  45.5 3.5 %collective-permute-start.3 = (bf16[2,16,32,128]{3,2,1,0:T(8,128)(2,1)S(1)}, bf16[2,16,32,128]{3,2,1,0:T(8,128)(2,1)S(1)}, u32[]{:S(2)}, u32[]{:S(2)}) collective-permute-start(bf16[2,16,32,128]{3,2,1,0:T(8,128)(2,1)S(1)} %get-tuple-element.27), channel_id=1, source_target_pairs={{0,8},{1,9},{2,46},{3,47},{4,76},{5,77},{6,106},{7,107},{8,136},{9... | collective-permute-start | bytes 786440 | tf_op jit(solution)/shard_map/ppermute | solution.py:34
  49.1 2.0 %collective-permute-start.4 = (bf16[2,16,32,128]{3,2,1,0:T(8,128)(2,1)S(1)}, bf16[2,16,32,128]{3,2,1,0:T(8,128)(2,1)S(1)}, u32[]{:S(2)}, u32[]{:S(2)}) collective-permute-start(bf16[2,16,32,128]{3,2,1,0:T(8,128)(2,1)S(1)} %get-tuple-element.29), channel_id=1, source_target_pairs={{0,136},{1,137},{2,138},{3,139},{4,140},{5,141},{6,142},{7,143},{8... | collective-permute-start | bytes 786440 | tf_op jit(solution)/shard_map/ppermute | solution.py:34
  51.3 2.1 %collective-permute-done.1.refs_5_.refs_1_ = bf16[2,16,32,128]{3,2,1,0:T(8,128)(2,1)S(1)} collective-permute-done((bf16[2,16,32,128]{3,2,1,0:T(8,128)(2,1)S(1)}, bf16[2,16,32,128]{3,2,1,0:T(8,128)(2,1)S(1)}, u32[]{:S(2)}, u32[]{:S(2)}) %collective-permute-start.1) | collective-permute-done | bytes 262176 | tf_op jit(solution)/shard_map/ppermute | solution.py:34
  53.5 22.5 %collective-permute-done.3.refs_1_ = bf16[2,16,32,128]{3,2,1,0:T(8,128)(2,1)S(1)} collective-permute-done((bf16[2,16,32,128]{3,2,1,0:T(8,128)(2,1)S(1)}, bf16[2,16,32,128]{3,2,1,0:T(8,128)(2,1)S(1)}, u32[]{:S(2)}, u32[]{:S(2)}) %collective-permute-start.3) | collective-permute-done | bytes 262176 | tf_op jit(solution)/shard_map/ppermute | solution.py:34
  76.2 4.8 %collective-permute-start.7 = (bf16[2,2,16,32,128]{4,3,2,1,0:T(8,128)(2,1)S(1)}, bf16[2,2,16,32,128]{4,3,2,1,0:T(8,128)(2,1)S(1)}, u32[]{:S(2)}, u32[]{:S(2)}) collective-permute-start(bf16[2,2,16,32,128]{4,3,2,1,0:T(8,128)(2,1)S(1)} %get-tuple-element.19.refs_0_), channel_id=1, source_target_pairs={{0,96},{1,97},{2,98},{3,99},{4,100},{5,101},{6,102},{7,103},{8,104... | collective-permute-start | bytes 1572872 | tf_op jit(solution)/shard_map/ppermute | solution.py:34
  80.9 3.0 %collective-permute-start.13 = (bf16[2,2,16,32,128]{4,3,2,1,0:T(8,128)(2,1)S(1)}, bf16[2,2,16,32,128]{4,3,2,1,0:T(8,128)(2,1)}, u32[]{:S(2)}, u32[]{:S(2)}) collective-permute-start(bf16[2,2,16,32,128]{4,3,2,1,0:T(8,128)(2,1)S(1)} %get-tuple-element.20.refs_1_), channel_id=1, source_target_pairs={{0,7},{1,0},{2,1},{3,2},{4,3},{5,4},{6,5},{7,6},{8,15},{9,8},{10,9... | collective-permute-start | bytes 1572872 | tf_op jit(solution)/shard_map/ppermute | solution.py:34
  84.0 8.3 %collective-permute-done.6.refs_2_.refs_1_ = bf16[2,2,16,32,128]{4,3,2,1,0:T(8,128)(2,1)S(1)} collective-permute-done((bf16[2,2,16,32,128]{4,3,2,1,0:T(8,128)(2,1)S(1)}, bf16[2,2,16,32,128]{4,3,2,1,0:T(8,128)(2,1)S(1)}, u32[]{:S(2)}, u32[]{:S(2)}) %collective-permute-start.6) | collective-permute-done | bytes 524320 | tf_op jit(solution)/shard_map/ppermute | solution.py:34
  93.1 2.7 %collective-permute-start.9 = (bf16[2,2,16,32,128]{4,3,2,1,0:T(8,128)(2,1)S(1)}, bf16[2,2,16,32,128]{4,3,2,1,0:T(8,128)(2,1)S(1)}, u32[]{:S(2)}, u32[]{:S(2)}) collective-permute-start(bf16[2,2,16,32,128]{4,3,2,1,0:T(8,128)(2,1)S(1)} %after.3.refs_0_), channel_id=1, source_target_pairs={{0,96},{1,97},{2,98},{3,99},{4,100},{5,101},{6,102},{7,103},{8,104... | collective-permute-start | bytes 1572872 | tf_op jit(solution)/shard_map/ppermute | solution.py:34
  95.7 2.7 %collective-permute-start.15 = (bf16[2,2,16,32,128]{4,3,2,1,0:T(8,128)(2,1)}, bf16[2,2,16,32,128]{4,3,2,1,0:T(8,128)(2,1)}, u32[]{:S(2)}, u32[]{:S(2)}) collective-permute-start(bf16[2,2,16,32,128]{4,3,2,1,0:T(8,128)(2,1)} %collective-permute-done.13.refs_3_), channel_id=1, source_target_pairs={{0,7},{1,0},{2,1},{3,2},{4,3},{5,4},{6,5},{7,6},{8,15},{9,8},{10,9... | collective-permute-start | bytes 1572872 | tf_op jit(solution)/shard_map/ppermute | solution.py:34
  98.5 1.4 collective-permute-done.17.refs_3_
  100.0 10.8 %collective-permute-done.18.refs_4_ = bf16[2,1,16,32,128]{4,3,2,1,0:T(8,128)(2,1)S(1)} collective-permute-done((bf16[2,1,16,32,128]{4,3,2,1,0:T(8,128)(2,1)S(1)}, bf16[2,1,16,32,128]{4,3,2,1,0:T(8,128)(2,1)S(1)}, u32[]{:S(2)}, u32[]{:S(2)}) %collective-permute-start.18) | collective-permute-done | bytes 262176 | tf_op jit(solution)/shard_map/ppermute | solution.py:34
  112.6 1.0 copy-done.3
  116.7 3.5 %gram_part.4 = (f32[1,320,512]{2,1,0:T(8,128)S(1)}, f32[1,320,512]{2,1,0:T(8,128)S(1)}) custom-call(s32[6]{0:T(128)S(1)} %stack.57.where, bf16[512,2048]{1,0:T(8,128)(2,1)S(1)} %columns.3.refs_0_.refs_1_, bf16[2,2,16,32,128]{4,3,2,1,0:T(8,128)(2,1)S(1)} %copy-done.16, bf16[2,2,16,32,128]{4,3,2,1,0:T(8,128)(2,1)} %collective-permute-done.12.refs_2_, ...), custom_call_target="tpu_custom_call" | custom-call | flops 1342177280 | bytes 4000000 | tf_op jit(solution)/shard_map/gram_part/pallas_call | solution.py:289
  120.2 2.7 %collective-permute-start.19 = (f32[1,320,512]{2,1,0:T(8,128)S(1)}, f32[1,320,512]{2,1,0:T(8,128)S(1)}, u32[]{:S(2)}, u32[]{:S(2)}) collective-permute-start(f32[1,320,512]{2,1,0:T(8,128)S(1)} %get-tuple-element.24), channel_id=1, source_target_pairs={{0,16},{1,17},{2,18},{3,19},{4,20},{5,21},{6,22},{7,23},{8,24},{9,... | collective-permute-start | bytes 1966088 | tf_op jit(solution)/shard_map/ppermute | solution.py:34
  122.9 2.7 %collective-permute-start.22 = (bf16[2,2,16,32,128]{4,3,2,1,0:T(8,128)(2,1)}, bf16[2,2,16,32,128]{4,3,2,1,0:T(8,128)(2,1)S(1)}, u32[]{:S(2)}, u32[]{:S(2)}) collective-permute-start(bf16[2,2,16,32,128]{4,3,2,1,0:T(8,128)(2,1)} %collective-permute-done.15.refs_5_), channel_id=1, source_target_pairs={{0,7},{1,0},{2,1},{3,2},{4,3},{5,4},{6,5},{7,6},{8,15},{9,8},{10,9... | collective-permute-start | bytes 1572872 | tf_op jit(solution)/shard_map/ppermute | solution.py:34
  127.3 1.1 collective-permute-start.10
  129.1 2.4 %collective-permute-start.11 = (bf16[2,1,16,32,128]{4,3,2,1,0:T(8,128)(2,1)}, bf16[2,1,16,32,128]{4,3,2,1,0:T(8,128)(2,1)}, u32[]{:S(2)}, u32[]{:S(2)}) collective-permute-start(bf16[2,1,16,32,128]{4,3,2,1,0:T(8,128)(2,1)} %slice.43), channel_id=1, source_target_pairs={{0,96},{1,97},{2,98},{3,99},{4,100},{5,101},{6,102},{7,103},{8,104... | collective-permute-start | bytes 786440 | tf_op jit(solution)/shard_map/ppermute | solution.py:34
  131.4 6.5 %collective-permute-done.21.refs_2_ = bf16[2,2,16,32,128]{4,3,2,1,0:T(8,128)(2,1)S(1)} collective-permute-done((bf16[2,2,16,32,128]{4,3,2,1,0:T(8,128)(2,1)}, bf16[2,2,16,32,128]{4,3,2,1,0:T(8,128)(2,1)S(1)}, u32[]{:S(2)}, u32[]{:S(2)}) %collective-permute-start.21) | collective-permute-done | bytes 524320 | tf_op jit(solution)/shard_map/ppermute | solution.py:34
  141.0 2.7 %collective-permute-start.24 = (bf16[1,2,16,32,128]{4,3,2,1,0:T(8,128)(2,1)}, bf16[1,2,16,32,128]{4,3,2,1,0:T(8,128)(2,1)}, u32[]{:S(2)}, u32[]{:S(2)}) collective-permute-start(bf16[1,2,16,32,128]{4,3,2,1,0:T(8,128)(2,1)} %slice.47), channel_id=1, source_target_pairs={{0,7},{1,0},{2,1},{3,2},{4,3},{5,4},{6,5},{7,6},{8,15},{9,8},{10,9... | collective-permute-start | bytes 786440 | tf_op jit(solution)/shard_map/ppermute | solution.py:34
  144.8 1.5 columns.2.refs_0_
  146.3 3.6 %gram_part.3 = (f32[1,320,512]{2,1,0:T(8,128)S(1)}, f32[1,320,512]{2,1,0:T(8,128)S(1)}) custom-call(s32[6]{0:T(128)S(1)} %stack.57.where, bf16[512,2048]{1,0:T(8,128)(2,1)S(1)} %columns.2.refs_0_, bf16[2,2,16,32,128]{4,3,2,1,0:T(8,128)(2,1)S(1)} %copy-done.17, bf16[2,2,16,32,128]{4,3,2,1,0:T(8,128)(2,1)} %collective-permute-done.12.refs_2_, ...), custom_call_target="tpu_custom_call" | custom-call | flops 1342177280 | bytes 4000000 | tf_op jit(solution)/shard_map/gram_part/pallas_call | solution.py:289
  150.0 3.1 %gram_part.5 = (f32[2,192,512]{2,1,0:T(8,128)S(1)}, f32[2,192,512]{2,1,0:T(8,128)S(1)}) custom-call(s32[6]{0:T(128)S(1)} %stack.57.where, bf16[512,2048]{1,0:T(8,128)(2,1)S(1)} %columns.2.refs_0_, bf16[512,2048]{1,0:T(8,128)(2,1)S(1)} %columns.3.refs_0_.refs_1_, bf16[2,2,16,32,128]{4,3,2,1,0:T(8,128)(2,1)S(1)} %copy-done.7, ...), custom_call_target="tpu_custom_call" | custom-call | flops 1610612736 | bytes 4000000 | tf_op jit(solution)/shard_map/gram_part/pallas_call | solution.py:289
  153.1 1.4 collective-permute-start.25
  154.6 1.8 %collective-permute-done.25.refs_4_ = f32[2,192,512]{2,1,0:T(8,128)S(1)} collective-permute-done((f32[2,192,512]{2,1,0:T(8,128)S(1)}, f32[2,192,512]{2,1,0:T(8,128)S(1)}, u32[]{:S(2)}, u32[]{:S(2)}) %collective-permute-start.25) | collective-permute-done | bytes 786464 | tf_op jit(solution)/shard_map/ppermute | solution.py:34
  156.5 2.1 %collective-permute-start.26 = (f32[192,512]{1,0:T(8,128)S(1)}, f32[192,512]{1,0:T(8,128)S(1)}, u32[]{:S(2)}, u32[]{:S(2)}) collective-permute-start(f32[192,512]{1,0:T(8,128)S(1)} %fusion), channel_id=1, source_target_pairs={{0,8},{1,9},{2,10},{3,11},{4,12},{5,13},{6,14},{7,15},{8,0},{9,1},... | collective-permute-start | bytes 1179656 | tf_op jit(solution)/shard_map/ppermute | solution.py:34
  158.6 9.2 %collective-permute-done.26.refs_5_ = f32[192,512]{1,0:T(8,128)S(1)} collective-permute-done((f32[192,512]{1,0:T(8,128)S(1)}, f32[192,512]{1,0:T(8,128)S(1)}, u32[]{:S(2)}, u32[]{:S(2)}) %collective-permute-start.26) | collective-permute-done | bytes 393248 | tf_op jit(solution)/shard_map/ppermute | solution.py:34
  167.8 2.4 %finish.1 = f32[512,512]{1,0:T(8,128)} custom-call(s32[6]{0:T(128)S(1)} %stack.57.where, f32[512,512]{1,0:T(8,128)S(1)} %copy-done.10, f32[1,320,512]{2,1,0:T(8,128)S(1)} %get-tuple-element.21.refs_7_.refs_0_, f32[1,320,512]{2,1,0:T(8,128)S(1)} %collective-permute-done.16.refs_1_, f32[320,512]{1,0:T(8,128)} %collective-permute-done.20.refs_6_.refs_2_, ...), custom_call_target="tpu_custom_call" | custom-call | flops 1000000 | bytes 5000000 | tf_op jit(solution)/shard_map/finish/pallas_call | solution.py:325
  (96 shorter events, 16.1 us)
Async XLA Ops:
  4.2 31.5 %copy-start.18 = (bf16[256,256]{1,0:T(8,128)(2,1)S(1)}, bf16[256,256]{1,0:T(8,128)(2,1)}, u32[]{:S(2)}) copy-start(bf16[256,256]{1,0:T(8,128)(2,1)} %constant.116.fwd) | copy-start | bytes 393220
  4.2 31.5 %copy-start.19 = (bf16[256,256]{1,0:T(8,128)(2,1)S(1)}, bf16[256,256]{1,0:T(8,128)(2,1)}, u32[]{:S(2)}) copy-start(bf16[256,256]{1,0:T(8,128)(2,1)} %constant.117.bwd) | copy-start | bytes 393220
  4.2 31.5 %copy-start.20 = (f32[128,128]{1,0:T(8,128)S(1)}, f32[128,128]{1,0:T(8,128)}, u32[]{:S(2)}) copy-start(f32[128,128]{1,0:T(8,128)} %constant.112.clone.t_cos) | copy-start | bytes 196612
  4.3 31.5 %copy-start.21 = (f32[128,128]{1,0:T(8,128)S(1)}, f32[128,128]{1,0:T(8,128)}, u32[]{:S(2)}) copy-start(f32[128,128]{1,0:T(8,128)} %constant.113.clone.t_sin) | copy-start | bytes 196612
  4.3 31.5 %all-to-all-start = ((bf16[16,96,512]{2,1,0:T(8,128)(2,1)}), bf16[16,96,512]{2,1,0:T(8,128)(2,1)S(1)}, u32[]{:S(2)}, u32[]{:S(2)}) async-start(bf16[16,96,512]{2,1,0:T(8,128)(2,1)} %prepare.1), calls=%async_computation | async-start | bytes 3145728 | tf_op jit(solution)/shard_map/all_to_all | solution.py:350
  42.1 2.2 %collective-permute-start = (bf16[2,16,32,128]{3,2,1,0:T(8,128)(2,1)S(1)}, bf16[2,16,32,128]{3,2,1,0:T(8,128)(2,1)S(1)}, u32[]{:S(2)}, u32[]{:S(2)}) collective-permute-start(bf16[2,16,32,128]{3,2,1,0:T(8,128)(2,1)S(1)} %get-tuple-element.17), channel_id=1, source_target_pairs={{0,16},{1,17},{2,18},{3,19},{4,20},{5,21},{6,22},{7,23},{8,24},{9,... | collective-permute-start | bytes 786440 | tf_op jit(solution)/shard_map/ppermute | solution.py:34
  44.3 9.1 %collective-permute-start.1 = (bf16[2,16,32,128]{3,2,1,0:T(8,128)(2,1)S(1)}, bf16[2,16,32,128]{3,2,1,0:T(8,128)(2,1)S(1)}, u32[]{:S(2)}, u32[]{:S(2)}) collective-permute-start(bf16[2,16,32,128]{3,2,1,0:T(8,128)(2,1)S(1)} %get-tuple-element.30.refs_4_.refs_0_), channel_id=1, source_target_pairs={{0,128},{1,129},{2,130},{3,131},{4,132},{5,133},{6,134},{7,135},{8... | collective-permute-start | bytes 786440 | tf_op jit(solution)/shard_map/ppermute | solution.py:34
  44.9 8.6 %collective-permute-start.2 = (bf16[2,16,32,128]{3,2,1,0:T(8,128)(2,1)S(1)}, bf16[2,16,32,128]{3,2,1,0:T(8,128)(2,1)S(1)}, u32[]{:S(2)}, u32[]{:S(2)}) collective-permute-start(bf16[2,16,32,128]{3,2,1,0:T(8,128)(2,1)S(1)} %get-tuple-element.28), channel_id=1, source_target_pairs={{0,0},{1,1},{2,38},{3,39},{4,68},{5,69},{6,98},{7,99},{8,128},{9,1... | collective-permute-start | bytes 786440 | tf_op jit(solution)/shard_map/ppermute | solution.py:34
  45.5 30.4 %collective-permute-start.3 = (bf16[2,16,32,128]{3,2,1,0:T(8,128)(2,1)S(1)}, bf16[2,16,32,128]{3,2,1,0:T(8,128)(2,1)S(1)}, u32[]{:S(2)}, u32[]{:S(2)}) collective-permute-start(bf16[2,16,32,128]{3,2,1,0:T(8,128)(2,1)S(1)} %get-tuple-element.27), channel_id=1, source_target_pairs={{0,8},{1,9},{2,46},{3,47},{4,76},{5,77},{6,106},{7,107},{8,136},{9... | collective-permute-start | bytes 786440 | tf_op jit(solution)/shard_map/ppermute | solution.py:34
  49.1 26.9 %collective-permute-start.4 = (bf16[2,16,32,128]{3,2,1,0:T(8,128)(2,1)S(1)}, bf16[2,16,32,128]{3,2,1,0:T(8,128)(2,1)S(1)}, u32[]{:S(2)}, u32[]{:S(2)}) collective-permute-start(bf16[2,16,32,128]{3,2,1,0:T(8,128)(2,1)S(1)} %get-tuple-element.29), channel_id=1, source_target_pairs={{0,136},{1,137},{2,138},{3,139},{4,140},{5,141},{6,142},{7,143},{8... | collective-permute-start | bytes 786440 | tf_op jit(solution)/shard_map/ppermute | solution.py:34
  51.0 24.9 %collective-permute-start.5 = (bf16[2,16,32,128]{3,2,1,0:T(8,128)(2,1)S(1)}, bf16[2,16,32,128]{3,2,1,0:T(8,128)(2,1)S(1)}, u32[]{:S(2)}, u32[]{:S(2)}) collective-permute-start(bf16[2,16,32,128]{3,2,1,0:T(8,128)(2,1)S(1)} %get-tuple-element.29), channel_id=1, source_target_pairs={{0,8},{1,9},{2,10},{3,11},{4,12},{5,13},{6,14},{7,15},{8,128},{9,1... | collective-permute-start | bytes 786440 | tf_op jit(solution)/shard_map/ppermute | solution.py:34
  76.1 16.2 %collective-permute-start.6 = (bf16[2,2,16,32,128]{4,3,2,1,0:T(8,128)(2,1)S(1)}, bf16[2,2,16,32,128]{4,3,2,1,0:T(8,128)(2,1)S(1)}, u32[]{:S(2)}, u32[]{:S(2)}) collective-permute-start(bf16[2,2,16,32,128]{4,3,2,1,0:T(8,128)(2,1)S(1)} %get-tuple-element.19.refs_0_), channel_id=1, source_target_pairs={{0,32},{1,33},{2,34},{3,35},{4,36},{5,37},{6,38},{7,39},{8,40},{9,... | collective-permute-start | bytes 1572872 | tf_op jit(solution)/shard_map/ppermute | solution.py:34
  76.2 16.2 %collective-permute-start.7 = (bf16[2,2,16,32,128]{4,3,2,1,0:T(8,128)(2,1)S(1)}, bf16[2,2,16,32,128]{4,3,2,1,0:T(8,128)(2,1)S(1)}, u32[]{:S(2)}, u32[]{:S(2)}) collective-permute-start(bf16[2,2,16,32,128]{4,3,2,1,0:T(8,128)(2,1)S(1)} %get-tuple-element.19.refs_0_), channel_id=1, source_target_pairs={{0,96},{1,97},{2,98},{3,99},{4,100},{5,101},{6,102},{7,103},{8,104... | collective-permute-start | bytes 1572872 | tf_op jit(solution)/shard_map/ppermute | solution.py:34
  80.9 14.8 %collective-permute-start.12 = (bf16[2,2,16,32,128]{4,3,2,1,0:T(8,128)(2,1)S(1)}, bf16[2,2,16,32,128]{4,3,2,1,0:T(8,128)(2,1)}, u32[]{:S(2)}, u32[]{:S(2)}) collective-permute-start(bf16[2,2,16,32,128]{4,3,2,1,0:T(8,128)(2,1)S(1)} %get-tuple-element.20.refs_1_), channel_id=1, source_target_pairs={{0,1},{1,2},{2,3},{3,4},{4,5},{5,6},{6,7},{7,0},{8,9},{9,10},{10,1... | collective-permute-start | bytes 1572872 | tf_op jit(solution)/shard_map/ppermute | solution.py:34
  80.9 14.8 %collective-permute-start.13 = (bf16[2,2,16,32,128]{4,3,2,1,0:T(8,128)(2,1)S(1)}, bf16[2,2,16,32,128]{4,3,2,1,0:T(8,128)(2,1)}, u32[]{:S(2)}, u32[]{:S(2)}) collective-permute-start(bf16[2,2,16,32,128]{4,3,2,1,0:T(8,128)(2,1)S(1)} %get-tuple-element.20.refs_1_), channel_id=1, source_target_pairs={{0,7},{1,0},{2,1},{3,2},{4,3},{5,4},{6,5},{7,6},{8,15},{9,8},{10,9... | collective-permute-start | bytes 1572872 | tf_op jit(solution)/shard_map/ppermute | solution.py:34
  92.3 7.6 %collective-permute-start.17 = (bf16[2,1,16,32,128]{4,3,2,1,0:T(8,128)(2,1)S(1)}, bf16[2,1,16,32,128]{4,3,2,1,0:T(8,128)(2,1)S(1)}, u32[]{:S(2)}, u32[]{:S(2)}) collective-permute-start(bf16[2,1,16,32,128]{4,3,2,1,0:T(8,128)(2,1)S(1)} %slice.44), channel_id=1, source_target_pairs={{0,32},{1,33},{2,34},{3,35},{4,36},{5,37},{6,38},{7,39},{8,40},{9,... | collective-permute-start | bytes 786440 | tf_op jit(solution)/shard_map/ppermute | solution.py:34
  93.1 18.5 %collective-permute-start.8 = (bf16[2,2,16,32,128]{4,3,2,1,0:T(8,128)(2,1)S(1)}, bf16[2,2,16,32,128]{4,3,2,1,0:T(8,128)(2,1)S(1)}, u32[]{:S(2)}, u32[]{:S(2)}) collective-permute-start(bf16[2,2,16,32,128]{4,3,2,1,0:T(8,128)(2,1)S(1)} %after.3.refs_0_), channel_id=1, source_target_pairs={{0,32},{1,33},{2,34},{3,35},{4,36},{5,37},{6,38},{7,39},{8,40},{9,... | collective-permute-start | bytes 1572872 | tf_op jit(solution)/shard_map/ppermute | solution.py:34
  93.1 18.5 %collective-permute-start.9 = (bf16[2,2,16,32,128]{4,3,2,1,0:T(8,128)(2,1)S(1)}, bf16[2,2,16,32,128]{4,3,2,1,0:T(8,128)(2,1)S(1)}, u32[]{:S(2)}, u32[]{:S(2)}) collective-permute-start(bf16[2,2,16,32,128]{4,3,2,1,0:T(8,128)(2,1)S(1)} %after.3.refs_0_), channel_id=1, source_target_pairs={{0,96},{1,97},{2,98},{3,99},{4,100},{5,101},{6,102},{7,103},{8,104... | collective-permute-start | bytes 1572872 | tf_op jit(solution)/shard_map/ppermute | solution.py:34
  95.7 20.8 %collective-permute-start.14 = (bf16[2,2,16,32,128]{4,3,2,1,0:T(8,128)(2,1)}, bf16[2,2,16,32,128]{4,3,2,1,0:T(8,128)(2,1)}, u32[]{:S(2)}, u32[]{:S(2)}) collective-permute-start(bf16[2,2,16,32,128]{4,3,2,1,0:T(8,128)(2,1)} %collective-permute-done.12.refs_2_), channel_id=1, source_target_pairs={{0,1},{1,2},{2,3},{3,4},{4,5},{5,6},{6,7},{7,0},{8,9},{9,10},{10,1... | collective-permute-start | bytes 1572872 | tf_op jit(solution)/shard_map/ppermute | solution.py:34
  95.7 20.8 %collective-permute-start.15 = (bf16[2,2,16,32,128]{4,3,2,1,0:T(8,128)(2,1)}, bf16[2,2,16,32,128]{4,3,2,1,0:T(8,128)(2,1)}, u32[]{:S(2)}, u32[]{:S(2)}) collective-permute-start(bf16[2,2,16,32,128]{4,3,2,1,0:T(8,128)(2,1)} %collective-permute-done.13.refs_3_), channel_id=1, source_target_pairs={{0,7},{1,0},{2,1},{3,2},{4,3},{5,4},{6,5},{7,6},{8,15},{9,8},{10,9... | collective-permute-start | bytes 1572872 | tf_op jit(solution)/shard_map/ppermute | solution.py:34
  99.9 10.9 %collective-permute-start.18 = (bf16[2,1,16,32,128]{4,3,2,1,0:T(8,128)(2,1)S(1)}, bf16[2,1,16,32,128]{4,3,2,1,0:T(8,128)(2,1)S(1)}, u32[]{:S(2)}, u32[]{:S(2)}) collective-permute-start(bf16[2,1,16,32,128]{4,3,2,1,0:T(8,128)(2,1)S(1)} %slice.45), channel_id=1, source_target_pairs={{0,96},{1,97},{2,98},{3,99},{4,100},{5,101},{6,102},{7,103},{8,104... | collective-permute-start | bytes 786440 | tf_op jit(solution)/shard_map/ppermute | solution.py:34
  120.2 5.4 %collective-permute-start.19 = (f32[1,320,512]{2,1,0:T(8,128)S(1)}, f32[1,320,512]{2,1,0:T(8,128)S(1)}, u32[]{:S(2)}, u32[]{:S(2)}) collective-permute-start(f32[1,320,512]{2,1,0:T(8,128)S(1)} %get-tuple-element.24), channel_id=1, source_target_pairs={{0,16},{1,17},{2,18},{3,19},{4,20},{5,21},{6,22},{7,23},{8,24},{9,... | collective-permute-start | bytes 1966088 | tf_op jit(solution)/shard_map/ppermute | solution.py:34
  122.9 15.0 %collective-permute-start.21 = (bf16[2,2,16,32,128]{4,3,2,1,0:T(8,128)(2,1)}, bf16[2,2,16,32,128]{4,3,2,1,0:T(8,128)(2,1)S(1)}, u32[]{:S(2)}, u32[]{:S(2)}) collective-permute-start(bf16[2,2,16,32,128]{4,3,2,1,0:T(8,128)(2,1)} %collective-permute-done.14.refs_4_), channel_id=1, source_target_pairs={{0,1},{1,2},{2,3},{3,4},{4,5},{5,6},{6,7},{7,0},{8,9},{9,10},{10,1... | collective-permute-start | bytes 1572872 | tf_op jit(solution)/shard_map/ppermute | solution.py:34
  122.9 16.5 %collective-permute-start.22 = (bf16[2,2,16,32,128]{4,3,2,1,0:T(8,128)(2,1)}, bf16[2,2,16,32,128]{4,3,2,1,0:T(8,128)(2,1)S(1)}, u32[]{:S(2)}, u32[]{:S(2)}) collective-permute-start(bf16[2,2,16,32,128]{4,3,2,1,0:T(8,128)(2,1)} %collective-permute-done.15.refs_5_), channel_id=1, source_target_pairs={{0,7},{1,0},{2,1},{3,2},{4,3},{5,4},{6,5},{7,6},{8,15},{9,8},{10,9... | collective-permute-start | bytes 1572872 | tf_op jit(solution)/shard_map/ppermute | solution.py:34
  126.6 23.4 %collective-permute-start.20 = (f32[320,512]{1,0:T(8,128)}, f32[320,512]{1,0:T(8,128)}, u32[]{:S(2)}, u32[]{:S(2)}) collective-permute-start(f32[320,512]{1,0:T(8,128)} %add_bitcast_fusion), channel_id=1, source_target_pairs={{0,8},{1,9},{2,10},{3,11},{4,12},{5,13},{6,14},{7,15},{8,0},{9,1},... | collective-permute-start | bytes 1966088 | tf_op jit(solution)/shard_map/ppermute | solution.py:34
  127.3 16.4 %collective-permute-start.10 = (bf16[2,1,16,32,128]{4,3,2,1,0:T(8,128)(2,1)}, bf16[2,1,16,32,128]{4,3,2,1,0:T(8,128)(2,1)}, u32[]{:S(2)}, u32[]{:S(2)}) collective-permute-start(bf16[2,1,16,32,128]{4,3,2,1,0:T(8,128)(2,1)} %slice.42), channel_id=1, source_target_pairs={{0,32},{1,33},{2,34},{3,35},{4,36},{5,37},{6,38},{7,39},{8,40},{9,... | collective-permute-start | bytes 786440 | tf_op jit(solution)/shard_map/ppermute | solution.py:34
  129.1 14.7 %collective-permute-start.11 = (bf16[2,1,16,32,128]{4,3,2,1,0:T(8,128)(2,1)}, bf16[2,1,16,32,128]{4,3,2,1,0:T(8,128)(2,1)}, u32[]{:S(2)}, u32[]{:S(2)}) collective-permute-start(bf16[2,1,16,32,128]{4,3,2,1,0:T(8,128)(2,1)} %slice.43), channel_id=1, source_target_pairs={{0,96},{1,97},{2,98},{3,99},{4,100},{5,101},{6,102},{7,103},{8,104... | collective-permute-start | bytes 786440 | tf_op jit(solution)/shard_map/ppermute | solution.py:34
  139.4 10.5 %collective-permute-start.23 = (bf16[1,2,16,32,128]{4,3,2,1,0:T(8,128)(2,1)}, bf16[1,2,16,32,128]{4,3,2,1,0:T(8,128)(2,1)S(1)}, u32[]{:S(2)}, u32[]{:S(2)}) collective-permute-start(bf16[1,2,16,32,128]{4,3,2,1,0:T(8,128)(2,1)} %slice.46), channel_id=1, source_target_pairs={{0,1},{1,2},{2,3},{3,4},{4,5},{5,6},{6,7},{7,0},{8,9},{9,10},{10,1... | collective-permute-start | bytes 786440 | tf_op jit(solution)/shard_map/ppermute | solution.py:34
  141.0 8.9 %collective-permute-start.24 = (bf16[1,2,16,32,128]{4,3,2,1,0:T(8,128)(2,1)}, bf16[1,2,16,32,128]{4,3,2,1,0:T(8,128)(2,1)}, u32[]{:S(2)}, u32[]{:S(2)}) collective-permute-start(bf16[1,2,16,32,128]{4,3,2,1,0:T(8,128)(2,1)} %slice.47), channel_id=1, source_target_pairs={{0,7},{1,0},{2,1},{3,2},{4,3},{5,4},{6,5},{7,6},{8,15},{9,8},{10,9... | collective-permute-start | bytes 786440 | tf_op jit(solution)/shard_map/ppermute | solution.py:34
  153.1 3.4 %collective-permute-start.25 = (f32[2,192,512]{2,1,0:T(8,128)S(1)}, f32[2,192,512]{2,1,0:T(8,128)S(1)}, u32[]{:S(2)}, u32[]{:S(2)}) collective-permute-start(f32[2,192,512]{2,1,0:T(8,128)S(1)} %get-tuple-element.26), channel_id=1, source_target_pairs={{0,16},{1,17},{2,18},{3,19},{4,20},{5,21},{6,22},{7,23},{8,24},{9,... | collective-permute-start | bytes 2359304 | tf_op jit(solution)/shard_map/ppermute | solution.py:34
  154.5 4.1 %collective-permute-start.16 = (f32[1,320,512]{2,1,0:T(8,128)S(1)}, f32[1,320,512]{2,1,0:T(8,128)S(1)}, u32[]{:S(2)}, u32[]{:S(2)}) collective-permute-start(f32[1,320,512]{2,1,0:T(8,128)S(1)} %get-tuple-element.22), channel_id=1, source_target_pairs={{0,16},{1,17},{2,18},{3,19},{4,20},{5,21},{6,22},{7,23},{8,24},{9,... | collective-permute-start | bytes 1966088 | tf_op jit(solution)/shard_map/ppermute | solution.py:34
  156.5 11.3 %collective-permute-start.26 = (f32[192,512]{1,0:T(8,128)S(1)}, f32[192,512]{1,0:T(8,128)S(1)}, u32[]{:S(2)}, u32[]{:S(2)}) collective-permute-start(f32[192,512]{1,0:T(8,128)S(1)} %fusion), channel_id=1, source_target_pairs={{0,8},{1,9},{2,10},{3,11},{4,12},{5,13},{6,14},{7,15},{8,0},{9,1},... | collective-permute-start | bytes 1179656 | tf_op jit(solution)/shard_map/ppermute | solution.py:34
  (20 other events, 169.7 us)

commit v3 on v2

--- a/solution.py
+++ b/solution.py
@@ -335,7 +335,7 @@
 
 
 STEPS = (0, -1, 1, -2, 2, -3, 3, 4)
-CHUNKS = (STEPS[:5], STEPS[5:])
+CHUNKS = (STEPS[:7], STEPS[7:])
 
 
 def local(gate_in, key_in, value_in, filt_in, skip_gain, running_gram):
@@ -371,18 +371,19 @@
     (own,) = after([[same, opposite]], near_up, near_down)
     near_far = along_y(near_up[:, :1], 1), along_y(near_down[:, 1:], 3)
     own_up, own_down = along_y(own, 1), along_y(own, 3)
-    right = columns(beside, [near, near_up, near_down, *near_far], own_up, own_down)
+    right = columns(beside, [near, near_up, near_down, *near_far])
     own_far = along_y(own_up[:, :1], 1), along_y(own_down[:, 1:], 3)
     own_right = columns(across, [own, own_up, own_down, *own_far])
 
-    early = [rows, ups[1], downs[1], ups[2], downs[2]]
-    keep, send = gram_part(CHUNKS[0], where, [right], early)
-    theirs_a = other_x_lo(keep[0] + other_core(send)[0])
-    keep_a, send_a = gram_part(CHUNKS[0], where, [own_right], early)
+    early = [rows, ups[1], downs[1], ups[2], downs[2], ups[3], downs[3]]
+    keep, send = gram_part(CHUNKS[0], where, [right], early, own_right)
+    half_a = keep[0] + other_core(send)[0]
+    theirs_a = other_x_lo(half_a)
+    keep_a, send_a = gram_part(CHUNKS[0], where, [own_right], early, keep)
     got_a = other_core(send_a)
 
-    late = [ups[3], downs[3], *far]
-    keep_b, send_b = gram_part(CHUNKS[1], where, [own_right, right], late, theirs_a, keep_a)
+    late = [*far]
+    keep_b, send_b = gram_part(CHUNKS[1], where, [own_right, right], late)
     got_b = other_core(send_b)
     theirs_b = other_x_lo(keep_b[1] + got_b[1])
     return finish(

time: 171 us -> 165 us (0.965)
  starting transfers between devices: 45.1 us -> 62.1 us
  waiting for transfers between devices: 85.9 us -> 70.9 us
  local copies, waits for them, and re-layouts: 12.2 us -> 5.96 us
    ppermute x27, starting transfers between devices: 36.5 us -> 53.5 us  [move(): return lax.ppermute(array, MESH, pairs)]
    ppermute x27, waiting for transfers between devices: 63.9 us -> 48.9 us  [move(): return lax.ppermute(array, MESH, pairs)]
    unnamed x48 -> x34, local copies, waits for them, and re-layouts: 8.23 us -> 2.69 us
  transfers between devices with their start and end apart: 28 -> 28, of which waited for: 10 -> 13; matrix products, arithmetic and copies ran while one was open for 3% -> 2% of each run, Pallas kernels for 4% -> 5%
where the time goes in v3:
time: 165 us
  waiting for transfers between devices  70.9 us (43%)
  starting transfers between devices  62.1 us (38%)
  Pallas kernels  25.1 us (15%)
  local copies, waits for them, and re-layouts  5.96 us (4%)
    ppermute x27, starting transfers between devices, move(): return lax.ppermute(array, MESH, pairs)  53.5 us
    ppermute x27, waiting for transfers between devices, move(): return lax.ppermute(array, MESH, pairs)  48.9 us
    all_to_all x1, waiting for transfers between devices, local(): lax.all_to_all(outgoing, 'seq', split_axis=0, concat_axis=0, tiled=True)  22 us
    pallas_call x3, Pallas kernels, gram_part(): pl.pallas_call(functools.partial(gram_kernel, steps, len(rights), len(ear...  9.97 us
    all_to_all x1, starting transfers between devices, local(): lax.all_to_all(outgoing, 'seq', split_axis=0, concat_axis=0, tiled=True)  8.59 us
    pallas_call x1, Pallas kernels, convolve(): pl.pallas_call(conv_kernel, in_specs=[SMEM, SMEM] + [VMEM] * 7, out_specs...  6.27 us
    pallas_call x1, Pallas kernels, prepare(): pl.pallas_call(prepare_kernel, grid=(4,), in_specs=[block] * 4, out_specs...  4.3 us
  transfers between devices with their start and end apart: 28, of which 13 were waited for; matrix products, arithmetic and copies ran while one was open for 2% of the time, Pallas kernels for 5%

profile of v3, /device:TPU:1, one launch (start us, length us, event | category | flops | bytes accessed | tf_op | source)
XLA Modules:
  0.0 164.6 jit_solution(17891335933511598216)
XLA Ops:
  0.0 4.3 %prepare.1 = bf16[16,96,512]{2,1,0:T(8,128)(2,1)} custom-call(bf16[512,512]{1,0:T(8,128)(2,1)} %gate.1, bf16[512,512]{1,0:T(8,128)(2,1)} %key.1, bf16[512,512]{1,0:T(8,128)(2,1)} %value.1, bf16[512,512]{1,0:T(8,128)(2,1)} %filt.1), custom_call_target="tpu_custom_call" | custom-call | tf_op jit(solution)/shard_map/prepare/pallas_call | solution.py:125
  4.3 8.6 %all-to-all-start = ((bf16[16,96,512]{2,1,0:T(8,128)(2,1)}), bf16[16,96,512]{2,1,0:T(8,128)(2,1)S(1)}, u32[]{:S(2)}, u32[]{:S(2)}) async-start(bf16[16,96,512]{2,1,0:T(8,128)(2,1)} %prepare.1), calls=%async_computation | async-start | bytes 3145728 | tf_op jit(solution)/shard_map/all_to_all | solution.py:350
  13.8 22.0 %all-to-all-done.data = bf16[16,96,512]{2,1,0:T(8,128)(2,1)S(1)} async-done(((bf16[16,96,512]{2,1,0:T(8,128)(2,1)}), bf16[16,96,512]{2,1,0:T(8,128)(2,1)S(1)}, u32[]{:S(2)}, u32[]{:S(2)}) %all-to-all-start) | async-done | bytes 1572896 | tf_op jit(solution)/shard_map/all_to_all | solution.py:350
  35.8 6.3 %convolve.1 = (bf16[16,32,128]{2,1,0:T(8,128)(2,1)S(1)}, bf16[16,32,128]{2,1,0:T(8,128)(2,1)S(1)}, bf16[2,16,32,128]{3,2,1,0:T(8,128)(2,1)S(1)}) custom-call(s32[6]{0:T(128)S(1)} %stack.57.where, f32[32]{0:T(128)S(1)} %dynamic_slice.3.skip, bf16[16,96,512]{2,1,0:T(8,128)(2,1)S(1)} %all-to-all-done.data, bf16[256,64]{1,0:T(8,128)(2,1)S(1)} %copy-done.13, ...), custom_call_target="tpu_custom_call" | custom-call | flops 4000000000 | bytes 3000000 | tf_op jit(solution)/shard_map/convolve/pallas_call | solution.py:212
  43.1 1.2 collective-permute-done
  45.5 5.0 %collective-permute-start.5 = (bf16[2,16,32,128]{3,2,1,0:T(8,128)(2,1)S(1)}, bf16[2,16,32,128]{3,2,1,0:T(8,128)(2,1)S(1)}, u32[]{:S(2)}, u32[]{:S(2)}) collective-permute-start(bf16[2,16,32,128]{3,2,1,0:T(8,128)(2,1)S(1)} %get-tuple-element.29), channel_id=1, source_target_pairs={{0,8},{1,9},{2,10},{3,11},{4,12},{5,13},{6,14},{7,15},{8,128},{9,1... | collective-permute-start | bytes 786440 | tf_op jit(solution)/shard_map/ppermute | solution.py:34
  50.4 1.9 %collective-permute-start.1 = (bf16[2,16,32,128]{3,2,1,0:T(8,128)(2,1)S(1)}, bf16[2,16,32,128]{3,2,1,0:T(8,128)(2,1)S(1)}, u32[]{:S(2)}, u32[]{:S(2)}) collective-permute-start(bf16[2,16,32,128]{3,2,1,0:T(8,128)(2,1)S(1)} %get-tuple-element.30.refs_4_.refs_0_), channel_id=1, source_target_pairs={{0,128},{1,129},{2,130},{3,131},{4,132},{5,133},{6,134},{7,135},{8... | collective-permute-start | bytes 786440 | tf_op jit(solution)/shard_map/ppermute | solution.py:34
  52.3 13.3 %collective-permute-done.3.refs_1_ = bf16[2,16,32,128]{3,2,1,0:T(8,128)(2,1)S(1)} collective-permute-done((bf16[2,16,32,128]{3,2,1,0:T(8,128)(2,1)S(1)}, bf16[2,16,32,128]{3,2,1,0:T(8,128)(2,1)S(1)}, u32[]{:S(2)}, u32[]{:S(2)}) %collective-permute-start.3) | collective-permute-done | bytes 262176 | tf_op jit(solution)/shard_map/ppermute | solution.py:34
  65.8 9.0 %collective-permute-start.13 = (bf16[2,2,16,32,128]{4,3,2,1,0:T(8,128)(2,1)S(1)}, bf16[2,2,16,32,128]{4,3,2,1,0:T(8,128)(2,1)S(1)}, u32[]{:S(2)}, u32[]{:S(2)}) collective-permute-start(bf16[2,2,16,32,128]{4,3,2,1,0:T(8,128)(2,1)S(1)} %get-tuple-element.20.refs_1_), channel_id=1, source_target_pairs={{0,7},{1,0},{2,1},{3,2},{4,3},{5,4},{6,5},{7,6},{8,15},{9,8},{10,9... | collective-permute-start | bytes 1572872 | tf_op jit(solution)/shard_map/ppermute | solution.py:34
  74.7 3.6 %collective-permute-start.7 = (bf16[2,2,16,32,128]{4,3,2,1,0:T(8,128)(2,1)S(1)}, bf16[2,2,16,32,128]{4,3,2,1,0:T(8,128)(2,1)S(1)}, u32[]{:S(2)}, u32[]{:S(2)}) collective-permute-start(bf16[2,2,16,32,128]{4,3,2,1,0:T(8,128)(2,1)S(1)} %get-tuple-element.19.refs_0_), channel_id=1, source_target_pairs={{0,96},{1,97},{2,98},{3,99},{4,100},{5,101},{6,102},{7,103},{8,104... | collective-permute-start | bytes 1572872 | tf_op jit(solution)/shard_map/ppermute | solution.py:34
  79.1 4.8 %collective-permute-done.13.refs_3_ = bf16[2,2,16,32,128]{4,3,2,1,0:T(8,128)(2,1)S(1)} collective-permute-done((bf16[2,2,16,32,128]{4,3,2,1,0:T(8,128)(2,1)S(1)}, bf16[2,2,16,32,128]{4,3,2,1,0:T(8,128)(2,1)S(1)}, u32[]{:S(2)}, u32[]{:S(2)}) %collective-permute-start.13) | collective-permute-done | bytes 524320 | tf_op jit(solution)/shard_map/ppermute | solution.py:34
  83.9 7.4 %collective-permute-start.15 = (bf16[2,2,16,32,128]{4,3,2,1,0:T(8,128)(2,1)S(1)}, bf16[2,2,16,32,128]{4,3,2,1,0:T(8,128)(2,1)}, u32[]{:S(2)}, u32[]{:S(2)}) collective-permute-start(bf16[2,2,16,32,128]{4,3,2,1,0:T(8,128)(2,1)S(1)} %collective-permute-done.13.refs_3_), channel_id=1, source_target_pairs={{0,7},{1,0},{2,1},{3,2},{4,3},{5,4},{6,5},{7,6},{8,15},{9,8},{10,9... | collective-permute-start | bytes 1572872 | tf_op jit(solution)/shard_map/ppermute | solution.py:34
  92.2 1.5 collective-permute-start.8
  93.7 1.6 collective-permute-start.19
  95.2 5.3 %collective-permute-done.15.refs_5_ = bf16[2,2,16,32,128]{4,3,2,1,0:T(8,128)(2,1)} collective-permute-done((bf16[2,2,16,32,128]{4,3,2,1,0:T(8,128)(2,1)S(1)}, bf16[2,2,16,32,128]{4,3,2,1,0:T(8,128)(2,1)}, u32[]{:S(2)}, u32[]{:S(2)}) %collective-permute-start.15) | collective-permute-done | bytes 524320 | tf_op jit(solution)/shard_map/ppermute | solution.py:34
  100.5 3.5 %collective-permute-start.17 = (bf16[2,2,16,32,128]{4,3,2,1,0:T(8,128)(2,1)}, bf16[2,2,16,32,128]{4,3,2,1,0:T(8,128)(2,1)S(1)}, u32[]{:S(2)}, u32[]{:S(2)}) collective-permute-start(bf16[2,2,16,32,128]{4,3,2,1,0:T(8,128)(2,1)} %collective-permute-done.15.refs_5_), channel_id=1, source_target_pairs={{0,7},{1,0},{2,1},{3,2},{4,3},{5,4},{6,5},{7,6},{8,15},{9,8},{10,9... | collective-permute-start | bytes 1572872 | tf_op jit(solution)/shard_map/ppermute | solution.py:34
  106.2 2.7 %collective-permute-start.11 = (bf16[2,1,16,32,128]{4,3,2,1,0:T(8,128)(2,1)}, bf16[2,1,16,32,128]{4,3,2,1,0:T(8,128)(2,1)}, u32[]{:S(2)}, u32[]{:S(2)}) collective-permute-start(bf16[2,1,16,32,128]{4,3,2,1,0:T(8,128)(2,1)} %slice.43), channel_id=1, source_target_pairs={{0,96},{1,97},{2,98},{3,99},{4,100},{5,101},{6,102},{7,103},{8,104... | collective-permute-start | bytes 786440 | tf_op jit(solution)/shard_map/ppermute | solution.py:34
  110.6 1.8 %collective-permute-done.18.refs_3_ = bf16[2,1,16,32,128]{4,3,2,1,0:T(8,128)(2,1)} collective-permute-done((bf16[2,1,16,32,128]{4,3,2,1,0:T(8,128)(2,1)}, bf16[2,1,16,32,128]{4,3,2,1,0:T(8,128)(2,1)}, u32[]{:S(2)}, u32[]{:S(2)}) %collective-permute-start.18) | collective-permute-done | bytes 262176 | tf_op jit(solution)/shard_map/ppermute | solution.py:34
  113.5 1.3 columns.3.refs_0_.refs_1_
  114.9 4.3 %collective-permute-done.10.refs_3_ = bf16[2,1,16,32,128]{4,3,2,1,0:T(8,128)(2,1)} collective-permute-done((bf16[2,1,16,32,128]{4,3,2,1,0:T(8,128)(2,1)}, bf16[2,1,16,32,128]{4,3,2,1,0:T(8,128)(2,1)}, u32[]{:S(2)}, u32[]{:S(2)}) %collective-permute-start.10) | collective-permute-done | bytes 262176 | tf_op jit(solution)/shard_map/ppermute | solution.py:34
  119.3 1.4 columns.2.refs_8_.refs_0_
  120.7 3.9 %gram_part.3 = (f32[1,448,512]{2,1,0:T(8,128)S(1)}, f32[1,448,512]{2,1,0:T(8,128)S(1)}) custom-call(s32[6]{0:T(128)S(1)} %stack.57.where, bf16[512,2048]{1,0:T(8,128)(2,1)S(1)} %columns.3.refs_0_.refs_1_, bf16[2,2,16,32,128]{4,3,2,1,0:T(8,128)(2,1)S(1)} %copy-done.4, bf16[2,2,16,32,128]{4,3,2,1,0:T(8,128)(2,1)S(1)} %copy-done.8, ...), custom_call_target="tpu_custom_call" | custom-call | flops 1879048192 | bytes 4000000 | tf_op jit(solution)/shard_map/gram_part/pallas_call | solution.py:289
  124.7 3.4 %collective-permute-start.21 = (f32[1,448,512]{2,1,0:T(8,128)S(1)}, f32[1,448,512]{2,1,0:T(8,128)S(1)}, u32[]{:S(2)}, u32[]{:S(2)}) collective-permute-start(f32[1,448,512]{2,1,0:T(8,128)S(1)} %get-tuple-element.24), channel_id=1, source_target_pairs={{0,16},{1,17},{2,18},{3,19},{4,20},{5,21},{6,22},{7,23},{8,24},{9,... | collective-permute-start | bytes 2752520 | tf_op jit(solution)/shard_map/ppermute | solution.py:34
  128.1 3.0 %collective-permute-start.24 = (bf16[1,2,16,32,128]{4,3,2,1,0:T(8,128)(2,1)S(1)}, bf16[1,2,16,32,128]{4,3,2,1,0:T(8,128)(2,1)S(1)}, u32[]{:S(2)}, u32[]{:S(2)}) collective-permute-start(bf16[1,2,16,32,128]{4,3,2,1,0:T(8,128)(2,1)S(1)} %slice.47), channel_id=1, source_target_pairs={{0,7},{1,0},{2,1},{3,2},{4,3},{5,4},{6,5},{7,6},{8,15},{9,8},{10,9... | collective-permute-start | bytes 786440 | tf_op jit(solution)/shard_map/ppermute | solution.py:34
  131.2 3.9 %gram_part.4 = (f32[1,448,512]{2,1,0:T(8,128)S(1)}, f32[1,448,512]{2,1,0:T(8,128)S(1)}) custom-call(s32[6]{0:T(128)S(1)} %stack.57.where, bf16[512,2048]{1,0:T(8,128)(2,1)S(1)} %columns.2.refs_8_.refs_0_, bf16[2,2,16,32,128]{4,3,2,1,0:T(8,128)(2,1)S(1)} %copy-done.4, bf16[2,2,16,32,128]{4,3,2,1,0:T(8,128)(2,1)S(1)} %copy-done.8, ...), custom_call_target="tpu_custom_call" | custom-call | flops 1879048192 | bytes 4000000 | tf_op jit(solution)/shard_map/gram_part/pallas_call | solution.py:289
  136.0 3.5 %collective-permute-start.22 = (f32[448,512]{1,0:T(8,128)S(1)}, f32[448,512]{1,0:T(8,128)S(1)}, u32[]{:S(2)}, u32[]{:S(2)}) collective-permute-start(f32[448,512]{1,0:T(8,128)S(1)} %add_bitcast_fusion), channel_id=1, source_target_pairs={{0,8},{1,9},{2,10},{3,11},{4,12},{5,13},{6,14},{7,15},{8,0},{9,1},... | collective-permute-start | bytes 2752520 | tf_op jit(solution)/shard_map/ppermute | solution.py:34
  140.0 2.1 %gram_part.5 = (f32[2,64,512]{2,1,0:T(8,128)S(1)}, f32[2,64,512]{2,1,0:T(8,128)S(1)}) custom-call(s32[6]{0:T(128)S(1)} %stack.57.where, bf16[512,2048]{1,0:T(8,128)(2,1)S(1)} %columns.2.refs_8_.refs_0_, bf16[512,2048]{1,0:T(8,128)(2,1)S(1)} %columns.3.refs_0_.refs_1_, bf16[1,2,16,32,128]{4,3,2,1,0:T(8,128)(2,1)S(1)} %collective-permute-done.23.refs_2_, ...), custom_call_target="tpu_custom_call" | custom-call | flops 536870912 | bytes 4000000 | tf_op jit(solution)/shard_map/gram_part/pallas_call | solution.py:289
  142.1 1.2 collective-permute-start.25
  143.3 1.2 collective-permute-done.25.refs_4_
  144.5 3.5 %collective-permute-start.26 = (f32[64,512]{1,0:T(8,128)S(1)}, f32[64,512]{1,0:T(8,128)S(1)}, u32[]{:S(2)}, u32[]{:S(2)}) collective-permute-start(f32[64,512]{1,0:T(8,128)S(1)} %fusion), channel_id=1, source_target_pairs={{0,8},{1,9},{2,10},{3,11},{4,12},{5,13},{6,14},{7,15},{8,0},{9,1},... | collective-permute-start | bytes 393224 | tf_op jit(solution)/shard_map/ppermute | solution.py:34
  148.0 14.9 %collective-permute-done.26.refs_5_ = f32[64,512]{1,0:T(8,128)S(1)} collective-permute-done((f32[64,512]{1,0:T(8,128)S(1)}, f32[64,512]{1,0:T(8,128)S(1)}, u32[]{:S(2)}, u32[]{:S(2)}) %collective-permute-start.26) | collective-permute-done | bytes 131104 | tf_op jit(solution)/shard_map/ppermute | solution.py:34
  162.9 1.7 %finish.1 = f32[512,512]{1,0:T(8,128)} custom-call(s32[6]{0:T(128)S(1)} %stack.57.where, f32[512,512]{1,0:T(8,128)S(1)} %copy-done.2, f32[1,448,512]{2,1,0:T(8,128)S(1)} %get-tuple-element.22.refs_0_, f32[1,448,512]{2,1,0:T(8,128)S(1)} %collective-permute-done.20.refs_1_, f32[448,512]{1,0:T(8,128)S(1)} %collective-permute-done.22.refs_2_, ...), custom_call_target="tpu_custom_call" | custom-call | flops 1000000 | bytes 5000000 | tf_op jit(solution)/shard_map/finish/pallas_call | solution.py:325
  (82 shorter events, 11.4 us)
Async XLA Ops:
  4.3 31.5 %copy-start.11 = (bf16[256,256]{1,0:T(8,128)(2,1)S(1)}, bf16[256,256]{1,0:T(8,128)(2,1)}, u32[]{:S(2)}) copy-start(bf16[256,256]{1,0:T(8,128)(2,1)} %constant.117.bwd) | copy-start | bytes 393220
  4.3 31.5 %copy-start.12 = (bf16[256,256]{1,0:T(8,128)(2,1)S(1)}, bf16[256,256]{1,0:T(8,128)(2,1)}, u32[]{:S(2)}) copy-start(bf16[256,256]{1,0:T(8,128)(2,1)} %constant.116.fwd) | copy-start | bytes 393220
  4.3 31.5 %copy-start.13 = (bf16[256,64]{1,0:T(8,128)(2,1)S(1)}, bf16[256,64]{1,0:T(8,128)(2,1)}, u32[]{:S(2)}) copy-start(bf16[256,64]{1,0:T(8,128)(2,1)} %constant.114.first) | copy-start | bytes 98308
  4.3 31.5 %copy-start.14 = (f32[128,128]{1,0:T(8,128)S(1)}, f32[128,128]{1,0:T(8,128)}, u32[]{:S(2)}) copy-start(f32[128,128]{1,0:T(8,128)} %constant.113.clone.t_sin) | copy-start | bytes 196612
  4.3 31.4 %all-to-all-start = ((bf16[16,96,512]{2,1,0:T(8,128)(2,1)}), bf16[16,96,512]{2,1,0:T(8,128)(2,1)S(1)}, u32[]{:S(2)}, u32[]{:S(2)}) async-start(bf16[16,96,512]{2,1,0:T(8,128)(2,1)} %prepare.1), calls=%async_computation | async-start | bytes 3145728 | tf_op jit(solution)/shard_map/all_to_all | solution.py:350
  42.1 2.2 %collective-permute-start = (bf16[2,16,32,128]{3,2,1,0:T(8,128)(2,1)S(1)}, bf16[2,16,32,128]{3,2,1,0:T(8,128)(2,1)S(1)}, u32[]{:S(2)}, u32[]{:S(2)}) collective-permute-start(bf16[2,16,32,128]{3,2,1,0:T(8,128)(2,1)S(1)} %get-tuple-element.17), channel_id=1, source_target_pairs={{0,16},{1,17},{2,18},{3,19},{4,20},{5,21},{6,22},{7,23},{8,24},{9,... | collective-permute-start | bytes 786440 | tf_op jit(solution)/shard_map/ppermute | solution.py:34
  44.4 21.3 %collective-permute-start.3 = (bf16[2,16,32,128]{3,2,1,0:T(8,128)(2,1)S(1)}, bf16[2,16,32,128]{3,2,1,0:T(8,128)(2,1)S(1)}, u32[]{:S(2)}, u32[]{:S(2)}) collective-permute-start(bf16[2,16,32,128]{3,2,1,0:T(8,128)(2,1)S(1)} %get-tuple-element.27), channel_id=1, source_target_pairs={{0,8},{1,9},{2,46},{3,47},{4,76},{5,77},{6,106},{7,107},{8,136},{9... | collective-permute-start | bytes 786440 | tf_op jit(solution)/shard_map/ppermute | solution.py:34
  44.8 20.9 %collective-permute-start.2 = (bf16[2,16,32,128]{3,2,1,0:T(8,128)(2,1)S(1)}, bf16[2,16,32,128]{3,2,1,0:T(8,128)(2,1)S(1)}, u32[]{:S(2)}, u32[]{:S(2)}) collective-permute-start(bf16[2,16,32,128]{3,2,1,0:T(8,128)(2,1)S(1)} %get-tuple-element.28), channel_id=1, source_target_pairs={{0,0},{1,1},{2,38},{3,39},{4,68},{5,69},{6,98},{7,99},{8,128},{9,1... | collective-permute-start | bytes 786440 | tf_op jit(solution)/shard_map/ppermute | solution.py:34
  45.5 20.2 %collective-permute-start.5 = (bf16[2,16,32,128]{3,2,1,0:T(8,128)(2,1)S(1)}, bf16[2,16,32,128]{3,2,1,0:T(8,128)(2,1)S(1)}, u32[]{:S(2)}, u32[]{:S(2)}) collective-permute-start(bf16[2,16,32,128]{3,2,1,0:T(8,128)(2,1)S(1)} %get-tuple-element.29), channel_id=1, source_target_pairs={{0,8},{1,9},{2,10},{3,11},{4,12},{5,13},{6,14},{7,15},{8,128},{9,1... | collective-permute-start | bytes 786440 | tf_op jit(solution)/shard_map/ppermute | solution.py:34
  50.4 15.2 %collective-permute-start.4 = (bf16[2,16,32,128]{3,2,1,0:T(8,128)(2,1)S(1)}, bf16[2,16,32,128]{3,2,1,0:T(8,128)(2,1)S(1)}, u32[]{:S(2)}, u32[]{:S(2)}) collective-permute-start(bf16[2,16,32,128]{3,2,1,0:T(8,128)(2,1)S(1)} %get-tuple-element.29), channel_id=1, source_target_pairs={{0,136},{1,137},{2,138},{3,139},{4,140},{5,141},{6,142},{7,143},{8... | collective-permute-start | bytes 786440 | tf_op jit(solution)/shard_map/ppermute | solution.py:34
  50.4 15.2 %collective-permute-start.1 = (bf16[2,16,32,128]{3,2,1,0:T(8,128)(2,1)S(1)}, bf16[2,16,32,128]{3,2,1,0:T(8,128)(2,1)S(1)}, u32[]{:S(2)}, u32[]{:S(2)}) collective-permute-start(bf16[2,16,32,128]{3,2,1,0:T(8,128)(2,1)S(1)} %get-tuple-element.30.refs_4_.refs_0_), channel_id=1, source_target_pairs={{0,128},{1,129},{2,130},{3,131},{4,132},{5,133},{6,134},{7,135},{8... | collective-permute-start | bytes 786440 | tf_op jit(solution)/shard_map/ppermute | solution.py:34
  65.8 18.2 %collective-permute-start.13 = (bf16[2,2,16,32,128]{4,3,2,1,0:T(8,128)(2,1)S(1)}, bf16[2,2,16,32,128]{4,3,2,1,0:T(8,128)(2,1)S(1)}, u32[]{:S(2)}, u32[]{:S(2)}) collective-permute-start(bf16[2,2,16,32,128]{4,3,2,1,0:T(8,128)(2,1)S(1)} %get-tuple-element.20.refs_1_), channel_id=1, source_target_pairs={{0,7},{1,0},{2,1},{3,2},{4,3},{5,4},{6,5},{7,6},{8,15},{9,8},{10,9... | collective-permute-start | bytes 1572872 | tf_op jit(solution)/shard_map/ppermute | solution.py:34
  74.7 17.3 %collective-permute-start.12 = (bf16[2,2,16,32,128]{4,3,2,1,0:T(8,128)(2,1)S(1)}, bf16[2,2,16,32,128]{4,3,2,1,0:T(8,128)(2,1)S(1)}, u32[]{:S(2)}, u32[]{:S(2)}) collective-permute-start(bf16[2,2,16,32,128]{4,3,2,1,0:T(8,128)(2,1)S(1)} %get-tuple-element.20.refs_1_), channel_id=1, source_target_pairs={{0,1},{1,2},{2,3},{3,4},{4,5},{5,6},{6,7},{7,0},{8,9},{9,10},{10,1... | collective-permute-start | bytes 1572872 | tf_op jit(solution)/shard_map/ppermute | solution.py:34
  74.7 17.3 %collective-permute-start.7 = (bf16[2,2,16,32,128]{4,3,2,1,0:T(8,128)(2,1)S(1)}, bf16[2,2,16,32,128]{4,3,2,1,0:T(8,128)(2,1)S(1)}, u32[]{:S(2)}, u32[]{:S(2)}) collective-permute-start(bf16[2,2,16,32,128]{4,3,2,1,0:T(8,128)(2,1)S(1)} %get-tuple-element.19.refs_0_), channel_id=1, source_target_pairs={{0,96},{1,97},{2,98},{3,99},{4,100},{5,101},{6,102},{7,103},{8,104... | collective-permute-start | bytes 1572872 | tf_op jit(solution)/shard_map/ppermute | solution.py:34
  78.3 13.7 %collective-permute-start.6 = (bf16[2,2,16,32,128]{4,3,2,1,0:T(8,128)(2,1)S(1)}, bf16[2,2,16,32,128]{4,3,2,1,0:T(8,128)(2,1)S(1)}, u32[]{:S(2)}, u32[]{:S(2)}) collective-permute-start(bf16[2,2,16,32,128]{4,3,2,1,0:T(8,128)(2,1)S(1)} %get-tuple-element.19.refs_0_), channel_id=1, source_target_pairs={{0,32},{1,33},{2,34},{3,35},{4,36},{5,37},{6,38},{7,39},{8,40},{9,... | collective-permute-start | bytes 1572872 | tf_op jit(solution)/shard_map/ppermute | solution.py:34
  83.9 16.6 %collective-permute-start.15 = (bf16[2,2,16,32,128]{4,3,2,1,0:T(8,128)(2,1)S(1)}, bf16[2,2,16,32,128]{4,3,2,1,0:T(8,128)(2,1)}, u32[]{:S(2)}, u32[]{:S(2)}) collective-permute-start(bf16[2,2,16,32,128]{4,3,2,1,0:T(8,128)(2,1)S(1)} %collective-permute-done.13.refs_3_), channel_id=1, source_target_pairs={{0,7},{1,0},{2,1},{3,2},{4,3},{5,4},{6,5},{7,6},{8,15},{9,8},{10,9... | collective-permute-start | bytes 1572872 | tf_op jit(solution)/shard_map/ppermute | solution.py:34
  92.0 12.7 %collective-permute-start.14 = (bf16[2,2,16,32,128]{4,3,2,1,0:T(8,128)(2,1)S(1)}, bf16[2,2,16,32,128]{4,3,2,1,0:T(8,128)(2,1)}, u32[]{:S(2)}, u32[]{:S(2)}) collective-permute-start(bf16[2,2,16,32,128]{4,3,2,1,0:T(8,128)(2,1)S(1)} %collective-permute-done.12.refs_2_), channel_id=1, source_target_pairs={{0,1},{1,2},{2,3},{3,4},{4,5},{5,6},{6,7},{7,0},{8,9},{9,10},{10,1... | collective-permute-start | bytes 1572872 | tf_op jit(solution)/shard_map/ppermute | solution.py:34
  92.1 13.4 %collective-permute-start.9 = (bf16[2,2,16,32,128]{4,3,2,1,0:T(8,128)(2,1)S(1)}, bf16[2,2,16,32,128]{4,3,2,1,0:T(8,128)(2,1)S(1)}, u32[]{:S(2)}, u32[]{:S(2)}) collective-permute-start(bf16[2,2,16,32,128]{4,3,2,1,0:T(8,128)(2,1)S(1)} %after.3.refs_0_), channel_id=1, source_target_pairs={{0,96},{1,97},{2,98},{3,99},{4,100},{5,101},{6,102},{7,103},{8,104... | collective-permute-start | bytes 1572872 | tf_op jit(solution)/shard_map/ppermute | solution.py:34
  92.2 14.0 %collective-permute-start.8 = (bf16[2,2,16,32,128]{4,3,2,1,0:T(8,128)(2,1)S(1)}, bf16[2,2,16,32,128]{4,3,2,1,0:T(8,128)(2,1)S(1)}, u32[]{:S(2)}, u32[]{:S(2)}) collective-permute-start(bf16[2,2,16,32,128]{4,3,2,1,0:T(8,128)(2,1)S(1)} %after.3.refs_0_), channel_id=1, source_target_pairs={{0,32},{1,33},{2,34},{3,35},{4,36},{5,37},{6,38},{7,39},{8,40},{9,... | collective-permute-start | bytes 1572872 | tf_op jit(solution)/shard_map/ppermute | solution.py:34
  93.7 16.8 %collective-permute-start.19 = (bf16[2,1,16,32,128]{4,3,2,1,0:T(8,128)(2,1)S(1)}, bf16[2,1,16,32,128]{4,3,2,1,0:T(8,128)(2,1)S(1)}, u32[]{:S(2)}, u32[]{:S(2)}) collective-permute-start(bf16[2,1,16,32,128]{4,3,2,1,0:T(8,128)(2,1)S(1)} %slice.45), channel_id=1, source_target_pairs={{0,96},{1,97},{2,98},{3,99},{4,100},{5,101},{6,102},{7,103},{8,104... | collective-permute-start | bytes 786440 | tf_op jit(solution)/shard_map/ppermute | solution.py:34
  100.5 20.2 %collective-permute-start.17 = (bf16[2,2,16,32,128]{4,3,2,1,0:T(8,128)(2,1)}, bf16[2,2,16,32,128]{4,3,2,1,0:T(8,128)(2,1)S(1)}, u32[]{:S(2)}, u32[]{:S(2)}) collective-permute-start(bf16[2,2,16,32,128]{4,3,2,1,0:T(8,128)(2,1)} %collective-permute-done.15.refs_5_), channel_id=1, source_target_pairs={{0,7},{1,0},{2,1},{3,2},{4,3},{5,4},{6,5},{7,6},{8,15},{9,8},{10,9... | collective-permute-start | bytes 1572872 | tf_op jit(solution)/shard_map/ppermute | solution.py:34
  104.8 15.9 %collective-permute-start.16 = (bf16[2,2,16,32,128]{4,3,2,1,0:T(8,128)(2,1)}, bf16[2,2,16,32,128]{4,3,2,1,0:T(8,128)(2,1)S(1)}, u32[]{:S(2)}, u32[]{:S(2)}) collective-permute-start(bf16[2,2,16,32,128]{4,3,2,1,0:T(8,128)(2,1)} %collective-permute-done.14.refs_4_), channel_id=1, source_target_pairs={{0,1},{1,2},{2,3},{3,4},{4,5},{5,6},{6,7},{7,0},{8,9},{9,10},{10,1... | collective-permute-start | bytes 1572872 | tf_op jit(solution)/shard_map/ppermute | solution.py:34
  105.5 6.9 %collective-permute-start.18 = (bf16[2,1,16,32,128]{4,3,2,1,0:T(8,128)(2,1)}, bf16[2,1,16,32,128]{4,3,2,1,0:T(8,128)(2,1)}, u32[]{:S(2)}, u32[]{:S(2)}) collective-permute-start(bf16[2,1,16,32,128]{4,3,2,1,0:T(8,128)(2,1)} %slice.44), channel_id=1, source_target_pairs={{0,32},{1,33},{2,34},{3,35},{4,36},{5,37},{6,38},{7,39},{8,40},{9,... | collective-permute-start | bytes 786440 | tf_op jit(solution)/shard_map/ppermute | solution.py:34
  106.2 8.7 %collective-permute-start.11 = (bf16[2,1,16,32,128]{4,3,2,1,0:T(8,128)(2,1)}, bf16[2,1,16,32,128]{4,3,2,1,0:T(8,128)(2,1)}, u32[]{:S(2)}, u32[]{:S(2)}) collective-permute-start(bf16[2,1,16,32,128]{4,3,2,1,0:T(8,128)(2,1)} %slice.43), channel_id=1, source_target_pairs={{0,96},{1,97},{2,98},{3,99},{4,100},{5,101},{6,102},{7,103},{8,104... | collective-permute-start | bytes 786440 | tf_op jit(solution)/shard_map/ppermute | solution.py:34
  110.5 8.8 %collective-permute-start.10 = (bf16[2,1,16,32,128]{4,3,2,1,0:T(8,128)(2,1)}, bf16[2,1,16,32,128]{4,3,2,1,0:T(8,128)(2,1)}, u32[]{:S(2)}, u32[]{:S(2)}) collective-permute-start(bf16[2,1,16,32,128]{4,3,2,1,0:T(8,128)(2,1)} %slice.42), channel_id=1, source_target_pairs={{0,32},{1,33},{2,34},{3,35},{4,36},{5,37},{6,38},{7,39},{8,40},{9,... | collective-permute-start | bytes 786440 | tf_op jit(solution)/shard_map/ppermute | solution.py:34
  124.7 11.1 %collective-permute-start.21 = (f32[1,448,512]{2,1,0:T(8,128)S(1)}, f32[1,448,512]{2,1,0:T(8,128)S(1)}, u32[]{:S(2)}, u32[]{:S(2)}) collective-permute-start(f32[1,448,512]{2,1,0:T(8,128)S(1)} %get-tuple-element.24), channel_id=1, source_target_pairs={{0,16},{1,17},{2,18},{3,19},{4,20},{5,21},{6,22},{7,23},{8,24},{9,... | collective-permute-start | bytes 2752520 | tf_op jit(solution)/shard_map/ppermute | solution.py:34
  128.1 11.4 %collective-permute-start.24 = (bf16[1,2,16,32,128]{4,3,2,1,0:T(8,128)(2,1)S(1)}, bf16[1,2,16,32,128]{4,3,2,1,0:T(8,128)(2,1)S(1)}, u32[]{:S(2)}, u32[]{:S(2)}) collective-permute-start(bf16[1,2,16,32,128]{4,3,2,1,0:T(8,128)(2,1)S(1)} %slice.47), channel_id=1, source_target_pairs={{0,7},{1,0},{2,1},{3,2},{4,3},{5,4},{6,5},{7,6},{8,15},{9,8},{10,9... | collective-permute-start | bytes 786440 | tf_op jit(solution)/shard_map/ppermute | solution.py:34
  131.1 8.9 %collective-permute-start.23 = (bf16[1,2,16,32,128]{4,3,2,1,0:T(8,128)(2,1)S(1)}, bf16[1,2,16,32,128]{4,3,2,1,0:T(8,128)(2,1)S(1)}, u32[]{:S(2)}, u32[]{:S(2)}) collective-permute-start(bf16[1,2,16,32,128]{4,3,2,1,0:T(8,128)(2,1)S(1)} %slice.46), channel_id=1, source_target_pairs={{0,1},{1,2},{2,3},{3,4},{4,5},{5,6},{6,7},{7,0},{8,9},{9,10},{10,1... | collective-permute-start | bytes 786440 | tf_op jit(solution)/shard_map/ppermute | solution.py:34
  135.2 27.7 %collective-permute-start.20 = (f32[1,448,512]{2,1,0:T(8,128)S(1)}, f32[1,448,512]{2,1,0:T(8,128)S(1)}, u32[]{:S(2)}, u32[]{:S(2)}) collective-permute-start(f32[1,448,512]{2,1,0:T(8,128)S(1)} %get-tuple-element.23), channel_id=1, source_target_pairs={{0,16},{1,17},{2,18},{3,19},{4,20},{5,21},{6,22},{7,23},{8,24},{9,... | collective-permute-start | bytes 2752520 | tf_op jit(solution)/shard_map/ppermute | solution.py:34
  136.0 26.9 %collective-permute-start.22 = (f32[448,512]{1,0:T(8,128)S(1)}, f32[448,512]{1,0:T(8,128)S(1)}, u32[]{:S(2)}, u32[]{:S(2)}) collective-permute-start(f32[448,512]{1,0:T(8,128)S(1)} %add_bitcast_fusion), channel_id=1, source_target_pairs={{0,8},{1,9},{2,10},{3,11},{4,12},{5,13},{6,14},{7,15},{8,0},{9,1},... | collective-permute-start | bytes 2752520 | tf_op jit(solution)/shard_map/ppermute | solution.py:34
  142.1 2.4 %collective-permute-start.25 = (f32[2,64,512]{2,1,0:T(8,128)S(1)}, f32[2,64,512]{2,1,0:T(8,128)S(1)}, u32[]{:S(2)}, u32[]{:S(2)}) collective-permute-start(f32[2,64,512]{2,1,0:T(8,128)S(1)} %get-tuple-element.26), channel_id=1, source_target_pairs={{0,16},{1,17},{2,18},{3,19},{4,20},{5,21},{6,22},{7,23},{8,24},{9,... | collective-permute-start | bytes 786440 | tf_op jit(solution)/shard_map/ppermute | solution.py:34
  144.5 18.4 %collective-permute-start.26 = (f32[64,512]{1,0:T(8,128)S(1)}, f32[64,512]{1,0:T(8,128)S(1)}, u32[]{:S(2)}, u32[]{:S(2)}) collective-permute-start(f32[64,512]{1,0:T(8,128)S(1)} %fusion), channel_id=1, source_target_pairs={{0,8},{1,9},{2,10},{3,11},{4,12},{5,13},{6,14},{7,15},{8,0},{9,1},... | collective-permute-start | bytes 393224 | tf_op jit(solution)/shard_map/ppermute | solution.py:34
  (13 other events, 168.6 us)

commit v4 on v3

--- a/solution.py
+++ b/solution.py
@@ -14,7 +14,6 @@
 MESH = ("seq", "grp")
 VMEM = pl.BlockSpec(memory_space=pltpu.VMEM)
 SMEM = pl.BlockSpec(memory_space=pltpu.SMEM)
-ANY = pl.BlockSpec(memory_space=pl.ANY)
 MIB = 1024 * 1024
 
 
@@ -78,7 +77,7 @@
         lambda *refs: after_kernel(
             len(stacks), *refs[: len(pieces)], *refs[len(pieces) + len(earlier) :]
         ),
-        in_specs=[VMEM] * len(pieces) + [ANY] * len(earlier),
+        in_specs=[VMEM] * (len(pieces) + len(earlier)),
         out_specs=[VMEM] * len(stacks),
         out_shape=shapes,
         compiler_params=pltpu.CompilerParams(vmem_limit_bytes=8 * MIB),
@@ -223,34 +222,29 @@
     )(where, skips, data, *tables())
 
 
-def columns_kernel(where, *refs):
-    y, core, first_x, second_x = where[1], where[2], where[4], where[5]
-    own, below, above, far_low, far_high = refs[:5]
-    right = refs[-1]
-    for j, from_x in enumerate((first_x, second_x)):
-        for step in (0, -1, 1, 2):
+def columns_kernel(where, own, below, above, far, right):
+    y, core = where[1], where[2]
+    for j in range(2):
+        from_x = where[4 + j]
+        for step, shard in ((0, own), (-1, below), (1, above), (2, far)):
             from_y = (y + step + 4) % 4
             base = 32 * (8 * (from_x // 2) + 2 * from_y)
             for rel in range(2):
                 row = pl.ds(pl.multiple_of(base + 32 * ((core + rel) % 2), 32), 32)
-                if step == 2:
-                    piece = (far_low, far_high)[rel].at[j, 0]
-                else:
-                    piece = {0: own, -1: below, 1: above}[step].at[j, rel]
                 for a in range(16):
-                    right[row, 128 * a : 128 * a + 128] = piece[a]
-
-
-def columns(where, shards, *earlier):
+                    right[row, 128 * a : 128 * a + 128] = shard[j, rel, a]
+
+
+def columns(where, *shards):
     return pl.pallas_call(
         columns_kernel,
-        in_specs=[SMEM] + [VMEM] * len(shards) + [ANY] * len(earlier),
+        in_specs=[SMEM] + [VMEM] * len(shards),
         out_specs=VMEM,
         out_shape=jax.ShapeDtypeStruct((512, 2048), BF),
         compiler_params=pltpu.CompilerParams(vmem_limit_bytes=12 * MIB),
         cost_estimate=pl.CostEstimate(flops=0, bytes_accessed=4 * 10**6, transcendentals=0),
         name="columns",
-    )(where, *shards, *earlier)
+    )(where, *shards)
 
 
 def gram_kernel(steps, n_right, n_earlier, where, *refs):
@@ -271,16 +265,40 @@
             for a in range(16):
                 left[pl.ds(row, 32), 128 * a : 128 * a + 128] = ref[j, rel, a]
     for half, right in enumerate(rights):
-        for sub in range(2):
-            lanes = slice(256 * sub, 256 * sub + 256)
-            part = lax.dot_general(
-                left[...],
-                right[lanes, :],
-                (((1,), (1,)), ((), ())),
-                preferred_element_type=F32,
-            )
-            keep[half, :, lanes] = part[:rows]
-            send[half, :, lanes] = part[rows:]
+        times(left, right, keep.at[half], send.at[half])
+
+
+def times(left, right, keep, send):
+    rows = keep.shape[0]
+    for sub in range(2):
+        lanes = slice(256 * sub, 256 * sub + 256)
+        part = lax.dot_general(
+            left[...],
+            right[lanes, :],
+            (((1,), (1,)), ((), ())),
+            preferred_element_type=F32,
+        )
+        keep[:, lanes] = part[:rows]
+        send[:, lanes] = part[rows:]
+
+
+def again_kernel(left, right, keep, send):
+    times(left, right, keep.at[0], send.at[0])
+
+
+def gram_again(left, right):
+    tile = jax.ShapeDtypeStruct((1, left.shape[0] // 2, 512), F32)
+    return pl.pallas_call(
+        again_kernel,
+        in_specs=[VMEM] * 2,
+        out_specs=[VMEM] * 2,
+        out_shape=[tile, tile],
+        compiler_params=pltpu.CompilerParams(vmem_limit_bytes=18 * MIB),
+        cost_estimate=pl.CostEstimate(
+            flops=2 * left.shape[0] * 512 * 2048, bytes_accessed=4 * 10**6, transcendentals=0
+        ),
+        name="gram_again",
+    )(left, right)
 
 
 def gram_part(steps, where, rights, shards, *earlier):
@@ -288,11 +306,10 @@
     tile = jax.ShapeDtypeStruct((len(rights), rows, 512), F32)
     return pl.pallas_call(
         functools.partial(gram_kernel, steps, len(rights), len(earlier)),
-        in_specs=[SMEM] + [VMEM] * (len(rights) + len(shards)) + [ANY] * len(earlier),
-        out_specs=[VMEM] * 2,
-        out_shape=[tile, tile],
-        scratch_shapes=[pltpu.VMEM((2 * rows, 2048), BF)],
-        compiler_params=pltpu.CompilerParams(vmem_limit_bytes=14 * MIB),
+        in_specs=[SMEM] + [VMEM] * (len(rights) + len(shards) + len(earlier)),
+        out_specs=[VMEM] * 3,
+        out_shape=[tile, tile, jax.ShapeDtypeStruct((2 * rows, 2048), BF)],
+        compiler_params=pltpu.CompilerParams(vmem_limit_bytes=18 * MIB),
         cost_estimate=pl.CostEstimate(
             flops=4 * rows * len(rights) * 512 * 2048,
             bytes_accessed=4 * 10**6,
@@ -369,21 +386,18 @@
 
     near_up, near_down = along_y(near, 1), along_y(near, 3)
     (own,) = after([[same, opposite]], near_up, near_down)
-    near_far = along_y(near_up[:, :1], 1), along_y(near_down[:, 1:], 3)
-    own_up, own_down = along_y(own, 1), along_y(own, 3)
-    right = columns(beside, [near, near_up, near_down, *near_far])
-    own_far = along_y(own_up[:, :1], 1), along_y(own_down[:, 1:], 3)
-    own_right = columns(across, [own, own_up, own_down, *own_far])
+    near_far, own_down = along_y(near_up, 1), along_y(own, 3)
+    own_up, own_far = along_y(own, 1), along_y(own_down, 3)
+    right = columns(beside, near, near_up, near_down, near_far)
+    own_right = columns(across, own, own_up, own_down, own_far)
 
     early = [rows, ups[1], downs[1], ups[2], downs[2], ups[3], downs[3]]
-    keep, send = gram_part(CHUNKS[0], where, [right], early, own_right)
-    half_a = keep[0] + other_core(send)[0]
-    theirs_a = other_x_lo(half_a)
-    keep_a, send_a = gram_part(CHUNKS[0], where, [own_right], early, keep)
+    keep, send, left = gram_part(CHUNKS[0], where, [right], early, own_right)
+    theirs_a = other_x_lo(keep[0] + other_core(send)[0])
+    keep_a, send_a = gram_again(left, own_right)
     got_a = other_core(send_a)
 
-    late = [*far]
-    keep_b, send_b = gram_part(CHUNKS[1], where, [own_right, right], late)
+    keep_b, send_b, _ = gram_part(CHUNKS[1], where, [own_right, right], far)
     got_b = other_core(send_b)
     theirs_b = other_x_lo(keep_b[1] + got_b[1])
     return finish(

time: 165 us -> 167 us (1.012)
  waiting for transfers between devices: 70.9 us -> 87.4 us
  starting transfers between devices: 62.1 us -> 49.7 us
    ppermute x27 -> x25, waiting for transfers between devices: 48.9 us -> 65.4 us  [move(): return lax.ppermute(array, MESH, pairs)]
    ppermute x27 -> x25, starting transfers between devices: 53.5 us -> 41.1 us  [move(): return lax.ppermute(array, MESH, pairs)]
    pallas_call x3 -> x2, Pallas kernels: 9.97 us -> 6.61 us  [gram_part(): pl.pallas_call(functools.partial(gram_kernel, steps, len(rights), len(ear...]
    pallas_call x2 -> x3, Pallas kernels: 2.74 us -> 5.33 us  [the longest x2 3.24 us: columns(): pl.pallas_call(columns_kernel, in_specs=[SMEM] + [VMEM] * len(shards), ou...]
    slice x4 -> x0, local copies, waits for them, and re-layouts: 2.22 us -> none  [the longest x2 1.49 us: local(): own_far = (along_y(own_up[:, :1], 1), along_y(own_down[:, 1:], 3))]
    unnamed x34 -> x26, local copies, waits for them, and re-layouts: 2.69 us -> 3.48 us
  transfers between devices with their start and end apart: 28 -> 26, of which waited for: 13 -> 11; matrix products, arithmetic and copies ran while one was open for 2% -> 1% of each run, Pallas kernels for 5% -> 5%
where the time goes in v4:
time: 167 us; the launch traced here: 166 us
  waiting for transfers between devices  87.4 us (52%)
  starting transfers between devices  49.7 us (30%)
  Pallas kernels  24.3 us (15%)
  local copies, waits for them, and re-layouts  4.53 us (3%)
    ppermute x25, waiting for transfers between devices, move(): return lax.ppermute(array, MESH, pairs)  65.4 us
    ppermute x25, starting transfers between devices, move(): return lax.ppermute(array, MESH, pairs)  41.1 us
    all_to_all x1, waiting for transfers between devices, local(): lax.all_to_all(outgoing, 'seq', split_axis=0, concat_axis=0, tiled=True)  22 us
    all_to_all x1, starting transfers between devices, local(): lax.all_to_all(outgoing, 'seq', split_axis=0, concat_axis=0, tiled=True)  8.59 us
    pallas_call x2, Pallas kernels, gram_part(): pl.pallas_call(functools.partial(gram_kernel, steps, len(rights), len(ear...  6.61 us
    pallas_call x1, Pallas kernels, convolve(): pl.pallas_call(conv_kernel, in_specs=[SMEM, SMEM] + [VMEM] * 7, out_specs...  6.26 us
    pallas_call x1, Pallas kernels, prepare(): pl.pallas_call(prepare_kernel, grid=(4,), in_specs=[block] * 4, out_specs...  4.26 us
    unnamed x26, local copies, waits for them, and re-layouts  3.48 us
  transfers between devices with their start and end apart: 26, of which 11 were waited for; matrix products, arithmetic and copies ran while one was open for 1% of the time, Pallas kernels for 5%

profile of v4, /device:TPU:1, one launch (start us, length us, event | category | flops | bytes accessed | tf_op | source)
XLA Modules:
  0.0 166.5 jit_solution(13342352713858548385)
XLA Ops:
  0.0 4.3 %prepare.1 = bf16[16,96,512]{2,1,0:T(8,128)(2,1)} custom-call(bf16[512,512]{1,0:T(8,128)(2,1)} %gate.1, bf16[512,512]{1,0:T(8,128)(2,1)} %key.1, bf16[512,512]{1,0:T(8,128)(2,1)} %value.1, bf16[512,512]{1,0:T(8,128)(2,1)} %filt.1), custom_call_target="tpu_custom_call" | custom-call | tf_op jit(solution)/shard_map/prepare/pallas_call | solution.py:124
  4.3 8.6 %all-to-all-start = ((bf16[16,96,512]{2,1,0:T(8,128)(2,1)}), bf16[16,96,512]{2,1,0:T(8,128)(2,1)S(1)}, u32[]{:S(2)}, u32[]{:S(2)}) async-start(bf16[16,96,512]{2,1,0:T(8,128)(2,1)} %prepare.1), calls=%async_computation | async-start | bytes 3145728 | tf_op jit(solution)/shard_map/all_to_all | solution.py:367
  13.7 22.0 %all-to-all-done.data = bf16[16,96,512]{2,1,0:T(8,128)(2,1)S(1)} async-done(((bf16[16,96,512]{2,1,0:T(8,128)(2,1)}), bf16[16,96,512]{2,1,0:T(8,128)(2,1)S(1)}, u32[]{:S(2)}, u32[]{:S(2)}) %all-to-all-start) | async-done | bytes 1572896 | tf_op jit(solution)/shard_map/all_to_all | solution.py:367
  35.8 6.3 %convolve.1 = (bf16[16,32,128]{2,1,0:T(8,128)(2,1)S(1)}, bf16[16,32,128]{2,1,0:T(8,128)(2,1)S(1)}, bf16[2,16,32,128]{3,2,1,0:T(8,128)(2,1)S(1)}) custom-call(s32[6]{0:T(128)S(1)} %stack.57.where, f32[32]{0:T(128)S(1)} %dynamic_slice.3.skip, bf16[16,96,512]{2,1,0:T(8,128)(2,1)S(1)} %all-to-all-done.data, bf16[256,64]{1,0:T(8,128)(2,1)S(1)} %copy-done.9, ...), custom_call_target="tpu_custom_call" | custom-call | flops 4000000000 | bytes 3000000 | tf_op jit(solution)/shard_map/convolve/pallas_call | solution.py:211
  43.1 1.2 collective-permute-done
  45.0 1.6 collective-permute-start.2
  46.7 3.0 %collective-permute-start.3 = (bf16[2,16,32,128]{3,2,1,0:T(8,128)(2,1)S(1)}, bf16[2,16,32,128]{3,2,1,0:T(8,128)(2,1)S(1)}, u32[]{:S(2)}, u32[]{:S(2)}) collective-permute-start(bf16[2,16,32,128]{3,2,1,0:T(8,128)(2,1)S(1)} %get-tuple-element.32), channel_id=1, source_target_pairs={{0,136},{1,137},{2,138},{3,139},{4,140},{5,141},{6,142},{7,143},{8... | collective-permute-start | bytes 786440 | tf_op jit(solution)/shard_map/ppermute | solution.py:33
  49.6 1.7 %collective-permute-start.5 = (bf16[2,16,32,128]{3,2,1,0:T(8,128)(2,1)S(1)}, bf16[2,16,32,128]{3,2,1,0:T(8,128)(2,1)S(1)}, u32[]{:S(2)}, u32[]{:S(2)}) collective-permute-start(bf16[2,16,32,128]{3,2,1,0:T(8,128)(2,1)S(1)} %get-tuple-element.31.refs_4_.refs_0_), channel_id=1, source_target_pairs={{0,128},{1,129},{2,130},{3,131},{4,132},{5,133},{6,134},{7,135},{8... | collective-permute-start | bytes 786440 | tf_op jit(solution)/shard_map/ppermute | solution.py:33
  51.4 20.8 %collective-permute-done.2.refs_1_ = bf16[2,16,32,128]{3,2,1,0:T(8,128)(2,1)S(1)} collective-permute-done((bf16[2,16,32,128]{3,2,1,0:T(8,128)(2,1)S(1)}, bf16[2,16,32,128]{3,2,1,0:T(8,128)(2,1)S(1)}, u32[]{:S(2)}, u32[]{:S(2)}) %collective-permute-start.2) | collective-permute-done | bytes 262176 | tf_op jit(solution)/shard_map/ppermute | solution.py:33
  72.3 2.1 %collective-permute-start.6 = (bf16[2,2,16,32,128]{4,3,2,1,0:T(8,128)(2,1)S(1)}, bf16[2,2,16,32,128]{4,3,2,1,0:T(8,128)(2,1)S(1)}, u32[]{:S(2)}, u32[]{:S(2)}) collective-permute-start(bf16[2,2,16,32,128]{4,3,2,1,0:T(8,128)(2,1)S(1)} %get-tuple-element.20.own), channel_id=1, source_target_pairs={{0,32},{1,33},{2,34},{3,35},{4,36},{5,37},{6,38},{7,39},{8,40},{9,... | collective-permute-start | bytes 1572872 | tf_op jit(solution)/shard_map/ppermute | solution.py:33
  74.4 5.4 %collective-permute-start.7 = (bf16[2,2,16,32,128]{4,3,2,1,0:T(8,128)(2,1)S(1)}, bf16[2,2,16,32,128]{4,3,2,1,0:T(8,128)(2,1)S(1)}, u32[]{:S(2)}, u32[]{:S(2)}) collective-permute-start(bf16[2,2,16,32,128]{4,3,2,1,0:T(8,128)(2,1)S(1)} %get-tuple-element.20.own), channel_id=1, source_target_pairs={{0,96},{1,97},{2,98},{3,99},{4,100},{5,101},{6,102},{7,103},{8,104... | collective-permute-start | bytes 1572872 | tf_op jit(solution)/shard_map/ppermute | solution.py:33
  81.5 4.2 %collective-permute-start.10 = (bf16[2,2,16,32,128]{4,3,2,1,0:T(8,128)(2,1)S(1)}, bf16[2,2,16,32,128]{4,3,2,1,0:T(8,128)(2,1)S(1)}, u32[]{:S(2)}, u32[]{:S(2)}) collective-permute-start(bf16[2,2,16,32,128]{4,3,2,1,0:T(8,128)(2,1)S(1)} %get-tuple-element.21.refs_1_), channel_id=1, source_target_pairs={{0,7},{1,0},{2,1},{3,2},{4,3},{5,4},{6,5},{7,6},{8,15},{9,8},{10,9... | collective-permute-start | bytes 1572872 | tf_op jit(solution)/shard_map/ppermute | solution.py:33
  85.7 5.6 %collective-permute-done.6.below.refs_2_ = bf16[2,2,16,32,128]{4,3,2,1,0:T(8,128)(2,1)S(1)} collective-permute-done((bf16[2,2,16,32,128]{4,3,2,1,0:T(8,128)(2,1)S(1)}, bf16[2,2,16,32,128]{4,3,2,1,0:T(8,128)(2,1)S(1)}, u32[]{:S(2)}, u32[]{:S(2)}) %collective-permute-start.6) | collective-permute-done | bytes 524320 | tf_op jit(solution)/shard_map/ppermute | solution.py:33
  91.4 2.5 %collective-permute-start.16 = (bf16[2,2,16,32,128]{4,3,2,1,0:T(8,128)(2,1)S(1)}, bf16[2,2,16,32,128]{4,3,2,1,0:T(8,128)(2,1)}, u32[]{:S(2)}, u32[]{:S(2)}) collective-permute-start(bf16[2,2,16,32,128]{4,3,2,1,0:T(8,128)(2,1)S(1)} %after.3.own), channel_id=1, source_target_pairs={{0,96},{1,97},{2,98},{3,99},{4,100},{5,101},{6,102},{7,103},{8,104... | collective-permute-start | bytes 1572872 | tf_op jit(solution)/shard_map/ppermute | solution.py:33
  93.9 2.3 %collective-permute-done.9.refs_2_ = bf16[2,2,16,32,128]{4,3,2,1,0:T(8,128)(2,1)S(1)} collective-permute-done((bf16[2,2,16,32,128]{4,3,2,1,0:T(8,128)(2,1)S(1)}, bf16[2,2,16,32,128]{4,3,2,1,0:T(8,128)(2,1)S(1)}, u32[]{:S(2)}, u32[]{:S(2)}) %collective-permute-start.9) | collective-permute-done | bytes 524320 | tf_op jit(solution)/shard_map/ppermute | solution.py:33
  97.0 2.7 %collective-permute-start.12 = (bf16[2,2,16,32,128]{4,3,2,1,0:T(8,128)(2,1)S(1)}, bf16[2,2,16,32,128]{4,3,2,1,0:T(8,128)(2,1)}, u32[]{:S(2)}, u32[]{:S(2)}) collective-permute-start(bf16[2,2,16,32,128]{4,3,2,1,0:T(8,128)(2,1)S(1)} %collective-permute-done.10.refs_3_), channel_id=1, source_target_pairs={{0,7},{1,0},{2,1},{3,2},{4,3},{5,4},{6,5},{7,6},{8,15},{9,8},{10,9... | collective-permute-start | bytes 1572872 | tf_op jit(solution)/shard_map/ppermute | solution.py:33
  100.5 3.3 %collective-permute-done.16.above = bf16[2,2,16,32,128]{4,3,2,1,0:T(8,128)(2,1)} collective-permute-done((bf16[2,2,16,32,128]{4,3,2,1,0:T(8,128)(2,1)S(1)}, bf16[2,2,16,32,128]{4,3,2,1,0:T(8,128)(2,1)}, u32[]{:S(2)}, u32[]{:S(2)}) %collective-permute-start.16) | collective-permute-done | bytes 524320 | tf_op jit(solution)/shard_map/ppermute | solution.py:33
  103.8 3.3 %collective-permute-start.17 = (bf16[2,2,16,32,128]{4,3,2,1,0:T(8,128)(2,1)}, bf16[2,2,16,32,128]{4,3,2,1,0:T(8,128)(2,1)}, u32[]{:S(2)}, u32[]{:S(2)}) collective-permute-start(bf16[2,2,16,32,128]{4,3,2,1,0:T(8,128)(2,1)} %collective-permute-done.16.above), channel_id=1, source_target_pairs={{0,96},{1,97},{2,98},{3,99},{4,100},{5,101},{6,102},{7,103},{8,104... | collective-permute-start | bytes 1572872 | tf_op jit(solution)/shard_map/ppermute | solution.py:33
  107.1 1.5 collective-permute-done.11.refs_4_
  108.6 3.2 %collective-permute-start.14 = (bf16[2,2,16,32,128]{4,3,2,1,0:T(8,128)(2,1)}, bf16[2,2,16,32,128]{4,3,2,1,0:T(8,128)(2,1)S(1)}, u32[]{:S(2)}, u32[]{:S(2)}) collective-permute-start(bf16[2,2,16,32,128]{4,3,2,1,0:T(8,128)(2,1)} %collective-permute-done.12.refs_5_), channel_id=1, source_target_pairs={{0,7},{1,0},{2,1},{3,2},{4,3},{5,4},{6,5},{7,6},{8,15},{9,8},{10,9... | collective-permute-start | bytes 1572872 | tf_op jit(solution)/shard_map/ppermute | solution.py:33
  111.9 11.6 %collective-permute-done.8.far = bf16[2,2,16,32,128]{4,3,2,1,0:T(8,128)(2,1)} collective-permute-done((bf16[2,2,16,32,128]{4,3,2,1,0:T(8,128)(2,1)S(1)}, bf16[2,2,16,32,128]{4,3,2,1,0:T(8,128)(2,1)}, u32[]{:S(2)}, u32[]{:S(2)}) %collective-permute-start.8) | collective-permute-done | bytes 524320 | tf_op jit(solution)/shard_map/ppermute | solution.py:33
  124.5 1.4 columns.2.refs_0_.refs_1_
  126.0 1.8 %columns.3.refs_8_.right.refs_0_ = bf16[512,2048]{1,0:T(8,128)(2,1)S(1)} custom-call(s32[6]{0:T(128)S(1)} %stack.66.where, bf16[2,2,16,32,128]{4,3,2,1,0:T(8,128)(2,1)S(1)} %after.3.own, bf16[2,2,16,32,128]{4,3,2,1,0:T(8,128)(2,1)} %collective-permute-done.15.below, bf16[2,2,16,32,128]{4,3,2,1,0:T(8,128)(2,1)} %collective-permute-done.16.above, ...), custom_call_target="tpu_custom_call" | custom-call | bytes 4000000 | tf_op jit(solution)/shard_map/columns/pallas_call | solution.py:239
  127.9 3.9 %gram_part.2 = (f32[1,448,512]{2,1,0:T(8,128)S(1)}, f32[1,448,512]{2,1,0:T(8,128)S(1)}, bf16[896,2048]{1,0:T(8,128)(2,1)S(1)}) custom-call(s32[6]{0:T(128)S(1)} %stack.57.where, bf16[512,2048]{1,0:T(8,128)(2,1)S(1)} %columns.2.refs_0_.refs_1_, bf16[2,2,16,32,128]{4,3,2,1,0:T(8,128)(2,1)S(1)} %get-tuple-element.21.refs_1_, ...), custom_call_target="tpu_custom_call" | custom-call | flops 1879048192 | bytes 4000000 | tf_op jit(solution)/shard_map/gram_part/pallas_call | solution.py:307
  131.8 4.0 %collective-permute-start.19 = (f32[1,448,512]{2,1,0:T(8,128)S(1)}, f32[1,448,512]{2,1,0:T(8,128)S(1)}, u32[]{:S(2)}, u32[]{:S(2)}) collective-permute-start(f32[1,448,512]{2,1,0:T(8,128)S(1)} %get-tuple-element.26), channel_id=1, source_target_pairs={{0,16},{1,17},{2,18},{3,19},{4,20},{5,21},{6,22},{7,23},{8,24},{9,... | collective-permute-start | bytes 2752520 | tf_op jit(solution)/shard_map/ppermute | solution.py:33
  135.8 2.1 %gram_again.1 = (f32[1,448,512]{2,1,0:T(8,128)S(1)}, f32[1,448,512]{2,1,0:T(8,128)S(1)}) custom-call(bf16[896,2048]{1,0:T(8,128)(2,1)S(1)} %get-tuple-element.22.left, bf16[512,2048]{1,0:T(8,128)(2,1)S(1)} %columns.3.refs_8_.right.refs_0_), custom_call_target="tpu_custom_call" | custom-call | flops 1879048192 | bytes 4000000 | tf_op jit(solution)/shard_map/gram_again/pallas_call | solution.py:291
  138.1 2.7 %collective-permute-start.22 = (bf16[1,2,16,32,128]{4,3,2,1,0:T(8,128)(2,1)S(1)}, bf16[1,2,16,32,128]{4,3,2,1,0:T(8,128)(2,1)S(1)}, u32[]{:S(2)}, u32[]{:S(2)}) collective-permute-start(bf16[1,2,16,32,128]{4,3,2,1,0:T(8,128)(2,1)S(1)} %slice.27), channel_id=1, source_target_pairs={{0,7},{1,0},{2,1},{3,2},{4,3},{5,4},{6,5},{7,6},{8,15},{9,8},{10,9... | collective-permute-start | bytes 786440 | tf_op jit(solution)/shard_map/ppermute | solution.py:33
  141.3 5.4 %collective-permute-done.21.refs_2_ = bf16[1,2,16,32,128]{4,3,2,1,0:T(8,128)(2,1)S(1)} collective-permute-done((bf16[1,2,16,32,128]{4,3,2,1,0:T(8,128)(2,1)S(1)}, bf16[1,2,16,32,128]{4,3,2,1,0:T(8,128)(2,1)S(1)}, u32[]{:S(2)}, u32[]{:S(2)}) %collective-permute-start.21) | collective-permute-done | bytes 262176 | tf_op jit(solution)/shard_map/ppermute | solution.py:33
  146.7 2.7 %gram_part.3 = (f32[2,64,512]{2,1,0:T(8,128)S(1)}, f32[2,64,512]{2,1,0:T(8,128)S(1)}, bf16[128,2048]{1,0:T(8,128)(2,1)}) custom-call(s32[6]{0:T(128)S(1)} %stack.57.where, bf16[512,2048]{1,0:T(8,128)(2,1)S(1)} %columns.3.refs_8_.right.refs_0_, bf16[512,2048]{1,0:T(8,128)(2,1)S(1)} %columns.2.refs_0_.refs_1_, ...), custom_call_target="tpu_custom_call" | custom-call | flops 536870912 | bytes 4000000 | tf_op jit(solution)/shard_map/gram_part/pallas_call | solution.py:307
  149.4 1.3 collective-permute-start.23
  152.2 12.6 %collective-permute-done.24.refs_5_ = f32[64,512]{1,0:T(8,128)S(1)} collective-permute-done((f32[64,512]{1,0:T(8,128)S(1)}, f32[64,512]{1,0:T(8,128)S(1)}, u32[]{:S(2)}, u32[]{:S(2)}) %collective-permute-start.24) | collective-permute-done | bytes 131104 | tf_op jit(solution)/shard_map/ppermute | solution.py:33
  164.8 1.7 %finish.1 = f32[512,512]{1,0:T(8,128)} custom-call(s32[6]{0:T(128)S(1)} %stack.57.where, f32[512,512]{1,0:T(8,128)S(1)} %copy-done, f32[1,448,512]{2,1,0:T(8,128)S(1)} %get-tuple-element.23.refs_0_, f32[1,448,512]{2,1,0:T(8,128)S(1)} %collective-permute-done.18.refs_1_, f32[448,512]{1,0:T(8,128)S(1)} %collective-permute-done.20.refs_2_, ...), custom_call_target="tpu_custom_call" | custom-call | flops 1000000 | bytes 5000000 | tf_op jit(solution)/shard_map/finish/pallas_call | solution.py:342
  (66 shorter events, 9.4 us)
Async XLA Ops:
  4.3 31.5 %copy-start.7 = (bf16[256,256]{1,0:T(8,128)(2,1)S(1)}, bf16[256,256]{1,0:T(8,128)(2,1)}, u32[]{:S(2)}) copy-start(bf16[256,256]{1,0:T(8,128)(2,1)} %constant.116.fwd) | copy-start | bytes 393220
  4.3 31.5 %copy-start.8 = (bf16[256,256]{1,0:T(8,128)(2,1)S(1)}, bf16[256,256]{1,0:T(8,128)(2,1)}, u32[]{:S(2)}) copy-start(bf16[256,256]{1,0:T(8,128)(2,1)} %constant.117.bwd) | copy-start | bytes 393220
  4.3 31.5 %copy-start.9 = (bf16[256,64]{1,0:T(8,128)(2,1)S(1)}, bf16[256,64]{1,0:T(8,128)(2,1)}, u32[]{:S(2)}) copy-start(bf16[256,64]{1,0:T(8,128)(2,1)} %constant.114.first) | copy-start | bytes 98308
  4.3 31.5 %copy-start.10 = (f32[128,128]{1,0:T(8,128)S(1)}, f32[128,128]{1,0:T(8,128)}, u32[]{:S(2)}) copy-start(f32[128,128]{1,0:T(8,128)} %constant.112.clone.t_cos) | copy-start | bytes 196612
  4.3 31.5 %copy-start.11 = (f32[128,128]{1,0:T(8,128)S(1)}, f32[128,128]{1,0:T(8,128)}, u32[]{:S(2)}) copy-start(f32[128,128]{1,0:T(8,128)} %constant.113.clone.t_sin) | copy-start | bytes 196612
  4.3 31.5 %copy-start.12 = (bf16[64,256]{1,0:T(8,128)(2,1)S(1)}, bf16[64,256]{1,0:T(8,128)(2,1)}, u32[]{:S(2)}) copy-start(bf16[64,256]{1,0:T(8,128)(2,1)} %constant.115.last) | copy-start | bytes 98308
  4.3 31.4 %all-to-all-start = ((bf16[16,96,512]{2,1,0:T(8,128)(2,1)}), bf16[16,96,512]{2,1,0:T(8,128)(2,1)S(1)}, u32[]{:S(2)}, u32[]{:S(2)}) async-start(bf16[16,96,512]{2,1,0:T(8,128)(2,1)} %prepare.1), calls=%async_computation | async-start | bytes 3145728 | tf_op jit(solution)/shard_map/all_to_all | solution.py:367
  42.1 2.2 %collective-permute-start = (bf16[2,16,32,128]{3,2,1,0:T(8,128)(2,1)S(1)}, bf16[2,16,32,128]{3,2,1,0:T(8,128)(2,1)S(1)}, u32[]{:S(2)}, u32[]{:S(2)}) collective-permute-start(bf16[2,16,32,128]{3,2,1,0:T(8,128)(2,1)S(1)} %get-tuple-element.18), channel_id=1, source_target_pairs={{0,16},{1,17},{2,18},{3,19},{4,20},{5,21},{6,22},{7,23},{8,24},{9,... | collective-permute-start | bytes 786440 | tf_op jit(solution)/shard_map/ppermute | solution.py:33
  44.4 7.0 %collective-permute-start.1 = (bf16[2,16,32,128]{3,2,1,0:T(8,128)(2,1)S(1)}, bf16[2,16,32,128]{3,2,1,0:T(8,128)(2,1)S(1)}, u32[]{:S(2)}, u32[]{:S(2)}) collective-permute-start(bf16[2,16,32,128]{3,2,1,0:T(8,128)(2,1)S(1)} %get-tuple-element.30), channel_id=1, source_target_pairs={{0,0},{1,1},{2,38},{3,39},{4,68},{5,69},{6,98},{7,99},{8,128},{9,1... | collective-permute-start | bytes 786440 | tf_op jit(solution)/shard_map/ppermute | solution.py:33
  45.0 27.2 %collective-permute-start.2 = (bf16[2,16,32,128]{3,2,1,0:T(8,128)(2,1)S(1)}, bf16[2,16,32,128]{3,2,1,0:T(8,128)(2,1)S(1)}, u32[]{:S(2)}, u32[]{:S(2)}) collective-permute-start(bf16[2,16,32,128]{3,2,1,0:T(8,128)(2,1)S(1)} %get-tuple-element.29), channel_id=1, source_target_pairs={{0,8},{1,9},{2,46},{3,47},{4,76},{5,77},{6,106},{7,107},{8,136},{9... | collective-permute-start | bytes 786440 | tf_op jit(solution)/shard_map/ppermute | solution.py:33
  46.7 25.5 %collective-permute-start.3 = (bf16[2,16,32,128]{3,2,1,0:T(8,128)(2,1)S(1)}, bf16[2,16,32,128]{3,2,1,0:T(8,128)(2,1)S(1)}, u32[]{:S(2)}, u32[]{:S(2)}) collective-permute-start(bf16[2,16,32,128]{3,2,1,0:T(8,128)(2,1)S(1)} %get-tuple-element.32), channel_id=1, source_target_pairs={{0,136},{1,137},{2,138},{3,139},{4,140},{5,141},{6,142},{7,143},{8... | collective-permute-start | bytes 786440 | tf_op jit(solution)/shard_map/ppermute | solution.py:33
  49.6 22.6 %collective-permute-start.4 = (bf16[2,16,32,128]{3,2,1,0:T(8,128)(2,1)S(1)}, bf16[2,16,32,128]{3,2,1,0:T(8,128)(2,1)S(1)}, u32[]{:S(2)}, u32[]{:S(2)}) collective-permute-start(bf16[2,16,32,128]{3,2,1,0:T(8,128)(2,1)S(1)} %get-tuple-element.32), channel_id=1, source_target_pairs={{0,8},{1,9},{2,10},{3,11},{4,12},{5,13},{6,14},{7,15},{8,128},{9,1... | collective-permute-start | bytes 786440 | tf_op jit(solution)/shard_map/ppermute | solution.py:33
  49.6 22.6 %collective-permute-start.5 = (bf16[2,16,32,128]{3,2,1,0:T(8,128)(2,1)S(1)}, bf16[2,16,32,128]{3,2,1,0:T(8,128)(2,1)S(1)}, u32[]{:S(2)}, u32[]{:S(2)}) collective-permute-start(bf16[2,16,32,128]{3,2,1,0:T(8,128)(2,1)S(1)} %get-tuple-element.31.refs_4_.refs_0_), channel_id=1, source_target_pairs={{0,128},{1,129},{2,130},{3,131},{4,132},{5,133},{6,134},{7,135},{8... | collective-permute-start | bytes 786440 | tf_op jit(solution)/shard_map/ppermute | solution.py:33
  72.3 19.1 %collective-permute-start.6 = (bf16[2,2,16,32,128]{4,3,2,1,0:T(8,128)(2,1)S(1)}, bf16[2,2,16,32,128]{4,3,2,1,0:T(8,128)(2,1)S(1)}, u32[]{:S(2)}, u32[]{:S(2)}) collective-permute-start(bf16[2,2,16,32,128]{4,3,2,1,0:T(8,128)(2,1)S(1)} %get-tuple-element.20.own), channel_id=1, source_target_pairs={{0,32},{1,33},{2,34},{3,35},{4,36},{5,37},{6,38},{7,39},{8,40},{9,... | collective-permute-start | bytes 1572872 | tf_op jit(solution)/shard_map/ppermute | solution.py:33
  74.4 16.9 %collective-permute-start.7 = (bf16[2,2,16,32,128]{4,3,2,1,0:T(8,128)(2,1)S(1)}, bf16[2,2,16,32,128]{4,3,2,1,0:T(8,128)(2,1)S(1)}, u32[]{:S(2)}, u32[]{:S(2)}) collective-permute-start(bf16[2,2,16,32,128]{4,3,2,1,0:T(8,128)(2,1)S(1)} %get-tuple-element.20.own), channel_id=1, source_target_pairs={{0,96},{1,97},{2,98},{3,99},{4,100},{5,101},{6,102},{7,103},{8,104... | collective-permute-start | bytes 1572872 | tf_op jit(solution)/shard_map/ppermute | solution.py:33
  80.6 15.6 %collective-permute-start.9 = (bf16[2,2,16,32,128]{4,3,2,1,0:T(8,128)(2,1)S(1)}, bf16[2,2,16,32,128]{4,3,2,1,0:T(8,128)(2,1)S(1)}, u32[]{:S(2)}, u32[]{:S(2)}) collective-permute-start(bf16[2,2,16,32,128]{4,3,2,1,0:T(8,128)(2,1)S(1)} %get-tuple-element.21.refs_1_), channel_id=1, source_target_pairs={{0,1},{1,2},{2,3},{3,4},{4,5},{5,6},{6,7},{7,0},{8,9},{9,10},{10,1... | collective-permute-start | bytes 1572872 | tf_op jit(solution)/shard_map/ppermute | solution.py:33
  81.5 15.5 %collective-permute-start.10 = (bf16[2,2,16,32,128]{4,3,2,1,0:T(8,128)(2,1)S(1)}, bf16[2,2,16,32,128]{4,3,2,1,0:T(8,128)(2,1)S(1)}, u32[]{:S(2)}, u32[]{:S(2)}) collective-permute-start(bf16[2,2,16,32,128]{4,3,2,1,0:T(8,128)(2,1)S(1)} %get-tuple-element.21.refs_1_), channel_id=1, source_target_pairs={{0,7},{1,0},{2,1},{3,2},{4,3},{5,4},{6,5},{7,6},{8,15},{9,8},{10,9... | collective-permute-start | bytes 1572872 | tf_op jit(solution)/shard_map/ppermute | solution.py:33
  91.4 12.4 %collective-permute-start.16 = (bf16[2,2,16,32,128]{4,3,2,1,0:T(8,128)(2,1)S(1)}, bf16[2,2,16,32,128]{4,3,2,1,0:T(8,128)(2,1)}, u32[]{:S(2)}, u32[]{:S(2)}) collective-permute-start(bf16[2,2,16,32,128]{4,3,2,1,0:T(8,128)(2,1)S(1)} %after.3.own), channel_id=1, source_target_pairs={{0,96},{1,97},{2,98},{3,99},{4,100},{5,101},{6,102},{7,103},{8,104... | collective-permute-start | bytes 1572872 | tf_op jit(solution)/shard_map/ppermute | solution.py:33
  96.2 12.3 %collective-permute-start.11 = (bf16[2,2,16,32,128]{4,3,2,1,0:T(8,128)(2,1)S(1)}, bf16[2,2,16,32,128]{4,3,2,1,0:T(8,128)(2,1)}, u32[]{:S(2)}, u32[]{:S(2)}) collective-permute-start(bf16[2,2,16,32,128]{4,3,2,1,0:T(8,128)(2,1)S(1)} %collective-permute-done.9.refs_2_), channel_id=1, source_target_pairs={{0,1},{1,2},{2,3},{3,4},{4,5},{5,6},{6,7},{7,0},{8,9},{9,10},{10,1... | collective-permute-start | bytes 1572872 | tf_op jit(solution)/shard_map/ppermute | solution.py:33
  97.0 11.5 %collective-permute-start.12 = (bf16[2,2,16,32,128]{4,3,2,1,0:T(8,128)(2,1)S(1)}, bf16[2,2,16,32,128]{4,3,2,1,0:T(8,128)(2,1)}, u32[]{:S(2)}, u32[]{:S(2)}) collective-permute-start(bf16[2,2,16,32,128]{4,3,2,1,0:T(8,128)(2,1)S(1)} %collective-permute-done.10.refs_3_), channel_id=1, source_target_pairs={{0,7},{1,0},{2,1},{3,2},{4,3},{5,4},{6,5},{7,6},{8,15},{9,8},{10,9... | collective-permute-start | bytes 1572872 | tf_op jit(solution)/shard_map/ppermute | solution.py:33
  100.5 25.5 %collective-permute-start.15 = (bf16[2,2,16,32,128]{4,3,2,1,0:T(8,128)(2,1)S(1)}, bf16[2,2,16,32,128]{4,3,2,1,0:T(8,128)(2,1)}, u32[]{:S(2)}, u32[]{:S(2)}) collective-permute-start(bf16[2,2,16,32,128]{4,3,2,1,0:T(8,128)(2,1)S(1)} %after.3.own), channel_id=1, source_target_pairs={{0,32},{1,33},{2,34},{3,35},{4,36},{5,37},{6,38},{7,39},{8,40},{9,... | collective-permute-start | bytes 1572872 | tf_op jit(solution)/shard_map/ppermute | solution.py:33
  100.5 23.0 %collective-permute-start.8 = (bf16[2,2,16,32,128]{4,3,2,1,0:T(8,128)(2,1)S(1)}, bf16[2,2,16,32,128]{4,3,2,1,0:T(8,128)(2,1)}, u32[]{:S(2)}, u32[]{:S(2)}) collective-permute-start(bf16[2,2,16,32,128]{4,3,2,1,0:T(8,128)(2,1)S(1)} %collective-permute-done.6.below.refs_2_), channel_id=1, source_target_pairs={{0,32},{1,33},{2,34},{3,35},{4,36},{5,37},{6,38},{7,39},{8,40},{9,... | collective-permute-start | bytes 1572872 | tf_op jit(solution)/shard_map/ppermute | solution.py:33
  103.8 22.2 %collective-permute-start.17 = (bf16[2,2,16,32,128]{4,3,2,1,0:T(8,128)(2,1)}, bf16[2,2,16,32,128]{4,3,2,1,0:T(8,128)(2,1)}, u32[]{:S(2)}, u32[]{:S(2)}) collective-permute-start(bf16[2,2,16,32,128]{4,3,2,1,0:T(8,128)(2,1)} %collective-permute-done.16.above), channel_id=1, source_target_pairs={{0,96},{1,97},{2,98},{3,99},{4,100},{5,101},{6,102},{7,103},{8,104... | collective-permute-start | bytes 1572872 | tf_op jit(solution)/shard_map/ppermute | solution.py:33
  108.5 19.3 %collective-permute-start.13 = (bf16[2,2,16,32,128]{4,3,2,1,0:T(8,128)(2,1)}, bf16[2,2,16,32,128]{4,3,2,1,0:T(8,128)(2,1)S(1)}, u32[]{:S(2)}, u32[]{:S(2)}) collective-permute-start(bf16[2,2,16,32,128]{4,3,2,1,0:T(8,128)(2,1)} %collective-permute-done.11.refs_4_), channel_id=1, source_target_pairs={{0,1},{1,2},{2,3},{3,4},{4,5},{5,6},{6,7},{7,0},{8,9},{9,10},{10,1... | collective-permute-start | bytes 1572872 | tf_op jit(solution)/shard_map/ppermute | solution.py:33
  108.6 19.3 %collective-permute-start.14 = (bf16[2,2,16,32,128]{4,3,2,1,0:T(8,128)(2,1)}, bf16[2,2,16,32,128]{4,3,2,1,0:T(8,128)(2,1)S(1)}, u32[]{:S(2)}, u32[]{:S(2)}) collective-permute-start(bf16[2,2,16,32,128]{4,3,2,1,0:T(8,128)(2,1)} %collective-permute-done.12.refs_5_), channel_id=1, source_target_pairs={{0,7},{1,0},{2,1},{3,2},{4,3},{5,4},{6,5},{7,6},{8,15},{9,8},{10,9... | collective-permute-start | bytes 1572872 | tf_op jit(solution)/shard_map/ppermute | solution.py:33
  131.8 9.0 %collective-permute-start.19 = (f32[1,448,512]{2,1,0:T(8,128)S(1)}, f32[1,448,512]{2,1,0:T(8,128)S(1)}, u32[]{:S(2)}, u32[]{:S(2)}) collective-permute-start(f32[1,448,512]{2,1,0:T(8,128)S(1)} %get-tuple-element.26), channel_id=1, source_target_pairs={{0,16},{1,17},{2,18},{3,19},{4,20},{5,21},{6,22},{7,23},{8,24},{9,... | collective-permute-start | bytes 2752520 | tf_op jit(solution)/shard_map/ppermute | solution.py:33
  137.9 26.9 %collective-permute-start.18 = (f32[1,448,512]{2,1,0:T(8,128)S(1)}, f32[1,448,512]{2,1,0:T(8,128)S(1)}, u32[]{:S(2)}, u32[]{:S(2)}) collective-permute-start(f32[1,448,512]{2,1,0:T(8,128)S(1)} %get-tuple-element.24), channel_id=1, source_target_pairs={{0,16},{1,17},{2,18},{3,19},{4,20},{5,21},{6,22},{7,23},{8,24},{9,... | collective-permute-start | bytes 2752520 | tf_op jit(solution)/shard_map/ppermute | solution.py:33
  138.0 8.7 %collective-permute-start.21 = (bf16[1,2,16,32,128]{4,3,2,1,0:T(8,128)(2,1)S(1)}, bf16[1,2,16,32,128]{4,3,2,1,0:T(8,128)(2,1)S(1)}, u32[]{:S(2)}, u32[]{:S(2)}) collective-permute-start(bf16[1,2,16,32,128]{4,3,2,1,0:T(8,128)(2,1)S(1)} %slice.26), channel_id=1, source_target_pairs={{0,1},{1,2},{2,3},{3,4},{4,5},{5,6},{6,7},{7,0},{8,9},{9,10},{10,1... | collective-permute-start | bytes 786440 | tf_op jit(solution)/shard_map/ppermute | solution.py:33
  138.1 8.6 %collective-permute-start.22 = (bf16[1,2,16,32,128]{4,3,2,1,0:T(8,128)(2,1)S(1)}, bf16[1,2,16,32,128]{4,3,2,1,0:T(8,128)(2,1)S(1)}, u32[]{:S(2)}, u32[]{:S(2)}) collective-permute-start(bf16[1,2,16,32,128]{4,3,2,1,0:T(8,128)(2,1)S(1)} %slice.27), channel_id=1, source_target_pairs={{0,7},{1,0},{2,1},{3,2},{4,3},{5,4},{6,5},{7,6},{8,15},{9,8},{10,9... | collective-permute-start | bytes 786440 | tf_op jit(solution)/shard_map/ppermute | solution.py:33
  141.1 23.7 %collective-permute-start.20 = (f32[448,512]{1,0:T(8,128)S(1)}, f32[448,512]{1,0:T(8,128)S(1)}, u32[]{:S(2)}, u32[]{:S(2)}) collective-permute-start(f32[448,512]{1,0:T(8,128)S(1)} %add_bitcast_fusion), channel_id=1, source_target_pairs={{0,8},{1,9},{2,10},{3,11},{4,12},{5,13},{6,14},{7,15},{8,0},{9,1},... | collective-permute-start | bytes 2752520 | tf_op jit(solution)/shard_map/ppermute | solution.py:33
  149.4 2.5 %collective-permute-start.23 = (f32[2,64,512]{2,1,0:T(8,128)S(1)}, f32[2,64,512]{2,1,0:T(8,128)S(1)}, u32[]{:S(2)}, u32[]{:S(2)}) collective-permute-start(f32[2,64,512]{2,1,0:T(8,128)S(1)} %get-tuple-element.28), channel_id=1, source_target_pairs={{0,16},{1,17},{2,18},{3,19},{4,20},{5,21},{6,22},{7,23},{8,24},{9,... | collective-permute-start | bytes 786440 | tf_op jit(solution)/shard_map/ppermute | solution.py:33
  151.9 12.8 %collective-permute-start.24 = (f32[64,512]{1,0:T(8,128)S(1)}, f32[64,512]{1,0:T(8,128)S(1)}, u32[]{:S(2)}, u32[]{:S(2)}) collective-permute-start(f32[64,512]{1,0:T(8,128)S(1)} %fusion), channel_id=1, source_target_pairs={{0,8},{1,9},{2,10},{3,11},{4,12},{5,13},{6,14},{7,15},{8,0},{9,1},... | collective-permute-start | bytes 393224 | tf_op jit(solution)/shard_map/ppermute | solution.py:33
  (7 other events, 30.9 us)

commit v5 on v4

--- a/solution.py
+++ b/solution.py
@@ -112,21 +112,29 @@
     eye = (row == col).astype(BF)
     mixed = (key[...].astype(F32) * value[...].astype(F32)).astype(BF)
     for place, block in enumerate((mixed, filt[...], gate[...])):
-        turned = lax.dot_general(
-            eye, block, (((1,), (1,)), ((), ())), preferred_element_type=F32
-        ).astype(BF)
-        for j in range(4):
-            out[j, 32 * place : 32 * place + 32, :] = turned[32 * j : 32 * j + 32, :]
+        for part in range(4):
+            turned = lax.dot_general(
+                eye,
+                block[:, 128 * part : 128 * part + 128],
+                (((1,), (1,)), ((), ())),
+                preferred_element_type=F32,
+            ).astype(BF)
+            for j in range(4):
+                out[4 * part + j, 32 * place : 32 * place + 32, :] = turned[
+                    32 * j : 32 * j + 32, :
+                ]
 
 
 def prepare(gate, key, value, filt):
-    block = pl.BlockSpec((512, 128), lambda i: (0, i))
     return pl.pallas_call(
         prepare_kernel,
-        grid=(4,),
-        in_specs=[block] * 4,
-        out_specs=pl.BlockSpec((4, 96, 512), lambda i: (i, 0, 0)),
+        in_specs=[VMEM] * 4,
+        out_specs=VMEM,
         out_shape=jax.ShapeDtypeStruct((16, 96, 512), BF),
+        compiler_params=pltpu.CompilerParams(vmem_limit_bytes=16 * MIB),
+        cost_estimate=pl.CostEstimate(
+            flops=10**8, bytes_accessed=4 * 10**6, transcendentals=0
+        ),
         name="prepare",
     )(gate, key, value, filt)
 
@@ -222,17 +230,21 @@
     )(where, skips, data, *tables())
 
 
-def columns_kernel(where, own, below, above, far, right):
+def columns_kernel(where, own, below, above, far_low, far_high, right):
     y, core = where[1], where[2]
     for j in range(2):
         from_x = where[4 + j]
-        for step, shard in ((0, own), (-1, below), (1, above), (2, far)):
+        for step in (0, -1, 1, 2):
             from_y = (y + step + 4) % 4
             base = 32 * (8 * (from_x // 2) + 2 * from_y)
             for rel in range(2):
                 row = pl.ds(pl.multiple_of(base + 32 * ((core + rel) % 2), 32), 32)
+                if step == 2:
+                    piece = (far_low, far_high)[rel].at[j, 0]
+                else:
+                    piece = {0: own, -1: below, 1: above}[step].at[j, rel]
                 for a in range(16):
-                    right[row, 128 * a : 128 * a + 128] = shard[j, rel, a]
+                    right[row, 128 * a : 128 * a + 128] = piece[a]
 
 
 def columns(where, *shards):
@@ -386,10 +398,11 @@
 
     near_up, near_down = along_y(near, 1), along_y(near, 3)
     (own,) = after([[same, opposite]], near_up, near_down)
-    near_far, own_down = along_y(near_up, 1), along_y(own, 3)
-    own_up, own_far = along_y(own, 1), along_y(own_down, 3)
-    right = columns(beside, near, near_up, near_down, near_far)
-    own_right = columns(across, own, own_up, own_down, own_far)
+    near_far = along_y(near_up[:, :1], 1), along_y(near_down[:, 1:], 3)
+    own_up, own_down = along_y(own, 1), along_y(own, 3)
+    own_far = along_y(own_up[:, :1], 1), along_y(own_down[:, 1:], 3)
+    right = columns(beside, near, near_up, near_down, *near_far)
+    own_right = columns(across, own, own_up, own_down, *own_far)
 
     early = [rows, ups[1], downs[1], ups[2], downs[2], ups[3], downs[3]]
     keep, send, left = gram_part(CHUNKS[0], where, [right], early, own_right)

time: 167 us -> 166 us (level)
  local copies, waits for them, and re-layouts: 4.53 us -> 10.2 us
  waiting for transfers between devices: 87.4 us -> 81.8 us
  Pallas kernels: 24.3 us -> 21.3 us
    ppermute x25 -> x27, waiting for transfers between devices: 65.4 us -> 59.8 us  [move(): return lax.ppermute(array, MESH, pairs)]
    unnamed x26 -> x42, local copies, waits for them, and re-layouts: 3.48 us -> 6.9 us
    pallas_call x1, Pallas kernels: 4.26 us -> 1.79 us  [prepare(): pl.pallas_call(prepare_kernel, in_specs=[VMEM] * 4, out_specs=VMEM, out_s...]
    slice x0 -> x4, local copies, waits for them, and re-layouts: none -> 2.22 us  [the longest x2 1.48 us: local(): own_far = (along_y(own_up[:, :1], 1), along_y(own_down[:, 1:], 3))]
    ppermute x25 -> x27, starting transfers between devices: 41.1 us -> 41.8 us  [move(): return lax.ppermute(array, MESH, pairs)]
  transfers between devices with their start and end apart: 26 -> 28, of which waited for: 11 -> 12; matrix products, arithmetic and copies ran while one was open for 1% -> 2% of each run, Pallas kernels for 5% -> 5%
where the time goes in v5:
time: 166 us; the launch traced here: 164 us
  waiting for transfers between devices  81.8 us (49%)
  starting transfers between devices  50.4 us (30%)
  Pallas kernels  21.3 us (13%)
  local copies, waits for them, and re-layouts  10.2 us (6%)
    ppermute x27, waiting for transfers between devices, move(): return lax.ppermute(array, MESH, pairs)  59.8 us
    ppermute x27, starting transfers between devices, move(): return lax.ppermute(array, MESH, pairs)  41.8 us
    all_to_all x1, waiting for transfers between devices, local(): lax.all_to_all(outgoing, 'seq', split_axis=0, concat_axis=0, tiled=True)  22 us
    all_to_all x1, starting transfers between devices, local(): lax.all_to_all(outgoing, 'seq', split_axis=0, concat_axis=0, tiled=True)  8.59 us
    unnamed x42, local copies, waits for them, and re-layouts  6.9 us
    pallas_call x2, Pallas kernels, gram_part(): pl.pallas_call(functools.partial(gram_kernel, steps, len(rights), len(ear...  6.61 us
    pallas_call x1, Pallas kernels, convolve(): pl.pallas_call(conv_kernel, in_specs=[SMEM, SMEM] + [VMEM] * 7, out_specs...  6.24 us
  transfers between devices with their start and end apart: 28, of which 12 were waited for; matrix products, arithmetic and copies ran while one was open for 2% of the time, Pallas kernels for 5%

profile of v5, /device:TPU:1, one launch (start us, length us, event | category | flops | bytes accessed | tf_op | source)
XLA Modules:
  0.0 164.3 jit_solution(8450260782077581261)
XLA Ops:
  4.2 1.8 %prepare.1 = bf16[16,96,512]{2,1,0:T(8,128)(2,1)} custom-call(bf16[512,512]{1,0:T(8,128)(2,1)S(1)} %copy-done.3, bf16[512,512]{1,0:T(8,128)(2,1)S(1)} %copy-done.4, bf16[512,512]{1,0:T(8,128)(2,1)S(1)} %copy-done.5, bf16[512,512]{1,0:T(8,128)(2,1)S(1)} %copy-done.6), custom_call_target="tpu_custom_call" | custom-call | flops 100000000 | bytes 4000000 | tf_op jit(solution)/shard_map/prepare/pallas_call | solution.py:129
  6.0 8.6 %all-to-all-start = ((bf16[16,96,512]{2,1,0:T(8,128)(2,1)}), bf16[16,96,512]{2,1,0:T(8,128)(2,1)S(1)}, u32[]{:S(2)}, u32[]{:S(2)}) async-start(bf16[16,96,512]{2,1,0:T(8,128)(2,1)} %prepare.1), calls=%async_computation | async-start | bytes 3145728 | tf_op jit(solution)/shard_map/all_to_all | solution.py:379
  15.4 22.0 %all-to-all-done.data = bf16[16,96,512]{2,1,0:T(8,128)(2,1)S(1)} async-done(((bf16[16,96,512]{2,1,0:T(8,128)(2,1)}), bf16[16,96,512]{2,1,0:T(8,128)(2,1)S(1)}, u32[]{:S(2)}, u32[]{:S(2)}) %all-to-all-start) | async-done | bytes 1572896 | tf_op jit(solution)/shard_map/all_to_all | solution.py:379
  37.5 6.2 %convolve.1 = (bf16[16,32,128]{2,1,0:T(8,128)(2,1)S(1)}, bf16[16,32,128]{2,1,0:T(8,128)(2,1)S(1)}, bf16[2,16,32,128]{3,2,1,0:T(8,128)(2,1)S(1)}) custom-call(s32[6]{0:T(128)S(1)} %stack.57.where, f32[32]{0:T(128)S(1)} %dynamic_slice.3.skip, bf16[16,96,512]{2,1,0:T(8,128)(2,1)S(1)} %all-to-all-done.data, bf16[256,64]{1,0:T(8,128)(2,1)S(1)} %copy-done.17, ...), custom_call_target="tpu_custom_call" | custom-call | flops 4000000000 | bytes 3000000 | tf_op jit(solution)/shard_map/convolve/pallas_call | solution.py:219
  44.7 1.2 collective-permute-done
  46.7 1.7 %collective-permute-start.2 = (bf16[2,16,32,128]{3,2,1,0:T(8,128)(2,1)S(1)}, bf16[2,16,32,128]{3,2,1,0:T(8,128)(2,1)S(1)}, u32[]{:S(2)}, u32[]{:S(2)}) collective-permute-start(bf16[2,16,32,128]{3,2,1,0:T(8,128)(2,1)S(1)} %get-tuple-element.29), channel_id=1, source_target_pairs={{0,8},{1,9},{2,46},{3,47},{4,76},{5,77},{6,106},{7,107},{8,136},{9... | collective-permute-start | bytes 786440 | tf_op jit(solution)/shard_map/ppermute | solution.py:33
  48.4 3.0 %collective-permute-start.3 = (bf16[2,16,32,128]{3,2,1,0:T(8,128)(2,1)S(1)}, bf16[2,16,32,128]{3,2,1,0:T(8,128)(2,1)S(1)}, u32[]{:S(2)}, u32[]{:S(2)}) collective-permute-start(bf16[2,16,32,128]{3,2,1,0:T(8,128)(2,1)S(1)} %get-tuple-element.32), channel_id=1, source_target_pairs={{0,136},{1,137},{2,138},{3,139},{4,140},{5,141},{6,142},{7,143},{8... | collective-permute-start | bytes 786440 | tf_op jit(solution)/shard_map/ppermute | solution.py:33
  51.3 1.7 %collective-permute-start.5 = (bf16[2,16,32,128]{3,2,1,0:T(8,128)(2,1)S(1)}, bf16[2,16,32,128]{3,2,1,0:T(8,128)(2,1)S(1)}, u32[]{:S(2)}, u32[]{:S(2)}) collective-permute-start(bf16[2,16,32,128]{3,2,1,0:T(8,128)(2,1)S(1)} %get-tuple-element.31.refs_4_.refs_0_), channel_id=1, source_target_pairs={{0,128},{1,129},{2,130},{3,131},{4,132},{5,133},{6,134},{7,135},{8... | collective-permute-start | bytes 786440 | tf_op jit(solution)/shard_map/ppermute | solution.py:33
  53.0 20.8 %collective-permute-done.2.refs_1_ = bf16[2,16,32,128]{3,2,1,0:T(8,128)(2,1)S(1)} collective-permute-done((bf16[2,16,32,128]{3,2,1,0:T(8,128)(2,1)S(1)}, bf16[2,16,32,128]{3,2,1,0:T(8,128)(2,1)S(1)}, u32[]{:S(2)}, u32[]{:S(2)}) %collective-permute-start.2) | collective-permute-done | bytes 262176 | tf_op jit(solution)/shard_map/ppermute | solution.py:33
  74.0 1.7 %collective-permute-start.10 = (bf16[2,2,16,32,128]{4,3,2,1,0:T(8,128)(2,1)S(1)}, bf16[2,2,16,32,128]{4,3,2,1,0:T(8,128)(2,1)S(1)}, u32[]{:S(2)}, u32[]{:S(2)}) collective-permute-start(bf16[2,2,16,32,128]{4,3,2,1,0:T(8,128)(2,1)S(1)} %get-tuple-element.21.refs_1_), channel_id=1, source_target_pairs={{0,1},{1,2},{2,3},{3,4},{4,5},{5,6},{6,7},{7,0},{8,9},{9,10},{10,1... | collective-permute-start | bytes 1572872 | tf_op jit(solution)/shard_map/ppermute | solution.py:33
  75.7 8.3 %collective-permute-start.11 = (bf16[2,2,16,32,128]{4,3,2,1,0:T(8,128)(2,1)S(1)}, bf16[2,2,16,32,128]{4,3,2,1,0:T(8,128)(2,1)S(1)}, u32[]{:S(2)}, u32[]{:S(2)}) collective-permute-start(bf16[2,2,16,32,128]{4,3,2,1,0:T(8,128)(2,1)S(1)} %get-tuple-element.21.refs_1_), channel_id=1, source_target_pairs={{0,7},{1,0},{2,1},{3,2},{4,3},{5,4},{6,5},{7,6},{8,15},{9,8},{10,9... | collective-permute-start | bytes 1572872 | tf_op jit(solution)/shard_map/ppermute | solution.py:33
  84.0 2.7 %collective-permute-start.7 = (bf16[2,2,16,32,128]{4,3,2,1,0:T(8,128)(2,1)S(1)}, bf16[2,2,16,32,128]{4,3,2,1,0:T(8,128)(2,1)S(1)}, u32[]{:S(2)}, u32[]{:S(2)}) collective-permute-start(bf16[2,2,16,32,128]{4,3,2,1,0:T(8,128)(2,1)S(1)} %get-tuple-element.20.own), channel_id=1, source_target_pairs={{0,96},{1,97},{2,98},{3,99},{4,100},{5,101},{6,102},{7,103},{8,104... | collective-permute-start | bytes 1572872 | tf_op jit(solution)/shard_map/ppermute | solution.py:33
  87.5 7.5 %collective-permute-done.10.refs_2_ = bf16[2,2,16,32,128]{4,3,2,1,0:T(8,128)(2,1)S(1)} collective-permute-done((bf16[2,2,16,32,128]{4,3,2,1,0:T(8,128)(2,1)S(1)}, bf16[2,2,16,32,128]{4,3,2,1,0:T(8,128)(2,1)S(1)}, u32[]{:S(2)}, u32[]{:S(2)}) %collective-permute-start.10) | collective-permute-done | bytes 524320 | tf_op jit(solution)/shard_map/ppermute | solution.py:33
  95.0 2.7 %collective-permute-start.13 = (bf16[2,2,16,32,128]{4,3,2,1,0:T(8,128)(2,1)S(1)}, bf16[2,2,16,32,128]{4,3,2,1,0:T(8,128)(2,1)}, u32[]{:S(2)}, u32[]{:S(2)}) collective-permute-start(bf16[2,2,16,32,128]{4,3,2,1,0:T(8,128)(2,1)S(1)} %collective-permute-done.11.refs_3_), channel_id=1, source_target_pairs={{0,7},{1,0},{2,1},{3,2},{4,3},{5,4},{6,5},{7,6},{8,15},{9,8},{10,9... | collective-permute-start | bytes 1572872 | tf_op jit(solution)/shard_map/ppermute | solution.py:33
  98.0 2.7 %collective-permute-start.17 = (bf16[2,2,16,32,128]{4,3,2,1,0:T(8,128)(2,1)S(1)}, bf16[2,2,16,32,128]{4,3,2,1,0:T(8,128)(2,1)S(1)}, u32[]{:S(2)}, u32[]{:S(2)}) collective-permute-start(bf16[2,2,16,32,128]{4,3,2,1,0:T(8,128)(2,1)S(1)} %after.3.own), channel_id=1, source_target_pairs={{0,96},{1,97},{2,98},{3,99},{4,100},{5,101},{6,102},{7,103},{8,104... | collective-permute-start | bytes 1572872 | tf_op jit(solution)/shard_map/ppermute | solution.py:33
  100.8 7.1 %collective-permute-done.12.refs_4_ = bf16[2,2,16,32,128]{4,3,2,1,0:T(8,128)(2,1)} collective-permute-done((bf16[2,2,16,32,128]{4,3,2,1,0:T(8,128)(2,1)S(1)}, bf16[2,2,16,32,128]{4,3,2,1,0:T(8,128)(2,1)}, u32[]{:S(2)}, u32[]{:S(2)}) %collective-permute-start.12) | collective-permute-done | bytes 524320 | tf_op jit(solution)/shard_map/ppermute | solution.py:33
  107.9 2.7 %collective-permute-start.15 = (bf16[2,2,16,32,128]{4,3,2,1,0:T(8,128)(2,1)}, bf16[2,2,16,32,128]{4,3,2,1,0:T(8,128)(2,1)S(1)}, u32[]{:S(2)}, u32[]{:S(2)}) collective-permute-start(bf16[2,2,16,32,128]{4,3,2,1,0:T(8,128)(2,1)} %collective-permute-done.13.refs_5_), channel_id=1, source_target_pairs={{0,7},{1,0},{2,1},{3,2},{4,3},{5,4},{6,5},{7,6},{8,15},{9,8},{10,9... | collective-permute-start | bytes 1572872 | tf_op jit(solution)/shard_map/ppermute | solution.py:33
  117.0 1.1 copy-done.14
  118.1 1.3 columns.2.refs_0_.refs_1_
  119.5 2.1 %collective-permute-done.18.far_low = bf16[2,1,16,32,128]{4,3,2,1,0:T(8,128)(2,1)} collective-permute-done((bf16[2,1,16,32,128]{4,3,2,1,0:T(8,128)(2,1)}, bf16[2,1,16,32,128]{4,3,2,1,0:T(8,128)(2,1)}, u32[]{:S(2)}, u32[]{:S(2)}) %collective-permute-start.18) | collective-permute-done | bytes 262176 | tf_op jit(solution)/shard_map/ppermute | solution.py:33
  121.6 2.0 %collective-permute-done.19.far_high = bf16[2,1,16,32,128]{4,3,2,1,0:T(8,128)(2,1)} collective-permute-done((bf16[2,1,16,32,128]{4,3,2,1,0:T(8,128)(2,1)}, bf16[2,1,16,32,128]{4,3,2,1,0:T(8,128)(2,1)}, u32[]{:S(2)}, u32[]{:S(2)}) %collective-permute-start.19) | collective-permute-done | bytes 262176 | tf_op jit(solution)/shard_map/ppermute | solution.py:33
  123.5 1.4 columns.3.refs_8_.right.refs_0_
  125.0 3.9 %gram_part.2 = (f32[1,448,512]{2,1,0:T(8,128)S(1)}, f32[1,448,512]{2,1,0:T(8,128)S(1)}, bf16[896,2048]{1,0:T(8,128)(2,1)S(1)}) custom-call(s32[6]{0:T(128)S(1)} %stack.57.where, bf16[512,2048]{1,0:T(8,128)(2,1)S(1)} %columns.2.refs_0_.refs_1_, bf16[2,2,16,32,128]{4,3,2,1,0:T(8,128)(2,1)S(1)} %copy-done.8, bf16[2,2,16,32,128]{4,3,2,1,0:T(8,128)(2,1)S(1)} %copy-done.10, ...), custom_call_target="tpu_custom_call" | custom-call | flops 1879048192 | bytes 4000000 | tf_op jit(solution)/shard_map/gram_part/pallas_call | solution.py:319
  129.0 4.4 %collective-permute-start.21 = (f32[1,448,512]{2,1,0:T(8,128)S(1)}, f32[1,448,512]{2,1,0:T(8,128)S(1)}, u32[]{:S(2)}, u32[]{:S(2)}) collective-permute-start(f32[1,448,512]{2,1,0:T(8,128)S(1)} %get-tuple-element.26), channel_id=1, source_target_pairs={{0,16},{1,17},{2,18},{3,19},{4,20},{5,21},{6,22},{7,23},{8,24},{9,... | collective-permute-start | bytes 2752520 | tf_op jit(solution)/shard_map/ppermute | solution.py:33
  133.3 2.1 %gram_again.1 = (f32[1,448,512]{2,1,0:T(8,128)S(1)}, f32[1,448,512]{2,1,0:T(8,128)S(1)}) custom-call(bf16[896,2048]{1,0:T(8,128)(2,1)S(1)} %get-tuple-element.22.left, bf16[512,2048]{1,0:T(8,128)(2,1)S(1)} %columns.3.refs_8_.right.refs_0_), custom_call_target="tpu_custom_call" | custom-call | flops 1879048192 | bytes 4000000 | tf_op jit(solution)/shard_map/gram_again/pallas_call | solution.py:303
  135.7 3.0 %collective-permute-start.24 = (bf16[1,2,16,32,128]{4,3,2,1,0:T(8,128)(2,1)S(1)}, bf16[1,2,16,32,128]{4,3,2,1,0:T(8,128)(2,1)S(1)}, u32[]{:S(2)}, u32[]{:S(2)}) collective-permute-start(bf16[1,2,16,32,128]{4,3,2,1,0:T(8,128)(2,1)S(1)} %slice.47), channel_id=1, source_target_pairs={{0,7},{1,0},{2,1},{3,2},{4,3},{5,4},{6,5},{7,6},{8,15},{9,8},{10,9... | collective-permute-start | bytes 786440 | tf_op jit(solution)/shard_map/ppermute | solution.py:33
  139.5 4.7 %collective-permute-done.23.refs_2_ = bf16[1,2,16,32,128]{4,3,2,1,0:T(8,128)(2,1)S(1)} collective-permute-done((bf16[1,2,16,32,128]{4,3,2,1,0:T(8,128)(2,1)S(1)}, bf16[1,2,16,32,128]{4,3,2,1,0:T(8,128)(2,1)S(1)}, u32[]{:S(2)}, u32[]{:S(2)}) %collective-permute-start.23) | collective-permute-done | bytes 262176 | tf_op jit(solution)/shard_map/ppermute | solution.py:33
  144.2 2.7 %gram_part.3 = (f32[2,64,512]{2,1,0:T(8,128)S(1)}, f32[2,64,512]{2,1,0:T(8,128)S(1)}, bf16[128,2048]{1,0:T(8,128)(2,1)}) custom-call(s32[6]{0:T(128)S(1)} %stack.57.where, bf16[512,2048]{1,0:T(8,128)(2,1)S(1)} %columns.3.refs_8_.right.refs_0_, bf16[512,2048]{1,0:T(8,128)(2,1)S(1)} %columns.2.refs_0_.refs_1_, ...), custom_call_target="tpu_custom_call" | custom-call | flops 536870912 | bytes 4000000 | tf_op jit(solution)/shard_map/gram_part/pallas_call | solution.py:319
  146.9 1.3 collective-permute-start.25
  148.2 1.2 collective-permute-done.25.refs_4_
  150.1 12.4 %collective-permute-done.26.refs_5_ = f32[64,512]{1,0:T(8,128)S(1)} collective-permute-done((f32[64,512]{1,0:T(8,128)S(1)}, f32[64,512]{1,0:T(8,128)S(1)}, u32[]{:S(2)}, u32[]{:S(2)}) %collective-permute-start.26) | collective-permute-done | bytes 131104 | tf_op jit(solution)/shard_map/ppermute | solution.py:33
  162.5 1.7 %finish.1 = f32[512,512]{1,0:T(8,128)} custom-call(s32[6]{0:T(128)S(1)} %stack.57.where, f32[512,512]{1,0:T(8,128)S(1)} %copy-done.2, f32[1,448,512]{2,1,0:T(8,128)S(1)} %get-tuple-element.23.refs_0_, f32[1,448,512]{2,1,0:T(8,128)S(1)} %collective-permute-done.20.refs_1_, f32[448,512]{1,0:T(8,128)S(1)} %collective-permute-done.22.refs_2_, ...), custom_call_target="tpu_custom_call" | custom-call | flops 1000000 | bytes 5000000 | tf_op jit(solution)/shard_map/finish/pallas_call | solution.py:354
  (90 shorter events, 16.4 us)
Async XLA Ops:
  6.0 31.5 %copy-start.17 = (bf16[256,64]{1,0:T(8,128)(2,1)S(1)}, bf16[256,64]{1,0:T(8,128)(2,1)}, u32[]{:S(2)}) copy-start(bf16[256,64]{1,0:T(8,128)(2,1)} %constant.114.first) | copy-start | bytes 98308
  6.0 31.5 %copy-start.18 = (f32[128,128]{1,0:T(8,128)S(1)}, f32[128,128]{1,0:T(8,128)}, u32[]{:S(2)}) copy-start(f32[128,128]{1,0:T(8,128)} %constant.112.clone.t_cos) | copy-start | bytes 196612
  6.0 31.5 %copy-start.19 = (f32[128,128]{1,0:T(8,128)S(1)}, f32[128,128]{1,0:T(8,128)}, u32[]{:S(2)}) copy-start(f32[128,128]{1,0:T(8,128)} %constant.113.clone.t_sin) | copy-start | bytes 196612
  6.0 31.5 %copy-start.20 = (bf16[64,256]{1,0:T(8,128)(2,1)S(1)}, bf16[64,256]{1,0:T(8,128)(2,1)}, u32[]{:S(2)}) copy-start(bf16[64,256]{1,0:T(8,128)(2,1)} %constant.115.last) | copy-start | bytes 98308
  6.0 31.4 %all-to-all-start = ((bf16[16,96,512]{2,1,0:T(8,128)(2,1)}), bf16[16,96,512]{2,1,0:T(8,128)(2,1)S(1)}, u32[]{:S(2)}, u32[]{:S(2)}) async-start(bf16[16,96,512]{2,1,0:T(8,128)(2,1)} %prepare.1), calls=%async_computation | async-start | bytes 3145728 | tf_op jit(solution)/shard_map/all_to_all | solution.py:379
  43.7 2.2 %collective-permute-start = (bf16[2,16,32,128]{3,2,1,0:T(8,128)(2,1)S(1)}, bf16[2,16,32,128]{3,2,1,0:T(8,128)(2,1)S(1)}, u32[]{:S(2)}, u32[]{:S(2)}) collective-permute-start(bf16[2,16,32,128]{3,2,1,0:T(8,128)(2,1)S(1)} %get-tuple-element.18), channel_id=1, source_target_pairs={{0,16},{1,17},{2,18},{3,19},{4,20},{5,21},{6,22},{7,23},{8,24},{9,... | collective-permute-start | bytes 786440 | tf_op jit(solution)/shard_map/ppermute | solution.py:33
  46.0 7.0 %collective-permute-start.1 = (bf16[2,16,32,128]{3,2,1,0:T(8,128)(2,1)S(1)}, bf16[2,16,32,128]{3,2,1,0:T(8,128)(2,1)S(1)}, u32[]{:S(2)}, u32[]{:S(2)}) collective-permute-start(bf16[2,16,32,128]{3,2,1,0:T(8,128)(2,1)S(1)} %get-tuple-element.30), channel_id=1, source_target_pairs={{0,0},{1,1},{2,38},{3,39},{4,68},{5,69},{6,98},{7,99},{8,128},{9,1... | collective-permute-start | bytes 786440 | tf_op jit(solution)/shard_map/ppermute | solution.py:33
  46.7 27.2 %collective-permute-start.2 = (bf16[2,16,32,128]{3,2,1,0:T(8,128)(2,1)S(1)}, bf16[2,16,32,128]{3,2,1,0:T(8,128)(2,1)S(1)}, u32[]{:S(2)}, u32[]{:S(2)}) collective-permute-start(bf16[2,16,32,128]{3,2,1,0:T(8,128)(2,1)S(1)} %get-tuple-element.29), channel_id=1, source_target_pairs={{0,8},{1,9},{2,46},{3,47},{4,76},{5,77},{6,106},{7,107},{8,136},{9... | collective-permute-start | bytes 786440 | tf_op jit(solution)/shard_map/ppermute | solution.py:33
  48.4 25.5 %collective-permute-start.3 = (bf16[2,16,32,128]{3,2,1,0:T(8,128)(2,1)S(1)}, bf16[2,16,32,128]{3,2,1,0:T(8,128)(2,1)S(1)}, u32[]{:S(2)}, u32[]{:S(2)}) collective-permute-start(bf16[2,16,32,128]{3,2,1,0:T(8,128)(2,1)S(1)} %get-tuple-element.32), channel_id=1, source_target_pairs={{0,136},{1,137},{2,138},{3,139},{4,140},{5,141},{6,142},{7,143},{8... | collective-permute-start | bytes 786440 | tf_op jit(solution)/shard_map/ppermute | solution.py:33
  51.3 22.6 %collective-permute-start.4 = (bf16[2,16,32,128]{3,2,1,0:T(8,128)(2,1)S(1)}, bf16[2,16,32,128]{3,2,1,0:T(8,128)(2,1)S(1)}, u32[]{:S(2)}, u32[]{:S(2)}) collective-permute-start(bf16[2,16,32,128]{3,2,1,0:T(8,128)(2,1)S(1)} %get-tuple-element.32), channel_id=1, source_target_pairs={{0,8},{1,9},{2,10},{3,11},{4,12},{5,13},{6,14},{7,15},{8,128},{9,1... | collective-permute-start | bytes 786440 | tf_op jit(solution)/shard_map/ppermute | solution.py:33
  51.3 22.6 %collective-permute-start.5 = (bf16[2,16,32,128]{3,2,1,0:T(8,128)(2,1)S(1)}, bf16[2,16,32,128]{3,2,1,0:T(8,128)(2,1)S(1)}, u32[]{:S(2)}, u32[]{:S(2)}) collective-permute-start(bf16[2,16,32,128]{3,2,1,0:T(8,128)(2,1)S(1)} %get-tuple-element.31.refs_4_.refs_0_), channel_id=1, source_target_pairs={{0,128},{1,129},{2,130},{3,131},{4,132},{5,133},{6,134},{7,135},{8... | collective-permute-start | bytes 786440 | tf_op jit(solution)/shard_map/ppermute | solution.py:33
  74.0 21.0 %collective-permute-start.10 = (bf16[2,2,16,32,128]{4,3,2,1,0:T(8,128)(2,1)S(1)}, bf16[2,2,16,32,128]{4,3,2,1,0:T(8,128)(2,1)S(1)}, u32[]{:S(2)}, u32[]{:S(2)}) collective-permute-start(bf16[2,2,16,32,128]{4,3,2,1,0:T(8,128)(2,1)S(1)} %get-tuple-element.21.refs_1_), channel_id=1, source_target_pairs={{0,1},{1,2},{2,3},{3,4},{4,5},{5,6},{6,7},{7,0},{8,9},{9,10},{10,1... | collective-permute-start | bytes 1572872 | tf_op jit(solution)/shard_map/ppermute | solution.py:33
  75.7 19.3 %collective-permute-start.11 = (bf16[2,2,16,32,128]{4,3,2,1,0:T(8,128)(2,1)S(1)}, bf16[2,2,16,32,128]{4,3,2,1,0:T(8,128)(2,1)S(1)}, u32[]{:S(2)}, u32[]{:S(2)}) collective-permute-start(bf16[2,2,16,32,128]{4,3,2,1,0:T(8,128)(2,1)S(1)} %get-tuple-element.21.refs_1_), channel_id=1, source_target_pairs={{0,7},{1,0},{2,1},{3,2},{4,3},{5,4},{6,5},{7,6},{8,15},{9,8},{10,9... | collective-permute-start | bytes 1572872 | tf_op jit(solution)/shard_map/ppermute | solution.py:33
  84.0 13.7 %collective-permute-start.6 = (bf16[2,2,16,32,128]{4,3,2,1,0:T(8,128)(2,1)S(1)}, bf16[2,2,16,32,128]{4,3,2,1,0:T(8,128)(2,1)S(1)}, u32[]{:S(2)}, u32[]{:S(2)}) collective-permute-start(bf16[2,2,16,32,128]{4,3,2,1,0:T(8,128)(2,1)S(1)} %get-tuple-element.20.own), channel_id=1, source_target_pairs={{0,32},{1,33},{2,34},{3,35},{4,36},{5,37},{6,38},{7,39},{8,40},{9,... | collective-permute-start | bytes 1572872 | tf_op jit(solution)/shard_map/ppermute | solution.py:33
  84.0 13.7 %collective-permute-start.7 = (bf16[2,2,16,32,128]{4,3,2,1,0:T(8,128)(2,1)S(1)}, bf16[2,2,16,32,128]{4,3,2,1,0:T(8,128)(2,1)S(1)}, u32[]{:S(2)}, u32[]{:S(2)}) collective-permute-start(bf16[2,2,16,32,128]{4,3,2,1,0:T(8,128)(2,1)S(1)} %get-tuple-element.20.own), channel_id=1, source_target_pairs={{0,96},{1,97},{2,98},{3,99},{4,100},{5,101},{6,102},{7,103},{8,104... | collective-permute-start | bytes 1572872 | tf_op jit(solution)/shard_map/ppermute | solution.py:33
  95.0 12.9 %collective-permute-start.12 = (bf16[2,2,16,32,128]{4,3,2,1,0:T(8,128)(2,1)S(1)}, bf16[2,2,16,32,128]{4,3,2,1,0:T(8,128)(2,1)}, u32[]{:S(2)}, u32[]{:S(2)}) collective-permute-start(bf16[2,2,16,32,128]{4,3,2,1,0:T(8,128)(2,1)S(1)} %collective-permute-done.10.refs_2_), channel_id=1, source_target_pairs={{0,1},{1,2},{2,3},{3,4},{4,5},{5,6},{6,7},{7,0},{8,9},{9,10},{10,1... | collective-permute-start | bytes 1572872 | tf_op jit(solution)/shard_map/ppermute | solution.py:33
  95.0 12.9 %collective-permute-start.13 = (bf16[2,2,16,32,128]{4,3,2,1,0:T(8,128)(2,1)S(1)}, bf16[2,2,16,32,128]{4,3,2,1,0:T(8,128)(2,1)}, u32[]{:S(2)}, u32[]{:S(2)}) collective-permute-start(bf16[2,2,16,32,128]{4,3,2,1,0:T(8,128)(2,1)S(1)} %collective-permute-done.11.refs_3_), channel_id=1, source_target_pairs={{0,7},{1,0},{2,1},{3,2},{4,3},{5,4},{6,5},{7,6},{8,15},{9,8},{10,9... | collective-permute-start | bytes 1572872 | tf_op jit(solution)/shard_map/ppermute | solution.py:33
  97.7 13.6 %collective-permute-start.16 = (bf16[2,2,16,32,128]{4,3,2,1,0:T(8,128)(2,1)S(1)}, bf16[2,2,16,32,128]{4,3,2,1,0:T(8,128)(2,1)S(1)}, u32[]{:S(2)}, u32[]{:S(2)}) collective-permute-start(bf16[2,2,16,32,128]{4,3,2,1,0:T(8,128)(2,1)S(1)} %after.3.own), channel_id=1, source_target_pairs={{0,32},{1,33},{2,34},{3,35},{4,36},{5,37},{6,38},{7,39},{8,40},{9,... | collective-permute-start | bytes 1572872 | tf_op jit(solution)/shard_map/ppermute | solution.py:33
  98.0 14.6 %collective-permute-start.17 = (bf16[2,2,16,32,128]{4,3,2,1,0:T(8,128)(2,1)S(1)}, bf16[2,2,16,32,128]{4,3,2,1,0:T(8,128)(2,1)S(1)}, u32[]{:S(2)}, u32[]{:S(2)}) collective-permute-start(bf16[2,2,16,32,128]{4,3,2,1,0:T(8,128)(2,1)S(1)} %after.3.own), channel_id=1, source_target_pairs={{0,96},{1,97},{2,98},{3,99},{4,100},{5,101},{6,102},{7,103},{8,104... | collective-permute-start | bytes 1572872 | tf_op jit(solution)/shard_map/ppermute | solution.py:33
  100.7 15.2 %collective-permute-start.8 = (bf16[2,1,16,32,128]{4,3,2,1,0:T(8,128)(2,1)S(1)}, bf16[2,1,16,32,128]{4,3,2,1,0:T(8,128)(2,1)S(1)}, u32[]{:S(2)}, u32[]{:S(2)}) collective-permute-start(bf16[2,1,16,32,128]{4,3,2,1,0:T(8,128)(2,1)S(1)} %slice.42), channel_id=1, source_target_pairs={{0,32},{1,33},{2,34},{3,35},{4,36},{5,37},{6,38},{7,39},{8,40},{9,... | collective-permute-start | bytes 786440 | tf_op jit(solution)/shard_map/ppermute | solution.py:33
  107.9 17.1 %collective-permute-start.14 = (bf16[2,2,16,32,128]{4,3,2,1,0:T(8,128)(2,1)}, bf16[2,2,16,32,128]{4,3,2,1,0:T(8,128)(2,1)S(1)}, u32[]{:S(2)}, u32[]{:S(2)}) collective-permute-start(bf16[2,2,16,32,128]{4,3,2,1,0:T(8,128)(2,1)} %collective-permute-done.12.refs_4_), channel_id=1, source_target_pairs={{0,1},{1,2},{2,3},{3,4},{4,5},{5,6},{6,7},{7,0},{8,9},{9,10},{10,1... | collective-permute-start | bytes 1572872 | tf_op jit(solution)/shard_map/ppermute | solution.py:33
  107.9 17.1 %collective-permute-start.15 = (bf16[2,2,16,32,128]{4,3,2,1,0:T(8,128)(2,1)}, bf16[2,2,16,32,128]{4,3,2,1,0:T(8,128)(2,1)S(1)}, u32[]{:S(2)}, u32[]{:S(2)}) collective-permute-start(bf16[2,2,16,32,128]{4,3,2,1,0:T(8,128)(2,1)} %collective-permute-done.13.refs_5_), channel_id=1, source_target_pairs={{0,7},{1,0},{2,1},{3,2},{4,3},{5,4},{6,5},{7,6},{8,15},{9,8},{10,9... | collective-permute-start | bytes 1572872 | tf_op jit(solution)/shard_map/ppermute | solution.py:33
  111.3 5.7 %collective-permute-start.9 = (bf16[2,1,16,32,128]{4,3,2,1,0:T(8,128)(2,1)}, bf16[2,1,16,32,128]{4,3,2,1,0:T(8,128)(2,1)}, u32[]{:S(2)}, u32[]{:S(2)}) collective-permute-start(bf16[2,1,16,32,128]{4,3,2,1,0:T(8,128)(2,1)} %slice.43), channel_id=1, source_target_pairs={{0,96},{1,97},{2,98},{3,99},{4,100},{5,101},{6,102},{7,103},{8,104... | collective-permute-start | bytes 786440 | tf_op jit(solution)/shard_map/ppermute | solution.py:33
  112.6 9.0 %collective-permute-start.18 = (bf16[2,1,16,32,128]{4,3,2,1,0:T(8,128)(2,1)}, bf16[2,1,16,32,128]{4,3,2,1,0:T(8,128)(2,1)}, u32[]{:S(2)}, u32[]{:S(2)}) collective-permute-start(bf16[2,1,16,32,128]{4,3,2,1,0:T(8,128)(2,1)} %slice.44), channel_id=1, source_target_pairs={{0,32},{1,33},{2,34},{3,35},{4,36},{5,37},{6,38},{7,39},{8,40},{9,... | collective-permute-start | bytes 786440 | tf_op jit(solution)/shard_map/ppermute | solution.py:33
  115.9 7.7 %collective-permute-start.19 = (bf16[2,1,16,32,128]{4,3,2,1,0:T(8,128)(2,1)}, bf16[2,1,16,32,128]{4,3,2,1,0:T(8,128)(2,1)}, u32[]{:S(2)}, u32[]{:S(2)}) collective-permute-start(bf16[2,1,16,32,128]{4,3,2,1,0:T(8,128)(2,1)} %slice.45), channel_id=1, source_target_pairs={{0,96},{1,97},{2,98},{3,99},{4,100},{5,101},{6,102},{7,103},{8,104... | collective-permute-start | bytes 786440 | tf_op jit(solution)/shard_map/ppermute | solution.py:33
  129.0 9.7 %collective-permute-start.21 = (f32[1,448,512]{2,1,0:T(8,128)S(1)}, f32[1,448,512]{2,1,0:T(8,128)S(1)}, u32[]{:S(2)}, u32[]{:S(2)}) collective-permute-start(f32[1,448,512]{2,1,0:T(8,128)S(1)} %get-tuple-element.26), channel_id=1, source_target_pairs={{0,16},{1,17},{2,18},{3,19},{4,20},{5,21},{6,22},{7,23},{8,24},{9,... | collective-permute-start | bytes 2752520 | tf_op jit(solution)/shard_map/ppermute | solution.py:33
  135.4 27.1 %collective-permute-start.20 = (f32[1,448,512]{2,1,0:T(8,128)S(1)}, f32[1,448,512]{2,1,0:T(8,128)S(1)}, u32[]{:S(2)}, u32[]{:S(2)}) collective-permute-start(f32[1,448,512]{2,1,0:T(8,128)S(1)} %get-tuple-element.24), channel_id=1, source_target_pairs={{0,16},{1,17},{2,18},{3,19},{4,20},{5,21},{6,22},{7,23},{8,24},{9,... | collective-permute-start | bytes 2752520 | tf_op jit(solution)/shard_map/ppermute | solution.py:33
  135.6 8.7 %collective-permute-start.23 = (bf16[1,2,16,32,128]{4,3,2,1,0:T(8,128)(2,1)S(1)}, bf16[1,2,16,32,128]{4,3,2,1,0:T(8,128)(2,1)S(1)}, u32[]{:S(2)}, u32[]{:S(2)}) collective-permute-start(bf16[1,2,16,32,128]{4,3,2,1,0:T(8,128)(2,1)S(1)} %slice.46), channel_id=1, source_target_pairs={{0,1},{1,2},{2,3},{3,4},{4,5},{5,6},{6,7},{7,0},{8,9},{9,10},{10,1... | collective-permute-start | bytes 786440 | tf_op jit(solution)/shard_map/ppermute | solution.py:33
  135.7 8.6 %collective-permute-start.24 = (bf16[1,2,16,32,128]{4,3,2,1,0:T(8,128)(2,1)S(1)}, bf16[1,2,16,32,128]{4,3,2,1,0:T(8,128)(2,1)S(1)}, u32[]{:S(2)}, u32[]{:S(2)}) collective-permute-start(bf16[1,2,16,32,128]{4,3,2,1,0:T(8,128)(2,1)S(1)} %slice.47), channel_id=1, source_target_pairs={{0,7},{1,0},{2,1},{3,2},{4,3},{5,4},{6,5},{7,6},{8,15},{9,8},{10,9... | collective-permute-start | bytes 786440 | tf_op jit(solution)/shard_map/ppermute | solution.py:33
  138.8 23.7 %collective-permute-start.22 = (f32[448,512]{1,0:T(8,128)S(1)}, f32[448,512]{1,0:T(8,128)S(1)}, u32[]{:S(2)}, u32[]{:S(2)}) collective-permute-start(f32[448,512]{1,0:T(8,128)S(1)} %add_bitcast_fusion), channel_id=1, source_target_pairs={{0,8},{1,9},{2,10},{3,11},{4,12},{5,13},{6,14},{7,15},{8,0},{9,1},... | collective-permute-start | bytes 2752520 | tf_op jit(solution)/shard_map/ppermute | solution.py:33
  146.9 2.5 %collective-permute-start.25 = (f32[2,64,512]{2,1,0:T(8,128)S(1)}, f32[2,64,512]{2,1,0:T(8,128)S(1)}, u32[]{:S(2)}, u32[]{:S(2)}) collective-permute-start(f32[2,64,512]{2,1,0:T(8,128)S(1)} %get-tuple-element.28), channel_id=1, source_target_pairs={{0,16},{1,17},{2,18},{3,19},{4,20},{5,21},{6,22},{7,23},{8,24},{9,... | collective-permute-start | bytes 786440 | tf_op jit(solution)/shard_map/ppermute | solution.py:33
  149.4 13.1 %collective-permute-start.26 = (f32[64,512]{1,0:T(8,128)S(1)}, f32[64,512]{1,0:T(8,128)S(1)}, u32[]{:S(2)}, u32[]{:S(2)}) collective-permute-start(f32[64,512]{1,0:T(8,128)S(1)} %fusion), channel_id=1, source_target_pairs={{0,8},{1,9},{2,10},{3,11},{4,12},{5,13},{6,14},{7,15},{8,0},{9,1},... | collective-permute-start | bytes 393224 | tf_op jit(solution)/shard_map/ppermute | solution.py:33
  (17 other events, 159.1 us)

commit v6 on v4

--- a/solution.py
+++ b/solution.py
@@ -222,17 +222,21 @@
     )(where, skips, data, *tables())
 
 
-def columns_kernel(where, own, below, above, far, right):
+def columns_kernel(where, own, below, above, far_low, far_high, right):
     y, core = where[1], where[2]
     for j in range(2):
         from_x = where[4 + j]
-        for step, shard in ((0, own), (-1, below), (1, above), (2, far)):
+        for step in (0, -1, 1, 2):
             from_y = (y + step + 4) % 4
             base = 32 * (8 * (from_x // 2) + 2 * from_y)
             for rel in range(2):
                 row = pl.ds(pl.multiple_of(base + 32 * ((core + rel) % 2), 32), 32)
+                if step == 2:
+                    piece = (far_low, far_high)[rel].at[j, 0]
+                else:
+                    piece = {0: own, -1: below, 1: above}[step].at[j, rel]
                 for a in range(16):
-                    right[row, 128 * a : 128 * a + 128] = shard[j, rel, a]
+                    right[row, 128 * a : 128 * a + 128] = piece[a]
 
 
 def columns(where, *shards):
@@ -386,10 +390,11 @@
 
     near_up, near_down = along_y(near, 1), along_y(near, 3)
     (own,) = after([[same, opposite]], near_up, near_down)
-    near_far, own_down = along_y(near_up, 1), along_y(own, 3)
-    own_up, own_far = along_y(own, 1), along_y(own_down, 3)
-    right = columns(beside, near, near_up, near_down, near_far)
-    own_right = columns(across, own, own_up, own_down, own_far)
+    near_far = along_y(near_up[:, :1], 1), along_y(near_down[:, 1:], 3)
+    own_up, own_down = along_y(own, 1), along_y(own, 3)
+    own_far = along_y(own_up[:, :1], 1), along_y(own_down[:, 1:], 3)
+    right = columns(beside, near, near_up, near_down, *near_far)
+    own_right = columns(across, own, own_up, own_down, *own_far)
 
     early = [rows, ups[1], downs[1], ups[2], downs[2], ups[3], downs[3]]
     keep, send, left = gram_part(CHUNKS[0], where, [right], early, own_right)

time: 167 us -> 164 us (0.982)
  waiting for transfers between devices: 87.4 us -> 81.4 us
    ppermute x25 -> x27, waiting for transfers between devices: 65.4 us -> 59.4 us  [move(): return lax.ppermute(array, MESH, pairs)]
    slice x0 -> x4, local copies, waits for them, and re-layouts: none -> 2.18 us  [the longest x2 1.44 us: local(): own_far = (along_y(own_up[:, :1], 1), along_y(own_down[:, 1:], 3))]
    ppermute x25 -> x27, starting transfers between devices: 41.1 us -> 42 us  [move(): return lax.ppermute(array, MESH, pairs)]
    unnamed x26 -> x34, local copies, waits for them, and re-layouts: 3.48 us -> 2.74 us
  transfers between devices with their start and end apart: 26 -> 28, of which waited for: 11 -> 12; matrix products, arithmetic and copies ran while one was open for 1% -> 2% of each run, Pallas kernels for 5% -> 5%
where the time goes in v6:
time: 164 us; the launch traced here: 162 us
  waiting for transfers between devices  81.4 us (50%)
  starting transfers between devices  50.5 us (31%)
  Pallas kernels  23.8 us (15%)
  local copies, waits for them, and re-layouts  5.97 us (4%)
    ppermute x27, waiting for transfers between devices, move(): return lax.ppermute(array, MESH, pairs)  59.4 us
    ppermute x27, starting transfers between devices, move(): return lax.ppermute(array, MESH, pairs)  42 us
    all_to_all x1, waiting for transfers between devices, local(): lax.all_to_all(outgoing, 'seq', split_axis=0, concat_axis=0, tiled=True)  22 us
    all_to_all x1, starting transfers between devices, local(): lax.all_to_all(outgoing, 'seq', split_axis=0, concat_axis=0, tiled=True)  8.59 us
    pallas_call x2, Pallas kernels, gram_part(): pl.pallas_call(functools.partial(gram_kernel, steps, len(rights), len(ear...  6.62 us
    pallas_call x1, Pallas kernels, convolve(): pl.pallas_call(conv_kernel, in_specs=[SMEM, SMEM] + [VMEM] * 7, out_specs...  6.27 us
    pallas_call x1, Pallas kernels, prepare(): pl.pallas_call(prepare_kernel, grid=(4,), in_specs=[block] * 4, out_specs...  4.3 us
  transfers between devices with their start and end apart: 28, of which 12 were waited for; matrix products, arithmetic and copies ran while one was open for 2% of the time, Pallas kernels for 5%

profile of v6, /device:TPU:1, one launch (start us, length us, event | category | flops | bytes accessed | tf_op | source)
XLA Modules:
  0.0 162.4 jit_solution(3534749015676028920)
XLA Ops:
  0.0 4.3 %prepare.1 = bf16[16,96,512]{2,1,0:T(8,128)(2,1)} custom-call(bf16[512,512]{1,0:T(8,128)(2,1)} %gate.1, bf16[512,512]{1,0:T(8,128)(2,1)} %key.1, bf16[512,512]{1,0:T(8,128)(2,1)} %value.1, bf16[512,512]{1,0:T(8,128)(2,1)} %filt.1), custom_call_target="tpu_custom_call" | custom-call | tf_op jit(solution)/shard_map/prepare/pallas_call | solution.py:124
  4.3 8.6 %all-to-all-start = ((bf16[16,96,512]{2,1,0:T(8,128)(2,1)}), bf16[16,96,512]{2,1,0:T(8,128)(2,1)S(1)}, u32[]{:S(2)}, u32[]{:S(2)}) async-start(bf16[16,96,512]{2,1,0:T(8,128)(2,1)} %prepare.1), calls=%async_computation | async-start | bytes 3145728 | tf_op jit(solution)/shard_map/all_to_all | solution.py:371
  13.8 22.0 %all-to-all-done.data = bf16[16,96,512]{2,1,0:T(8,128)(2,1)S(1)} async-done(((bf16[16,96,512]{2,1,0:T(8,128)(2,1)}), bf16[16,96,512]{2,1,0:T(8,128)(2,1)S(1)}, u32[]{:S(2)}, u32[]{:S(2)}) %all-to-all-start) | async-done | bytes 1572896 | tf_op jit(solution)/shard_map/all_to_all | solution.py:371
  35.8 6.3 %convolve.1 = (bf16[16,32,128]{2,1,0:T(8,128)(2,1)S(1)}, bf16[16,32,128]{2,1,0:T(8,128)(2,1)S(1)}, bf16[2,16,32,128]{3,2,1,0:T(8,128)(2,1)S(1)}) custom-call(s32[6]{0:T(128)S(1)} %stack.57.where, f32[32]{0:T(128)S(1)} %dynamic_slice.3.skip, bf16[16,96,512]{2,1,0:T(8,128)(2,1)S(1)} %all-to-all-done.data, bf16[256,64]{1,0:T(8,128)(2,1)S(1)} %copy-done.13, ...), custom_call_target="tpu_custom_call" | custom-call | flops 4000000000 | bytes 3000000 | tf_op jit(solution)/shard_map/convolve/pallas_call | solution.py:211
  43.1 1.2 collective-permute-done
  45.1 1.7 %collective-permute-start.2 = (bf16[2,16,32,128]{3,2,1,0:T(8,128)(2,1)S(1)}, bf16[2,16,32,128]{3,2,1,0:T(8,128)(2,1)S(1)}, u32[]{:S(2)}, u32[]{:S(2)}) collective-permute-start(bf16[2,16,32,128]{3,2,1,0:T(8,128)(2,1)S(1)} %get-tuple-element.29), channel_id=1, source_target_pairs={{0,8},{1,9},{2,46},{3,47},{4,76},{5,77},{6,106},{7,107},{8,136},{9... | collective-permute-start | bytes 786440 | tf_op jit(solution)/shard_map/ppermute | solution.py:33
  46.7 3.0 %collective-permute-start.3 = (bf16[2,16,32,128]{3,2,1,0:T(8,128)(2,1)S(1)}, bf16[2,16,32,128]{3,2,1,0:T(8,128)(2,1)S(1)}, u32[]{:S(2)}, u32[]{:S(2)}) collective-permute-start(bf16[2,16,32,128]{3,2,1,0:T(8,128)(2,1)S(1)} %get-tuple-element.32), channel_id=1, source_target_pairs={{0,136},{1,137},{2,138},{3,139},{4,140},{5,141},{6,142},{7,143},{8... | collective-permute-start | bytes 786440 | tf_op jit(solution)/shard_map/ppermute | solution.py:33
  49.7 1.7 %collective-permute-start.5 = (bf16[2,16,32,128]{3,2,1,0:T(8,128)(2,1)S(1)}, bf16[2,16,32,128]{3,2,1,0:T(8,128)(2,1)S(1)}, u32[]{:S(2)}, u32[]{:S(2)}) collective-permute-start(bf16[2,16,32,128]{3,2,1,0:T(8,128)(2,1)S(1)} %get-tuple-element.31.refs_4_.refs_0_), channel_id=1, source_target_pairs={{0,128},{1,129},{2,130},{3,131},{4,132},{5,133},{6,134},{7,135},{8... | collective-permute-start | bytes 786440 | tf_op jit(solution)/shard_map/ppermute | solution.py:33
  51.4 20.8 %collective-permute-done.2.refs_1_ = bf16[2,16,32,128]{3,2,1,0:T(8,128)(2,1)S(1)} collective-permute-done((bf16[2,16,32,128]{3,2,1,0:T(8,128)(2,1)S(1)}, bf16[2,16,32,128]{3,2,1,0:T(8,128)(2,1)S(1)}, u32[]{:S(2)}, u32[]{:S(2)}) %collective-permute-start.2) | collective-permute-done | bytes 262176 | tf_op jit(solution)/shard_map/ppermute | solution.py:33
  72.3 1.7 %collective-permute-start.10 = (bf16[2,2,16,32,128]{4,3,2,1,0:T(8,128)(2,1)S(1)}, bf16[2,2,16,32,128]{4,3,2,1,0:T(8,128)(2,1)S(1)}, u32[]{:S(2)}, u32[]{:S(2)}) collective-permute-start(bf16[2,2,16,32,128]{4,3,2,1,0:T(8,128)(2,1)S(1)} %get-tuple-element.21.refs_1_), channel_id=1, source_target_pairs={{0,1},{1,2},{2,3},{3,4},{4,5},{5,6},{6,7},{7,0},{8,9},{9,10},{10,1... | collective-permute-start | bytes 1572872 | tf_op jit(solution)/shard_map/ppermute | solution.py:33
  74.1 8.3 %collective-permute-start.11 = (bf16[2,2,16,32,128]{4,3,2,1,0:T(8,128)(2,1)S(1)}, bf16[2,2,16,32,128]{4,3,2,1,0:T(8,128)(2,1)S(1)}, u32[]{:S(2)}, u32[]{:S(2)}) collective-permute-start(bf16[2,2,16,32,128]{4,3,2,1,0:T(8,128)(2,1)S(1)} %get-tuple-element.21.refs_1_), channel_id=1, source_target_pairs={{0,7},{1,0},{2,1},{3,2},{4,3},{5,4},{6,5},{7,6},{8,15},{9,8},{10,9... | collective-permute-start | bytes 1572872 | tf_op jit(solution)/shard_map/ppermute | solution.py:33
  82.4 2.7 %collective-permute-start.7 = (bf16[2,2,16,32,128]{4,3,2,1,0:T(8,128)(2,1)S(1)}, bf16[2,2,16,32,128]{4,3,2,1,0:T(8,128)(2,1)S(1)}, u32[]{:S(2)}, u32[]{:S(2)}) collective-permute-start(bf16[2,2,16,32,128]{4,3,2,1,0:T(8,128)(2,1)S(1)} %get-tuple-element.20.own), channel_id=1, source_target_pairs={{0,96},{1,97},{2,98},{3,99},{4,100},{5,101},{6,102},{7,103},{8,104... | collective-permute-start | bytes 1572872 | tf_op jit(solution)/shard_map/ppermute | solution.py:33
  85.9 7.5 %collective-permute-done.10.refs_2_ = bf16[2,2,16,32,128]{4,3,2,1,0:T(8,128)(2,1)S(1)} collective-permute-done((bf16[2,2,16,32,128]{4,3,2,1,0:T(8,128)(2,1)S(1)}, bf16[2,2,16,32,128]{4,3,2,1,0:T(8,128)(2,1)S(1)}, u32[]{:S(2)}, u32[]{:S(2)}) %collective-permute-start.10) | collective-permute-done | bytes 524320 | tf_op jit(solution)/shard_map/ppermute | solution.py:33
  93.4 2.7 %collective-permute-start.13 = (bf16[2,2,16,32,128]{4,3,2,1,0:T(8,128)(2,1)S(1)}, bf16[2,2,16,32,128]{4,3,2,1,0:T(8,128)(2,1)}, u32[]{:S(2)}, u32[]{:S(2)}) collective-permute-start(bf16[2,2,16,32,128]{4,3,2,1,0:T(8,128)(2,1)S(1)} %collective-permute-done.11.refs_3_), channel_id=1, source_target_pairs={{0,7},{1,0},{2,1},{3,2},{4,3},{5,4},{6,5},{7,6},{8,15},{9,8},{10,9... | collective-permute-start | bytes 1572872 | tf_op jit(solution)/shard_map/ppermute | solution.py:33
  96.2 2.7 %collective-permute-start.17 = (bf16[2,2,16,32,128]{4,3,2,1,0:T(8,128)(2,1)S(1)}, bf16[2,2,16,32,128]{4,3,2,1,0:T(8,128)(2,1)S(1)}, u32[]{:S(2)}, u32[]{:S(2)}) collective-permute-start(bf16[2,2,16,32,128]{4,3,2,1,0:T(8,128)(2,1)S(1)} %after.3.own), channel_id=1, source_target_pairs={{0,96},{1,97},{2,98},{3,99},{4,100},{5,101},{6,102},{7,103},{8,104... | collective-permute-start | bytes 1572872 | tf_op jit(solution)/shard_map/ppermute | solution.py:33
  99.0 7.3 %collective-permute-done.12.refs_4_ = bf16[2,2,16,32,128]{4,3,2,1,0:T(8,128)(2,1)} collective-permute-done((bf16[2,2,16,32,128]{4,3,2,1,0:T(8,128)(2,1)S(1)}, bf16[2,2,16,32,128]{4,3,2,1,0:T(8,128)(2,1)}, u32[]{:S(2)}, u32[]{:S(2)}) %collective-permute-start.12) | collective-permute-done | bytes 524320 | tf_op jit(solution)/shard_map/ppermute | solution.py:33
  106.3 2.7 %collective-permute-start.15 = (bf16[2,2,16,32,128]{4,3,2,1,0:T(8,128)(2,1)}, bf16[2,2,16,32,128]{4,3,2,1,0:T(8,128)(2,1)S(1)}, u32[]{:S(2)}, u32[]{:S(2)}) collective-permute-start(bf16[2,2,16,32,128]{4,3,2,1,0:T(8,128)(2,1)} %collective-permute-done.13.refs_5_), channel_id=1, source_target_pairs={{0,7},{1,0},{2,1},{3,2},{4,3},{5,4},{6,5},{7,6},{8,15},{9,8},{10,9... | collective-permute-start | bytes 1572872 | tf_op jit(solution)/shard_map/ppermute | solution.py:33
  114.1 1.1 collective-permute-start.19
  116.5 1.3 columns.2.refs_0_.refs_1_
  117.9 1.9 %collective-permute-done.18.far_low = bf16[2,1,16,32,128]{4,3,2,1,0:T(8,128)(2,1)} collective-permute-done((bf16[2,1,16,32,128]{4,3,2,1,0:T(8,128)(2,1)}, bf16[2,1,16,32,128]{4,3,2,1,0:T(8,128)(2,1)}, u32[]{:S(2)}, u32[]{:S(2)}) %collective-permute-start.18) | collective-permute-done | bytes 262176 | tf_op jit(solution)/shard_map/ppermute | solution.py:33
  119.8 2.0 %collective-permute-done.19.far_high = bf16[2,1,16,32,128]{4,3,2,1,0:T(8,128)(2,1)} collective-permute-done((bf16[2,1,16,32,128]{4,3,2,1,0:T(8,128)(2,1)}, bf16[2,1,16,32,128]{4,3,2,1,0:T(8,128)(2,1)}, u32[]{:S(2)}, u32[]{:S(2)}) %collective-permute-start.19) | collective-permute-done | bytes 262176 | tf_op jit(solution)/shard_map/ppermute | solution.py:33
  121.7 1.4 columns.3.refs_8_.right.refs_0_
  123.2 3.9 %gram_part.2 = (f32[1,448,512]{2,1,0:T(8,128)S(1)}, f32[1,448,512]{2,1,0:T(8,128)S(1)}, bf16[896,2048]{1,0:T(8,128)(2,1)S(1)}) custom-call(s32[6]{0:T(128)S(1)} %stack.57.where, bf16[512,2048]{1,0:T(8,128)(2,1)S(1)} %columns.2.refs_0_.refs_1_, bf16[2,2,16,32,128]{4,3,2,1,0:T(8,128)(2,1)S(1)} %copy-done.4, bf16[2,2,16,32,128]{4,3,2,1,0:T(8,128)(2,1)S(1)} %copy-done.6, ...), custom_call_target="tpu_custom_call" | custom-call | flops 1879048192 | bytes 4000000 | tf_op jit(solution)/shard_map/gram_part/pallas_call | solution.py:311
  127.2 4.3 %collective-permute-start.21 = (f32[1,448,512]{2,1,0:T(8,128)S(1)}, f32[1,448,512]{2,1,0:T(8,128)S(1)}, u32[]{:S(2)}, u32[]{:S(2)}) collective-permute-start(f32[1,448,512]{2,1,0:T(8,128)S(1)} %get-tuple-element.26), channel_id=1, source_target_pairs={{0,16},{1,17},{2,18},{3,19},{4,20},{5,21},{6,22},{7,23},{8,24},{9,... | collective-permute-start | bytes 2752520 | tf_op jit(solution)/shard_map/ppermute | solution.py:33
  131.4 2.1 %gram_again.1 = (f32[1,448,512]{2,1,0:T(8,128)S(1)}, f32[1,448,512]{2,1,0:T(8,128)S(1)}) custom-call(bf16[896,2048]{1,0:T(8,128)(2,1)S(1)} %get-tuple-element.22.left, bf16[512,2048]{1,0:T(8,128)(2,1)S(1)} %columns.3.refs_8_.right.refs_0_), custom_call_target="tpu_custom_call" | custom-call | flops 1879048192 | bytes 4000000 | tf_op jit(solution)/shard_map/gram_again/pallas_call | solution.py:295
  133.8 2.7 %collective-permute-start.24 = (bf16[1,2,16,32,128]{4,3,2,1,0:T(8,128)(2,1)S(1)}, bf16[1,2,16,32,128]{4,3,2,1,0:T(8,128)(2,1)S(1)}, u32[]{:S(2)}, u32[]{:S(2)}) collective-permute-start(bf16[1,2,16,32,128]{4,3,2,1,0:T(8,128)(2,1)S(1)} %slice.47), channel_id=1, source_target_pairs={{0,7},{1,0},{2,1},{3,2},{4,3},{5,4},{6,5},{7,6},{8,15},{9,8},{10,9... | collective-permute-start | bytes 786440 | tf_op jit(solution)/shard_map/ppermute | solution.py:33
  137.7 4.6 %collective-permute-done.23.refs_2_ = bf16[1,2,16,32,128]{4,3,2,1,0:T(8,128)(2,1)S(1)} collective-permute-done((bf16[1,2,16,32,128]{4,3,2,1,0:T(8,128)(2,1)S(1)}, bf16[1,2,16,32,128]{4,3,2,1,0:T(8,128)(2,1)S(1)}, u32[]{:S(2)}, u32[]{:S(2)}) %collective-permute-start.23) | collective-permute-done | bytes 262176 | tf_op jit(solution)/shard_map/ppermute | solution.py:33
  142.3 2.7 %gram_part.3 = (f32[2,64,512]{2,1,0:T(8,128)S(1)}, f32[2,64,512]{2,1,0:T(8,128)S(1)}, bf16[128,2048]{1,0:T(8,128)(2,1)}) custom-call(s32[6]{0:T(128)S(1)} %stack.57.where, bf16[512,2048]{1,0:T(8,128)(2,1)S(1)} %columns.3.refs_8_.right.refs_0_, bf16[512,2048]{1,0:T(8,128)(2,1)S(1)} %columns.2.refs_0_.refs_1_, ...), custom_call_target="tpu_custom_call" | custom-call | flops 536870912 | bytes 4000000 | tf_op jit(solution)/shard_map/gram_part/pallas_call | solution.py:311
  145.0 1.3 collective-permute-start.25
  146.4 1.2 collective-permute-done.25.refs_4_
  148.4 12.2 %collective-permute-done.26.refs_5_ = f32[64,512]{1,0:T(8,128)S(1)} collective-permute-done((f32[64,512]{1,0:T(8,128)S(1)}, f32[64,512]{1,0:T(8,128)S(1)}, u32[]{:S(2)}, u32[]{:S(2)}) %collective-permute-start.26) | collective-permute-done | bytes 131104 | tf_op jit(solution)/shard_map/ppermute | solution.py:33
  160.6 1.7 %finish.1 = f32[512,512]{1,0:T(8,128)} custom-call(s32[6]{0:T(128)S(1)} %stack.57.where, f32[512,512]{1,0:T(8,128)S(1)} %copy-done.2, f32[1,448,512]{2,1,0:T(8,128)S(1)} %get-tuple-element.23.refs_0_, f32[1,448,512]{2,1,0:T(8,128)S(1)} %collective-permute-done.20.refs_1_, f32[448,512]{1,0:T(8,128)S(1)} %collective-permute-done.22.refs_2_, ...), custom_call_target="tpu_custom_call" | custom-call | flops 1000000 | bytes 5000000 | tf_op jit(solution)/shard_map/finish/pallas_call | solution.py:346
  (82 shorter events, 12.5 us)
Async XLA Ops:
  4.3 31.5 %copy-start.11 = (bf16[256,256]{1,0:T(8,128)(2,1)S(1)}, bf16[256,256]{1,0:T(8,128)(2,1)}, u32[]{:S(2)}) copy-start(bf16[256,256]{1,0:T(8,128)(2,1)} %constant.116.fwd) | copy-start | bytes 393220
  4.3 31.5 %copy-start.12 = (bf16[256,256]{1,0:T(8,128)(2,1)S(1)}, bf16[256,256]{1,0:T(8,128)(2,1)}, u32[]{:S(2)}) copy-start(bf16[256,256]{1,0:T(8,128)(2,1)} %constant.117.bwd) | copy-start | bytes 393220
  4.3 31.5 %copy-start.13 = (bf16[256,64]{1,0:T(8,128)(2,1)S(1)}, bf16[256,64]{1,0:T(8,128)(2,1)}, u32[]{:S(2)}) copy-start(bf16[256,64]{1,0:T(8,128)(2,1)} %constant.114.first) | copy-start | bytes 98308
  4.3 31.5 %copy-start.14 = (f32[128,128]{1,0:T(8,128)S(1)}, f32[128,128]{1,0:T(8,128)}, u32[]{:S(2)}) copy-start(f32[128,128]{1,0:T(8,128)} %constant.112.clone.t_cos) | copy-start | bytes 196612
  4.3 31.4 %all-to-all-start = ((bf16[16,96,512]{2,1,0:T(8,128)(2,1)}), bf16[16,96,512]{2,1,0:T(8,128)(2,1)S(1)}, u32[]{:S(2)}, u32[]{:S(2)}) async-start(bf16[16,96,512]{2,1,0:T(8,128)(2,1)} %prepare.1), calls=%async_computation | async-start | bytes 3145728 | tf_op jit(solution)/shard_map/all_to_all | solution.py:371
  42.1 2.2 %collective-permute-start = (bf16[2,16,32,128]{3,2,1,0:T(8,128)(2,1)S(1)}, bf16[2,16,32,128]{3,2,1,0:T(8,128)(2,1)S(1)}, u32[]{:S(2)}, u32[]{:S(2)}) collective-permute-start(bf16[2,16,32,128]{3,2,1,0:T(8,128)(2,1)S(1)} %get-tuple-element.18), channel_id=1, source_target_pairs={{0,16},{1,17},{2,18},{3,19},{4,20},{5,21},{6,22},{7,23},{8,24},{9,... | collective-permute-start | bytes 786440 | tf_op jit(solution)/shard_map/ppermute | solution.py:33
  44.4 7.0 %collective-permute-start.1 = (bf16[2,16,32,128]{3,2,1,0:T(8,128)(2,1)S(1)}, bf16[2,16,32,128]{3,2,1,0:T(8,128)(2,1)S(1)}, u32[]{:S(2)}, u32[]{:S(2)}) collective-permute-start(bf16[2,16,32,128]{3,2,1,0:T(8,128)(2,1)S(1)} %get-tuple-element.30), channel_id=1, source_target_pairs={{0,0},{1,1},{2,38},{3,39},{4,68},{5,69},{6,98},{7,99},{8,128},{9,1... | collective-permute-start | bytes 786440 | tf_op jit(solution)/shard_map/ppermute | solution.py:33
  45.1 27.2 %collective-permute-start.2 = (bf16[2,16,32,128]{3,2,1,0:T(8,128)(2,1)S(1)}, bf16[2,16,32,128]{3,2,1,0:T(8,128)(2,1)S(1)}, u32[]{:S(2)}, u32[]{:S(2)}) collective-permute-start(bf16[2,16,32,128]{3,2,1,0:T(8,128)(2,1)S(1)} %get-tuple-element.29), channel_id=1, source_target_pairs={{0,8},{1,9},{2,46},{3,47},{4,76},{5,77},{6,106},{7,107},{8,136},{9... | collective-permute-start | bytes 786440 | tf_op jit(solution)/shard_map/ppermute | solution.py:33
  46.7 25.5 %collective-permute-start.3 = (bf16[2,16,32,128]{3,2,1,0:T(8,128)(2,1)S(1)}, bf16[2,16,32,128]{3,2,1,0:T(8,128)(2,1)S(1)}, u32[]{:S(2)}, u32[]{:S(2)}) collective-permute-start(bf16[2,16,32,128]{3,2,1,0:T(8,128)(2,1)S(1)} %get-tuple-element.32), channel_id=1, source_target_pairs={{0,136},{1,137},{2,138},{3,139},{4,140},{5,141},{6,142},{7,143},{8... | collective-permute-start | bytes 786440 | tf_op jit(solution)/shard_map/ppermute | solution.py:33
  49.7 22.6 %collective-permute-start.4 = (bf16[2,16,32,128]{3,2,1,0:T(8,128)(2,1)S(1)}, bf16[2,16,32,128]{3,2,1,0:T(8,128)(2,1)S(1)}, u32[]{:S(2)}, u32[]{:S(2)}) collective-permute-start(bf16[2,16,32,128]{3,2,1,0:T(8,128)(2,1)S(1)} %get-tuple-element.32), channel_id=1, source_target_pairs={{0,8},{1,9},{2,10},{3,11},{4,12},{5,13},{6,14},{7,15},{8,128},{9,1... | collective-permute-start | bytes 786440 | tf_op jit(solution)/shard_map/ppermute | solution.py:33
  49.7 22.6 %collective-permute-start.5 = (bf16[2,16,32,128]{3,2,1,0:T(8,128)(2,1)S(1)}, bf16[2,16,32,128]{3,2,1,0:T(8,128)(2,1)S(1)}, u32[]{:S(2)}, u32[]{:S(2)}) collective-permute-start(bf16[2,16,32,128]{3,2,1,0:T(8,128)(2,1)S(1)} %get-tuple-element.31.refs_4_.refs_0_), channel_id=1, source_target_pairs={{0,128},{1,129},{2,130},{3,131},{4,132},{5,133},{6,134},{7,135},{8... | collective-permute-start | bytes 786440 | tf_op jit(solution)/shard_map/ppermute | solution.py:33
  72.3 21.0 %collective-permute-start.10 = (bf16[2,2,16,32,128]{4,3,2,1,0:T(8,128)(2,1)S(1)}, bf16[2,2,16,32,128]{4,3,2,1,0:T(8,128)(2,1)S(1)}, u32[]{:S(2)}, u32[]{:S(2)}) collective-permute-start(bf16[2,2,16,32,128]{4,3,2,1,0:T(8,128)(2,1)S(1)} %get-tuple-element.21.refs_1_), channel_id=1, source_target_pairs={{0,1},{1,2},{2,3},{3,4},{4,5},{5,6},{6,7},{7,0},{8,9},{9,10},{10,1... | collective-permute-start | bytes 1572872 | tf_op jit(solution)/shard_map/ppermute | solution.py:33
  74.1 19.3 %collective-permute-start.11 = (bf16[2,2,16,32,128]{4,3,2,1,0:T(8,128)(2,1)S(1)}, bf16[2,2,16,32,128]{4,3,2,1,0:T(8,128)(2,1)S(1)}, u32[]{:S(2)}, u32[]{:S(2)}) collective-permute-start(bf16[2,2,16,32,128]{4,3,2,1,0:T(8,128)(2,1)S(1)} %get-tuple-element.21.refs_1_), channel_id=1, source_target_pairs={{0,7},{1,0},{2,1},{3,2},{4,3},{5,4},{6,5},{7,6},{8,15},{9,8},{10,9... | collective-permute-start | bytes 1572872 | tf_op jit(solution)/shard_map/ppermute | solution.py:33
  82.4 13.7 %collective-permute-start.6 = (bf16[2,2,16,32,128]{4,3,2,1,0:T(8,128)(2,1)S(1)}, bf16[2,2,16,32,128]{4,3,2,1,0:T(8,128)(2,1)S(1)}, u32[]{:S(2)}, u32[]{:S(2)}) collective-permute-start(bf16[2,2,16,32,128]{4,3,2,1,0:T(8,128)(2,1)S(1)} %get-tuple-element.20.own), channel_id=1, source_target_pairs={{0,32},{1,33},{2,34},{3,35},{4,36},{5,37},{6,38},{7,39},{8,40},{9,... | collective-permute-start | bytes 1572872 | tf_op jit(solution)/shard_map/ppermute | solution.py:33
  82.4 13.7 %collective-permute-start.7 = (bf16[2,2,16,32,128]{4,3,2,1,0:T(8,128)(2,1)S(1)}, bf16[2,2,16,32,128]{4,3,2,1,0:T(8,128)(2,1)S(1)}, u32[]{:S(2)}, u32[]{:S(2)}) collective-permute-start(bf16[2,2,16,32,128]{4,3,2,1,0:T(8,128)(2,1)S(1)} %get-tuple-element.20.own), channel_id=1, source_target_pairs={{0,96},{1,97},{2,98},{3,99},{4,100},{5,101},{6,102},{7,103},{8,104... | collective-permute-start | bytes 1572872 | tf_op jit(solution)/shard_map/ppermute | solution.py:33
  93.4 12.9 %collective-permute-start.12 = (bf16[2,2,16,32,128]{4,3,2,1,0:T(8,128)(2,1)S(1)}, bf16[2,2,16,32,128]{4,3,2,1,0:T(8,128)(2,1)}, u32[]{:S(2)}, u32[]{:S(2)}) collective-permute-start(bf16[2,2,16,32,128]{4,3,2,1,0:T(8,128)(2,1)S(1)} %collective-permute-done.10.refs_2_), channel_id=1, source_target_pairs={{0,1},{1,2},{2,3},{3,4},{4,5},{5,6},{6,7},{7,0},{8,9},{9,10},{10,1... | collective-permute-start | bytes 1572872 | tf_op jit(solution)/shard_map/ppermute | solution.py:33
  93.4 12.9 %collective-permute-start.13 = (bf16[2,2,16,32,128]{4,3,2,1,0:T(8,128)(2,1)S(1)}, bf16[2,2,16,32,128]{4,3,2,1,0:T(8,128)(2,1)}, u32[]{:S(2)}, u32[]{:S(2)}) collective-permute-start(bf16[2,2,16,32,128]{4,3,2,1,0:T(8,128)(2,1)S(1)} %collective-permute-done.11.refs_3_), channel_id=1, source_target_pairs={{0,7},{1,0},{2,1},{3,2},{4,3},{5,4},{6,5},{7,6},{8,15},{9,8},{10,9... | collective-permute-start | bytes 1572872 | tf_op jit(solution)/shard_map/ppermute | solution.py:33
  96.1 13.6 %collective-permute-start.16 = (bf16[2,2,16,32,128]{4,3,2,1,0:T(8,128)(2,1)S(1)}, bf16[2,2,16,32,128]{4,3,2,1,0:T(8,128)(2,1)S(1)}, u32[]{:S(2)}, u32[]{:S(2)}) collective-permute-start(bf16[2,2,16,32,128]{4,3,2,1,0:T(8,128)(2,1)S(1)} %after.3.own), channel_id=1, source_target_pairs={{0,32},{1,33},{2,34},{3,35},{4,36},{5,37},{6,38},{7,39},{8,40},{9,... | collective-permute-start | bytes 1572872 | tf_op jit(solution)/shard_map/ppermute | solution.py:33
  96.2 14.8 %collective-permute-start.17 = (bf16[2,2,16,32,128]{4,3,2,1,0:T(8,128)(2,1)S(1)}, bf16[2,2,16,32,128]{4,3,2,1,0:T(8,128)(2,1)S(1)}, u32[]{:S(2)}, u32[]{:S(2)}) collective-permute-start(bf16[2,2,16,32,128]{4,3,2,1,0:T(8,128)(2,1)S(1)} %after.3.own), channel_id=1, source_target_pairs={{0,96},{1,97},{2,98},{3,99},{4,100},{5,101},{6,102},{7,103},{8,104... | collective-permute-start | bytes 1572872 | tf_op jit(solution)/shard_map/ppermute | solution.py:33
  98.9 15.2 %collective-permute-start.8 = (bf16[2,1,16,32,128]{4,3,2,1,0:T(8,128)(2,1)S(1)}, bf16[2,1,16,32,128]{4,3,2,1,0:T(8,128)(2,1)S(1)}, u32[]{:S(2)}, u32[]{:S(2)}) collective-permute-start(bf16[2,1,16,32,128]{4,3,2,1,0:T(8,128)(2,1)S(1)} %slice.42), channel_id=1, source_target_pairs={{0,32},{1,33},{2,34},{3,35},{4,36},{5,37},{6,38},{7,39},{8,40},{9,... | collective-permute-start | bytes 786440 | tf_op jit(solution)/shard_map/ppermute | solution.py:33
  106.3 16.9 %collective-permute-start.14 = (bf16[2,2,16,32,128]{4,3,2,1,0:T(8,128)(2,1)}, bf16[2,2,16,32,128]{4,3,2,1,0:T(8,128)(2,1)S(1)}, u32[]{:S(2)}, u32[]{:S(2)}) collective-permute-start(bf16[2,2,16,32,128]{4,3,2,1,0:T(8,128)(2,1)} %collective-permute-done.12.refs_4_), channel_id=1, source_target_pairs={{0,1},{1,2},{2,3},{3,4},{4,5},{5,6},{6,7},{7,0},{8,9},{9,10},{10,1... | collective-permute-start | bytes 1572872 | tf_op jit(solution)/shard_map/ppermute | solution.py:33
  106.3 16.9 %collective-permute-start.15 = (bf16[2,2,16,32,128]{4,3,2,1,0:T(8,128)(2,1)}, bf16[2,2,16,32,128]{4,3,2,1,0:T(8,128)(2,1)S(1)}, u32[]{:S(2)}, u32[]{:S(2)}) collective-permute-start(bf16[2,2,16,32,128]{4,3,2,1,0:T(8,128)(2,1)} %collective-permute-done.13.refs_5_), channel_id=1, source_target_pairs={{0,7},{1,0},{2,1},{3,2},{4,3},{5,4},{6,5},{7,6},{8,15},{9,8},{10,9... | collective-permute-start | bytes 1572872 | tf_op jit(solution)/shard_map/ppermute | solution.py:33
  109.7 5.7 %collective-permute-start.9 = (bf16[2,1,16,32,128]{4,3,2,1,0:T(8,128)(2,1)}, bf16[2,1,16,32,128]{4,3,2,1,0:T(8,128)(2,1)}, u32[]{:S(2)}, u32[]{:S(2)}) collective-permute-start(bf16[2,1,16,32,128]{4,3,2,1,0:T(8,128)(2,1)} %slice.43), channel_id=1, source_target_pairs={{0,96},{1,97},{2,98},{3,99},{4,100},{5,101},{6,102},{7,103},{8,104... | collective-permute-start | bytes 786440 | tf_op jit(solution)/shard_map/ppermute | solution.py:33
  111.0 8.8 %collective-permute-start.18 = (bf16[2,1,16,32,128]{4,3,2,1,0:T(8,128)(2,1)}, bf16[2,1,16,32,128]{4,3,2,1,0:T(8,128)(2,1)}, u32[]{:S(2)}, u32[]{:S(2)}) collective-permute-start(bf16[2,1,16,32,128]{4,3,2,1,0:T(8,128)(2,1)} %slice.44), channel_id=1, source_target_pairs={{0,32},{1,33},{2,34},{3,35},{4,36},{5,37},{6,38},{7,39},{8,40},{9,... | collective-permute-start | bytes 786440 | tf_op jit(solution)/shard_map/ppermute | solution.py:33
  114.1 7.7 %collective-permute-start.19 = (bf16[2,1,16,32,128]{4,3,2,1,0:T(8,128)(2,1)}, bf16[2,1,16,32,128]{4,3,2,1,0:T(8,128)(2,1)}, u32[]{:S(2)}, u32[]{:S(2)}) collective-permute-start(bf16[2,1,16,32,128]{4,3,2,1,0:T(8,128)(2,1)} %slice.45), channel_id=1, source_target_pairs={{0,96},{1,97},{2,98},{3,99},{4,100},{5,101},{6,102},{7,103},{8,104... | collective-permute-start | bytes 786440 | tf_op jit(solution)/shard_map/ppermute | solution.py:33
  127.2 9.4 %collective-permute-start.21 = (f32[1,448,512]{2,1,0:T(8,128)S(1)}, f32[1,448,512]{2,1,0:T(8,128)S(1)}, u32[]{:S(2)}, u32[]{:S(2)}) collective-permute-start(f32[1,448,512]{2,1,0:T(8,128)S(1)} %get-tuple-element.26), channel_id=1, source_target_pairs={{0,16},{1,17},{2,18},{3,19},{4,20},{5,21},{6,22},{7,23},{8,24},{9,... | collective-permute-start | bytes 2752520 | tf_op jit(solution)/shard_map/ppermute | solution.py:33
  133.5 27.1 %collective-permute-start.20 = (f32[1,448,512]{2,1,0:T(8,128)S(1)}, f32[1,448,512]{2,1,0:T(8,128)S(1)}, u32[]{:S(2)}, u32[]{:S(2)}) collective-permute-start(f32[1,448,512]{2,1,0:T(8,128)S(1)} %get-tuple-element.24), channel_id=1, source_target_pairs={{0,16},{1,17},{2,18},{3,19},{4,20},{5,21},{6,22},{7,23},{8,24},{9,... | collective-permute-start | bytes 2752520 | tf_op jit(solution)/shard_map/ppermute | solution.py:33
  133.7 8.7 %collective-permute-start.23 = (bf16[1,2,16,32,128]{4,3,2,1,0:T(8,128)(2,1)S(1)}, bf16[1,2,16,32,128]{4,3,2,1,0:T(8,128)(2,1)S(1)}, u32[]{:S(2)}, u32[]{:S(2)}) collective-permute-start(bf16[1,2,16,32,128]{4,3,2,1,0:T(8,128)(2,1)S(1)} %slice.46), channel_id=1, source_target_pairs={{0,1},{1,2},{2,3},{3,4},{4,5},{5,6},{6,7},{7,0},{8,9},{9,10},{10,1... | collective-permute-start | bytes 786440 | tf_op jit(solution)/shard_map/ppermute | solution.py:33
  133.8 8.6 %collective-permute-start.24 = (bf16[1,2,16,32,128]{4,3,2,1,0:T(8,128)(2,1)S(1)}, bf16[1,2,16,32,128]{4,3,2,1,0:T(8,128)(2,1)S(1)}, u32[]{:S(2)}, u32[]{:S(2)}) collective-permute-start(bf16[1,2,16,32,128]{4,3,2,1,0:T(8,128)(2,1)S(1)} %slice.47), channel_id=1, source_target_pairs={{0,7},{1,0},{2,1},{3,2},{4,3},{5,4},{6,5},{7,6},{8,15},{9,8},{10,9... | collective-permute-start | bytes 786440 | tf_op jit(solution)/shard_map/ppermute | solution.py:33
  136.7 23.9 %collective-permute-start.22 = (f32[448,512]{1,0:T(8,128)S(1)}, f32[448,512]{1,0:T(8,128)S(1)}, u32[]{:S(2)}, u32[]{:S(2)}) collective-permute-start(f32[448,512]{1,0:T(8,128)S(1)} %add_bitcast_fusion), channel_id=1, source_target_pairs={{0,8},{1,9},{2,10},{3,11},{4,12},{5,13},{6,14},{7,15},{8,0},{9,1},... | collective-permute-start | bytes 2752520 | tf_op jit(solution)/shard_map/ppermute | solution.py:33
  145.0 2.5 %collective-permute-start.25 = (f32[2,64,512]{2,1,0:T(8,128)S(1)}, f32[2,64,512]{2,1,0:T(8,128)S(1)}, u32[]{:S(2)}, u32[]{:S(2)}) collective-permute-start(f32[2,64,512]{2,1,0:T(8,128)S(1)} %get-tuple-element.28), channel_id=1, source_target_pairs={{0,16},{1,17},{2,18},{3,19},{4,20},{5,21},{6,22},{7,23},{8,24},{9,... | collective-permute-start | bytes 786440 | tf_op jit(solution)/shard_map/ppermute | solution.py:33
  147.5 13.1 %collective-permute-start.26 = (f32[64,512]{1,0:T(8,128)S(1)}, f32[64,512]{1,0:T(8,128)S(1)}, u32[]{:S(2)}, u32[]{:S(2)}) collective-permute-start(f32[64,512]{1,0:T(8,128)S(1)} %fusion), channel_id=1, source_target_pairs={{0,8},{1,9},{2,10},{3,11},{4,12},{5,13},{6,14},{7,15},{8,0},{9,1},... | collective-permute-start | bytes 393224 | tf_op jit(solution)/shard_map/ppermute | solution.py:33
  (13 other events, 154.3 us)

commit v7 on v6

--- a/solution.py
+++ b/solution.py
@@ -381,7 +381,8 @@
     above = along_x(other, 3)
     opposite = along_x(same, 2)
 
-    rows, near = after([[row_a, row_b], [above, below]], same, opposite)
+    (rows,) = after([[row_a, row_b]])
+    (near,) = after([[above, below]], same)
     ups, downs = [rows], [rows]
     for _ in range(3):
         ups.append(along_z(ups[-1], 1))

time: 164 us -> 164 us (level)
    unnamed x34 -> x30, local copies, waits for them, and re-layouts: 2.74 us -> 0.86 us
  transfers between devices with their start and end apart: 28 -> 28, of which waited for: 12 -> 11; matrix products, arithmetic and copies ran while one was open for 2% -> 3% of each run, Pallas kernels for 5% -> 5%
where the time goes in v7:
time: 164 us; the launch traced here: 163 us
  waiting for transfers between devices  82.3 us (50%)
  starting transfers between devices  50.9 us (31%)
  Pallas kernels  24.1 us (15%)
  local copies, waits for them, and re-layouts  5.04 us (3%)
    ppermute x27, waiting for transfers between devices, move(): return lax.ppermute(array, MESH, pairs)  60.3 us
    ppermute x27, starting transfers between devices, move(): return lax.ppermute(array, MESH, pairs)  42.3 us
    all_to_all x1, waiting for transfers between devices, local(): lax.all_to_all(outgoing, 'seq', split_axis=0, concat_axis=0, tiled=True)  22 us
    all_to_all x1, starting transfers between devices, local(): lax.all_to_all(outgoing, 'seq', split_axis=0, concat_axis=0, tiled=True)  8.59 us
    pallas_call x2, Pallas kernels, gram_part(): pl.pallas_call(functools.partial(gram_kernel, steps, len(rights), len(ear...  6.77 us
    pallas_call x1, Pallas kernels, convolve(): pl.pallas_call(conv_kernel, in_specs=[SMEM, SMEM] + [VMEM] * 7, out_specs...  6.25 us
    pallas_call x1, Pallas kernels, prepare(): pl.pallas_call(prepare_kernel, grid=(4,), in_specs=[block] * 4, out_specs...  4.26 us
  transfers between devices with their start and end apart: 28, of which 11 were waited for; matrix products, arithmetic and copies ran while one was open for 3% of the time, Pallas kernels for 5%

profile of v7, /device:TPU:1, one launch (start us, length us, event | category | flops | bytes accessed | tf_op | source)
XLA Modules:
  0.0 162.9 jit_solution(6535572921727088649)
XLA Ops:
  0.0 4.3 %prepare.1 = bf16[16,96,512]{2,1,0:T(8,128)(2,1)} custom-call(bf16[512,512]{1,0:T(8,128)(2,1)} %gate.1, bf16[512,512]{1,0:T(8,128)(2,1)} %key.1, bf16[512,512]{1,0:T(8,128)(2,1)} %value.1, bf16[512,512]{1,0:T(8,128)(2,1)} %filt.1), custom_call_target="tpu_custom_call" | custom-call | tf_op jit(solution)/shard_map/prepare/pallas_call | solution.py:124
  4.3 8.6 %all-to-all-start = ((bf16[16,96,512]{2,1,0:T(8,128)(2,1)}), bf16[16,96,512]{2,1,0:T(8,128)(2,1)S(1)}, u32[]{:S(2)}, u32[]{:S(2)}) async-start(bf16[16,96,512]{2,1,0:T(8,128)(2,1)} %prepare.1), calls=%async_computation | async-start | bytes 3145728 | tf_op jit(solution)/shard_map/all_to_all | solution.py:371
  13.7 22.0 %all-to-all-done.data = bf16[16,96,512]{2,1,0:T(8,128)(2,1)S(1)} async-done(((bf16[16,96,512]{2,1,0:T(8,128)(2,1)}), bf16[16,96,512]{2,1,0:T(8,128)(2,1)S(1)}, u32[]{:S(2)}, u32[]{:S(2)}) %all-to-all-start) | async-done | bytes 1572896 | tf_op jit(solution)/shard_map/all_to_all | solution.py:371
  35.8 6.3 %convolve.1 = (bf16[16,32,128]{2,1,0:T(8,128)(2,1)S(1)}, bf16[16,32,128]{2,1,0:T(8,128)(2,1)S(1)}, bf16[2,16,32,128]{3,2,1,0:T(8,128)(2,1)S(1)}) custom-call(s32[6]{0:T(128)S(1)} %stack.57.where, f32[32]{0:T(128)S(1)} %dynamic_slice.3.skip, bf16[16,96,512]{2,1,0:T(8,128)(2,1)S(1)} %all-to-all-done.data, bf16[256,64]{1,0:T(8,128)(2,1)S(1)} %copy-done.11, ...), custom_call_target="tpu_custom_call" | custom-call | flops 4000000000 | bytes 3000000 | tf_op jit(solution)/shard_map/convolve/pallas_call | solution.py:211
  45.0 1.7 %collective-permute-start.8 = (bf16[2,16,32,128]{3,2,1,0:T(8,128)(2,1)S(1)}, bf16[2,16,32,128]{3,2,1,0:T(8,128)(2,1)S(1)}, u32[]{:S(2)}, u32[]{:S(2)}) collective-permute-start(bf16[2,16,32,128]{3,2,1,0:T(8,128)(2,1)S(1)} %get-tuple-element.25), channel_id=1, source_target_pairs={{0,8},{1,9},{2,46},{3,47},{4,76},{5,77},{6,106},{7,107},{8,136},{9... | collective-permute-start | bytes 786440 | tf_op jit(solution)/shard_map/ppermute | solution.py:33
  46.7 3.0 %collective-permute-start.1 = (bf16[2,16,32,128]{3,2,1,0:T(8,128)(2,1)S(1)}, bf16[2,16,32,128]{3,2,1,0:T(8,128)(2,1)S(1)}, u32[]{:S(2)}, u32[]{:S(2)}) collective-permute-start(bf16[2,16,32,128]{3,2,1,0:T(8,128)(2,1)S(1)} %get-tuple-element.27), channel_id=1, source_target_pairs={{0,136},{1,137},{2,138},{3,139},{4,140},{5,141},{6,142},{7,143},{8... | collective-permute-start | bytes 786440 | tf_op jit(solution)/shard_map/ppermute | solution.py:33
  49.7 22.6 %collective-permute-done.8.refs_1_ = bf16[2,16,32,128]{3,2,1,0:T(8,128)(2,1)S(1)} collective-permute-done((bf16[2,16,32,128]{3,2,1,0:T(8,128)(2,1)S(1)}, bf16[2,16,32,128]{3,2,1,0:T(8,128)(2,1)S(1)}, u32[]{:S(2)}, u32[]{:S(2)}) %collective-permute-start.8) | collective-permute-done | bytes 262176 | tf_op jit(solution)/shard_map/ppermute | solution.py:33
  72.3 1.7 %collective-permute-start.9 = (bf16[2,2,16,32,128]{4,3,2,1,0:T(8,128)(2,1)S(1)}, bf16[2,2,16,32,128]{4,3,2,1,0:T(8,128)(2,1)S(1)}, u32[]{:S(2)}, u32[]{:S(2)}) collective-permute-start(bf16[2,2,16,32,128]{4,3,2,1,0:T(8,128)(2,1)S(1)} %after.4.refs_1_), channel_id=1, source_target_pairs={{0,1},{1,2},{2,3},{3,4},{4,5},{5,6},{6,7},{7,0},{8,9},{9,10},{10,1... | collective-permute-start | bytes 1572872 | tf_op jit(solution)/shard_map/ppermute | solution.py:33
  74.0 7.3 %collective-permute-start.10 = (bf16[2,2,16,32,128]{4,3,2,1,0:T(8,128)(2,1)S(1)}, bf16[2,2,16,32,128]{4,3,2,1,0:T(8,128)(2,1)S(1)}, u32[]{:S(2)}, u32[]{:S(2)}) collective-permute-start(bf16[2,2,16,32,128]{4,3,2,1,0:T(8,128)(2,1)S(1)} %after.4.refs_1_), channel_id=1, source_target_pairs={{0,7},{1,0},{2,1},{3,2},{4,3},{5,4},{6,5},{7,6},{8,15},{9,8},{10,9... | collective-permute-start | bytes 1572872 | tf_op jit(solution)/shard_map/ppermute | solution.py:33
  81.4 2.7 %collective-permute-start.4 = (bf16[2,2,16,32,128]{4,3,2,1,0:T(8,128)(2,1)S(1)}, bf16[2,2,16,32,128]{4,3,2,1,0:T(8,128)(2,1)S(1)}, u32[]{:S(2)}, u32[]{:S(2)}) collective-permute-start(bf16[2,2,16,32,128]{4,3,2,1,0:T(8,128)(2,1)S(1)} %after.3.own), channel_id=1, source_target_pairs={{0,96},{1,97},{2,98},{3,99},{4,100},{5,101},{6,102},{7,103},{8,104... | collective-permute-start | bytes 1572872 | tf_op jit(solution)/shard_map/ppermute | solution.py:33
  84.7 7.5 %collective-permute-done.9.refs_2_ = bf16[2,2,16,32,128]{4,3,2,1,0:T(8,128)(2,1)S(1)} collective-permute-done((bf16[2,2,16,32,128]{4,3,2,1,0:T(8,128)(2,1)S(1)}, bf16[2,2,16,32,128]{4,3,2,1,0:T(8,128)(2,1)S(1)}, u32[]{:S(2)}, u32[]{:S(2)}) %collective-permute-start.9) | collective-permute-done | bytes 524320 | tf_op jit(solution)/shard_map/ppermute | solution.py:33
  92.3 2.7 %collective-permute-start.12 = (bf16[2,2,16,32,128]{4,3,2,1,0:T(8,128)(2,1)S(1)}, bf16[2,2,16,32,128]{4,3,2,1,0:T(8,128)(2,1)}, u32[]{:S(2)}, u32[]{:S(2)}) collective-permute-start(bf16[2,2,16,32,128]{4,3,2,1,0:T(8,128)(2,1)S(1)} %collective-permute-done.10.refs_3_), channel_id=1, source_target_pairs={{0,7},{1,0},{2,1},{3,2},{4,3},{5,4},{6,5},{7,6},{8,15},{9,8},{10,9... | collective-permute-start | bytes 1572872 | tf_op jit(solution)/shard_map/ppermute | solution.py:33
  95.1 2.7 %collective-permute-start.17 = (bf16[2,2,16,32,128]{4,3,2,1,0:T(8,128)(2,1)S(1)}, bf16[2,2,16,32,128]{4,3,2,1,0:T(8,128)(2,1)S(1)}, u32[]{:S(2)}, u32[]{:S(2)}) collective-permute-start(bf16[2,2,16,32,128]{4,3,2,1,0:T(8,128)(2,1)S(1)} %after.5.own), channel_id=1, source_target_pairs={{0,96},{1,97},{2,98},{3,99},{4,100},{5,101},{6,102},{7,103},{8,104... | collective-permute-start | bytes 1572872 | tf_op jit(solution)/shard_map/ppermute | solution.py:33
  97.9 7.3 %collective-permute-done.11.refs_4_ = bf16[2,2,16,32,128]{4,3,2,1,0:T(8,128)(2,1)} collective-permute-done((bf16[2,2,16,32,128]{4,3,2,1,0:T(8,128)(2,1)S(1)}, bf16[2,2,16,32,128]{4,3,2,1,0:T(8,128)(2,1)}, u32[]{:S(2)}, u32[]{:S(2)}) %collective-permute-start.11) | collective-permute-done | bytes 524320 | tf_op jit(solution)/shard_map/ppermute | solution.py:33
  105.2 2.7 %collective-permute-start.14 = (bf16[2,2,16,32,128]{4,3,2,1,0:T(8,128)(2,1)}, bf16[2,2,16,32,128]{4,3,2,1,0:T(8,128)(2,1)}, u32[]{:S(2)}, u32[]{:S(2)}) collective-permute-start(bf16[2,2,16,32,128]{4,3,2,1,0:T(8,128)(2,1)} %collective-permute-done.12.refs_5_), channel_id=1, source_target_pairs={{0,7},{1,0},{2,1},{3,2},{4,3},{5,4},{6,5},{7,6},{8,15},{9,8},{10,9... | collective-permute-start | bytes 1572872 | tf_op jit(solution)/shard_map/ppermute | solution.py:33
  112.9 1.3 collective-permute-start.19
  114.4 1.4 columns.2.refs_0_.refs_1_
  115.8 2.8 %collective-permute-done.18.far_low = bf16[2,1,16,32,128]{4,3,2,1,0:T(8,128)(2,1)} collective-permute-done((bf16[2,1,16,32,128]{4,3,2,1,0:T(8,128)(2,1)}, bf16[2,1,16,32,128]{4,3,2,1,0:T(8,128)(2,1)}, u32[]{:S(2)}, u32[]{:S(2)}) %collective-permute-start.18) | collective-permute-done | bytes 262176 | tf_op jit(solution)/shard_map/ppermute | solution.py:33
  118.6 2.0 %collective-permute-done.19.far_high = bf16[2,1,16,32,128]{4,3,2,1,0:T(8,128)(2,1)} collective-permute-done((bf16[2,1,16,32,128]{4,3,2,1,0:T(8,128)(2,1)}, bf16[2,1,16,32,128]{4,3,2,1,0:T(8,128)(2,1)}, u32[]{:S(2)}, u32[]{:S(2)}) %collective-permute-start.19) | collective-permute-done | bytes 262176 | tf_op jit(solution)/shard_map/ppermute | solution.py:33
  120.6 1.4 columns.3.refs_8_.right.refs_0_
  122.1 4.1 %gram_part.2 = (f32[1,448,512]{2,1,0:T(8,128)S(1)}, f32[1,448,512]{2,1,0:T(8,128)S(1)}, bf16[896,2048]{1,0:T(8,128)(2,1)S(1)}) custom-call(s32[6]{0:T(128)S(1)} %stack.57.where, bf16[512,2048]{1,0:T(8,128)(2,1)S(1)} %columns.2.refs_0_.refs_1_, bf16[2,2,16,32,128]{4,3,2,1,0:T(8,128)(2,1)S(1)} %after.4.refs_1_, bf16[2,2,16,32,128]{4,3,2,1,0:T(8,128)(2,1)S(1)} %copy-done.6, ...), custom_call_target="tpu_custom_call" | custom-call | flops 1879048192 | bytes 4000000 | tf_op jit(solution)/shard_map/gram_part/pallas_call | solution.py:311
  126.2 4.2 %collective-permute-start.21 = (f32[1,448,512]{2,1,0:T(8,128)S(1)}, f32[1,448,512]{2,1,0:T(8,128)S(1)}, u32[]{:S(2)}, u32[]{:S(2)}) collective-permute-start(f32[1,448,512]{2,1,0:T(8,128)S(1)} %get-tuple-element.22), channel_id=1, source_target_pairs={{0,16},{1,17},{2,18},{3,19},{4,20},{5,21},{6,22},{7,23},{8,24},{9,... | collective-permute-start | bytes 2752520 | tf_op jit(solution)/shard_map/ppermute | solution.py:33
  130.4 2.1 %gram_again.1 = (f32[1,448,512]{2,1,0:T(8,128)S(1)}, f32[1,448,512]{2,1,0:T(8,128)S(1)}) custom-call(bf16[896,2048]{1,0:T(8,128)(2,1)S(1)} %get-tuple-element.18.left, bf16[512,2048]{1,0:T(8,128)(2,1)S(1)} %columns.3.refs_8_.right.refs_0_), custom_call_target="tpu_custom_call" | custom-call | flops 1879048192 | bytes 4000000 | tf_op jit(solution)/shard_map/gram_again/pallas_call | solution.py:295
  133.7 2.7 %collective-permute-start.24 = (bf16[1,2,16,32,128]{4,3,2,1,0:T(8,128)(2,1)S(1)}, bf16[1,2,16,32,128]{4,3,2,1,0:T(8,128)(2,1)S(1)}, u32[]{:S(2)}, u32[]{:S(2)}) collective-permute-start(bf16[1,2,16,32,128]{4,3,2,1,0:T(8,128)(2,1)S(1)} %slice.47), channel_id=1, source_target_pairs={{0,7},{1,0},{2,1},{3,2},{4,3},{5,4},{6,5},{7,6},{8,15},{9,8},{10,9... | collective-permute-start | bytes 786440 | tf_op jit(solution)/shard_map/ppermute | solution.py:33
  136.6 2.0 %collective-permute-start.22 = (f32[448,512]{1,0:T(8,128)S(1)}, f32[448,512]{1,0:T(8,128)S(1)}, u32[]{:S(2)}, u32[]{:S(2)}) collective-permute-start(f32[448,512]{1,0:T(8,128)S(1)} %add_bitcast_fusion), channel_id=1, source_target_pairs={{0,8},{1,9},{2,10},{3,11},{4,12},{5,13},{6,14},{7,15},{8,0},{9,1},... | collective-permute-start | bytes 2752520 | tf_op jit(solution)/shard_map/ppermute | solution.py:33
  138.7 2.6 %collective-permute-done.23.refs_2_ = bf16[1,2,16,32,128]{4,3,2,1,0:T(8,128)(2,1)S(1)} collective-permute-done((bf16[1,2,16,32,128]{4,3,2,1,0:T(8,128)(2,1)S(1)}, bf16[1,2,16,32,128]{4,3,2,1,0:T(8,128)(2,1)S(1)}, u32[]{:S(2)}, u32[]{:S(2)}) %collective-permute-start.23) | collective-permute-done | bytes 262176 | tf_op jit(solution)/shard_map/ppermute | solution.py:33
  141.3 2.7 %gram_part.3 = (f32[2,64,512]{2,1,0:T(8,128)S(1)}, f32[2,64,512]{2,1,0:T(8,128)S(1)}, bf16[128,2048]{1,0:T(8,128)(2,1)}) custom-call(s32[6]{0:T(128)S(1)} %stack.57.where, bf16[512,2048]{1,0:T(8,128)(2,1)S(1)} %columns.3.refs_8_.right.refs_0_, bf16[512,2048]{1,0:T(8,128)(2,1)S(1)} %columns.2.refs_0_.refs_1_, ...), custom_call_target="tpu_custom_call" | custom-call | flops 536870912 | bytes 4000000 | tf_op jit(solution)/shard_map/gram_part/pallas_call | solution.py:311
  144.0 1.7 %collective-permute-start.25 = (f32[2,64,512]{2,1,0:T(8,128)S(1)}, f32[2,64,512]{2,1,0:T(8,128)S(1)}, u32[]{:S(2)}, u32[]{:S(2)}) collective-permute-start(f32[2,64,512]{2,1,0:T(8,128)S(1)} %get-tuple-element.24), channel_id=1, source_target_pairs={{0,16},{1,17},{2,18},{3,19},{4,20},{5,21},{6,22},{7,23},{8,24},{9,... | collective-permute-start | bytes 786440 | tf_op jit(solution)/shard_map/ppermute | solution.py:33
  145.6 1.2 collective-permute-done.25.refs_4_
  146.8 1.8 %collective-permute-start.26 = (f32[64,512]{1,0:T(8,128)S(1)}, f32[64,512]{1,0:T(8,128)S(1)}, u32[]{:S(2)}, u32[]{:S(2)}) collective-permute-start(f32[64,512]{1,0:T(8,128)S(1)} %fusion), channel_id=1, source_target_pairs={{0,8},{1,9},{2,10},{3,11},{4,12},{5,13},{6,14},{7,15},{8,0},{9,1},... | collective-permute-start | bytes 393224 | tf_op jit(solution)/shard_map/ppermute | solution.py:33
  148.7 12.5 %collective-permute-done.26.refs_5_ = f32[64,512]{1,0:T(8,128)S(1)} collective-permute-done((f32[64,512]{1,0:T(8,128)S(1)}, f32[64,512]{1,0:T(8,128)S(1)}, u32[]{:S(2)}, u32[]{:S(2)}) %collective-permute-start.26) | collective-permute-done | bytes 131104 | tf_op jit(solution)/shard_map/ppermute | solution.py:33
  161.1 1.7 %finish.1 = f32[512,512]{1,0:T(8,128)} custom-call(s32[6]{0:T(128)S(1)} %stack.57.where, f32[512,512]{1,0:T(8,128)S(1)} %copy-done.4, f32[1,448,512]{2,1,0:T(8,128)S(1)} %get-tuple-element.19.refs_0_, f32[1,448,512]{2,1,0:T(8,128)S(1)} %collective-permute-done.20.refs_1_, f32[448,512]{1,0:T(8,128)S(1)} %collective-permute-done.22.refs_2_, ...), custom_call_target="tpu_custom_call" | custom-call | flops 1000000 | bytes 5000000 | tf_op jit(solution)/shard_map/finish/pallas_call | solution.py:346
  (79 shorter events, 11.5 us)
Async XLA Ops:
  4.3 31.5 %copy-start.9 = (bf16[256,256]{1,0:T(8,128)(2,1)S(1)}, bf16[256,256]{1,0:T(8,128)(2,1)}, u32[]{:S(2)}) copy-start(bf16[256,256]{1,0:T(8,128)(2,1)} %constant.116.fwd) | copy-start | bytes 393220
  4.3 31.5 %copy-start.10 = (bf16[256,256]{1,0:T(8,128)(2,1)S(1)}, bf16[256,256]{1,0:T(8,128)(2,1)}, u32[]{:S(2)}) copy-start(bf16[256,256]{1,0:T(8,128)(2,1)} %constant.117.bwd) | copy-start | bytes 393220
  4.3 31.5 %copy-start.11 = (bf16[256,64]{1,0:T(8,128)(2,1)S(1)}, bf16[256,64]{1,0:T(8,128)(2,1)}, u32[]{:S(2)}) copy-start(bf16[256,64]{1,0:T(8,128)(2,1)} %constant.114.first) | copy-start | bytes 98308
  4.3 31.5 %copy-start.12 = (f32[128,128]{1,0:T(8,128)S(1)}, f32[128,128]{1,0:T(8,128)}, u32[]{:S(2)}) copy-start(f32[128,128]{1,0:T(8,128)} %constant.112.clone.t_cos) | copy-start | bytes 196612
  4.3 31.4 %all-to-all-start = ((bf16[16,96,512]{2,1,0:T(8,128)(2,1)}), bf16[16,96,512]{2,1,0:T(8,128)(2,1)S(1)}, u32[]{:S(2)}, u32[]{:S(2)}) async-start(bf16[16,96,512]{2,1,0:T(8,128)(2,1)} %prepare.1), calls=%async_computation | async-start | bytes 3145728 | tf_op jit(solution)/shard_map/all_to_all | solution.py:371
  42.1 2.2 %collective-permute-start = (bf16[2,16,32,128]{3,2,1,0:T(8,128)(2,1)S(1)}, bf16[2,16,32,128]{3,2,1,0:T(8,128)(2,1)S(1)}, u32[]{:S(2)}, u32[]{:S(2)}) collective-permute-start(bf16[2,16,32,128]{3,2,1,0:T(8,128)(2,1)S(1)} %get-tuple-element.16), channel_id=1, source_target_pairs={{0,16},{1,17},{2,18},{3,19},{4,20},{5,21},{6,22},{7,23},{8,24},{9,... | collective-permute-start | bytes 786440 | tf_op jit(solution)/shard_map/ppermute | solution.py:33
  44.4 5.3 %collective-permute-start.7 = (bf16[2,16,32,128]{3,2,1,0:T(8,128)(2,1)S(1)}, bf16[2,16,32,128]{3,2,1,0:T(8,128)(2,1)S(1)}, u32[]{:S(2)}, u32[]{:S(2)}) collective-permute-start(bf16[2,16,32,128]{3,2,1,0:T(8,128)(2,1)S(1)} %get-tuple-element.26), channel_id=1, source_target_pairs={{0,0},{1,1},{2,38},{3,39},{4,68},{5,69},{6,98},{7,99},{8,128},{9,1... | collective-permute-start | bytes 786440 | tf_op jit(solution)/shard_map/ppermute | solution.py:33
  45.0 27.2 %collective-permute-start.8 = (bf16[2,16,32,128]{3,2,1,0:T(8,128)(2,1)S(1)}, bf16[2,16,32,128]{3,2,1,0:T(8,128)(2,1)S(1)}, u32[]{:S(2)}, u32[]{:S(2)}) collective-permute-start(bf16[2,16,32,128]{3,2,1,0:T(8,128)(2,1)S(1)} %get-tuple-element.25), channel_id=1, source_target_pairs={{0,8},{1,9},{2,46},{3,47},{4,76},{5,77},{6,106},{7,107},{8,136},{9... | collective-permute-start | bytes 786440 | tf_op jit(solution)/shard_map/ppermute | solution.py:33
  46.7 34.6 %collective-permute-start.1 = (bf16[2,16,32,128]{3,2,1,0:T(8,128)(2,1)S(1)}, bf16[2,16,32,128]{3,2,1,0:T(8,128)(2,1)S(1)}, u32[]{:S(2)}, u32[]{:S(2)}) collective-permute-start(bf16[2,16,32,128]{3,2,1,0:T(8,128)(2,1)S(1)} %get-tuple-element.27), channel_id=1, source_target_pairs={{0,136},{1,137},{2,138},{3,139},{4,140},{5,141},{6,142},{7,143},{8... | collective-permute-start | bytes 786440 | tf_op jit(solution)/shard_map/ppermute | solution.py:33
  49.6 31.6 %collective-permute-start.2 = (bf16[2,16,32,128]{3,2,1,0:T(8,128)(2,1)S(1)}, bf16[2,16,32,128]{3,2,1,0:T(8,128)(2,1)S(1)}, u32[]{:S(2)}, u32[]{:S(2)}) collective-permute-start(bf16[2,16,32,128]{3,2,1,0:T(8,128)(2,1)S(1)} %get-tuple-element.27), channel_id=1, source_target_pairs={{0,8},{1,9},{2,10},{3,11},{4,12},{5,13},{6,14},{7,15},{8,128},{9,1... | collective-permute-start | bytes 786440 | tf_op jit(solution)/shard_map/ppermute | solution.py:33
  72.3 20.0 %collective-permute-start.9 = (bf16[2,2,16,32,128]{4,3,2,1,0:T(8,128)(2,1)S(1)}, bf16[2,2,16,32,128]{4,3,2,1,0:T(8,128)(2,1)S(1)}, u32[]{:S(2)}, u32[]{:S(2)}) collective-permute-start(bf16[2,2,16,32,128]{4,3,2,1,0:T(8,128)(2,1)S(1)} %after.4.refs_1_), channel_id=1, source_target_pairs={{0,1},{1,2},{2,3},{3,4},{4,5},{5,6},{6,7},{7,0},{8,9},{9,10},{10,1... | collective-permute-start | bytes 1572872 | tf_op jit(solution)/shard_map/ppermute | solution.py:33
  74.0 18.3 %collective-permute-start.10 = (bf16[2,2,16,32,128]{4,3,2,1,0:T(8,128)(2,1)S(1)}, bf16[2,2,16,32,128]{4,3,2,1,0:T(8,128)(2,1)S(1)}, u32[]{:S(2)}, u32[]{:S(2)}) collective-permute-start(bf16[2,2,16,32,128]{4,3,2,1,0:T(8,128)(2,1)S(1)} %after.4.refs_1_), channel_id=1, source_target_pairs={{0,7},{1,0},{2,1},{3,2},{4,3},{5,4},{6,5},{7,6},{8,15},{9,8},{10,9... | collective-permute-start | bytes 1572872 | tf_op jit(solution)/shard_map/ppermute | solution.py:33
  81.3 13.6 %collective-permute-start.3 = (bf16[2,2,16,32,128]{4,3,2,1,0:T(8,128)(2,1)S(1)}, bf16[2,2,16,32,128]{4,3,2,1,0:T(8,128)(2,1)S(1)}, u32[]{:S(2)}, u32[]{:S(2)}) collective-permute-start(bf16[2,2,16,32,128]{4,3,2,1,0:T(8,128)(2,1)S(1)} %after.3.own), channel_id=1, source_target_pairs={{0,32},{1,33},{2,34},{3,35},{4,36},{5,37},{6,38},{7,39},{8,40},{9,... | collective-permute-start | bytes 1572872 | tf_op jit(solution)/shard_map/ppermute | solution.py:33
  81.4 13.5 %collective-permute-start.4 = (bf16[2,2,16,32,128]{4,3,2,1,0:T(8,128)(2,1)S(1)}, bf16[2,2,16,32,128]{4,3,2,1,0:T(8,128)(2,1)S(1)}, u32[]{:S(2)}, u32[]{:S(2)}) collective-permute-start(bf16[2,2,16,32,128]{4,3,2,1,0:T(8,128)(2,1)S(1)} %after.3.own), channel_id=1, source_target_pairs={{0,96},{1,97},{2,98},{3,99},{4,100},{5,101},{6,102},{7,103},{8,104... | collective-permute-start | bytes 1572872 | tf_op jit(solution)/shard_map/ppermute | solution.py:33
  84.1 10.8 %collective-permute-start.15 = (bf16[2,16,32,128]{3,2,1,0:T(8,128)(2,1)S(1)}, bf16[2,16,32,128]{3,2,1,0:T(8,128)(2,1)S(1)}, u32[]{:S(2)}, u32[]{:S(2)}) collective-permute-start(bf16[2,16,32,128]{3,2,1,0:T(8,128)(2,1)S(1)} %get-tuple-element.28.refs_2_.refs_0_), channel_id=1, source_target_pairs={{0,128},{1,129},{2,130},{3,131},{4,132},{5,133},{6,134},{7,135},{8... | collective-permute-start | bytes 786440 | tf_op jit(solution)/shard_map/ppermute | solution.py:33
  92.2 12.9 %collective-permute-start.11 = (bf16[2,2,16,32,128]{4,3,2,1,0:T(8,128)(2,1)S(1)}, bf16[2,2,16,32,128]{4,3,2,1,0:T(8,128)(2,1)}, u32[]{:S(2)}, u32[]{:S(2)}) collective-permute-start(bf16[2,2,16,32,128]{4,3,2,1,0:T(8,128)(2,1)S(1)} %collective-permute-done.9.refs_2_), channel_id=1, source_target_pairs={{0,1},{1,2},{2,3},{3,4},{4,5},{5,6},{6,7},{7,0},{8,9},{9,10},{10,1... | collective-permute-start | bytes 1572872 | tf_op jit(solution)/shard_map/ppermute | solution.py:33
  92.3 12.9 %collective-permute-start.12 = (bf16[2,2,16,32,128]{4,3,2,1,0:T(8,128)(2,1)S(1)}, bf16[2,2,16,32,128]{4,3,2,1,0:T(8,128)(2,1)}, u32[]{:S(2)}, u32[]{:S(2)}) collective-permute-start(bf16[2,2,16,32,128]{4,3,2,1,0:T(8,128)(2,1)S(1)} %collective-permute-done.10.refs_3_), channel_id=1, source_target_pairs={{0,7},{1,0},{2,1},{3,2},{4,3},{5,4},{6,5},{7,6},{8,15},{9,8},{10,9... | collective-permute-start | bytes 1572872 | tf_op jit(solution)/shard_map/ppermute | solution.py:33
  95.0 13.6 %collective-permute-start.16 = (bf16[2,2,16,32,128]{4,3,2,1,0:T(8,128)(2,1)S(1)}, bf16[2,2,16,32,128]{4,3,2,1,0:T(8,128)(2,1)S(1)}, u32[]{:S(2)}, u32[]{:S(2)}) collective-permute-start(bf16[2,2,16,32,128]{4,3,2,1,0:T(8,128)(2,1)S(1)} %after.5.own), channel_id=1, source_target_pairs={{0,32},{1,33},{2,34},{3,35},{4,36},{5,37},{6,38},{7,39},{8,40},{9,... | collective-permute-start | bytes 1572872 | tf_op jit(solution)/shard_map/ppermute | solution.py:33
  95.1 14.9 %collective-permute-start.17 = (bf16[2,2,16,32,128]{4,3,2,1,0:T(8,128)(2,1)S(1)}, bf16[2,2,16,32,128]{4,3,2,1,0:T(8,128)(2,1)S(1)}, u32[]{:S(2)}, u32[]{:S(2)}) collective-permute-start(bf16[2,2,16,32,128]{4,3,2,1,0:T(8,128)(2,1)S(1)} %after.5.own), channel_id=1, source_target_pairs={{0,96},{1,97},{2,98},{3,99},{4,100},{5,101},{6,102},{7,103},{8,104... | collective-permute-start | bytes 1572872 | tf_op jit(solution)/shard_map/ppermute | solution.py:33
  97.8 15.2 %collective-permute-start.5 = (bf16[2,1,16,32,128]{4,3,2,1,0:T(8,128)(2,1)S(1)}, bf16[2,1,16,32,128]{4,3,2,1,0:T(8,128)(2,1)S(1)}, u32[]{:S(2)}, u32[]{:S(2)}) collective-permute-start(bf16[2,1,16,32,128]{4,3,2,1,0:T(8,128)(2,1)S(1)} %slice.42), channel_id=1, source_target_pairs={{0,32},{1,33},{2,34},{3,35},{4,36},{5,37},{6,38},{7,39},{8,40},{9,... | collective-permute-start | bytes 786440 | tf_op jit(solution)/shard_map/ppermute | solution.py:33
  105.2 16.9 %collective-permute-start.13 = (bf16[2,2,16,32,128]{4,3,2,1,0:T(8,128)(2,1)}, bf16[2,2,16,32,128]{4,3,2,1,0:T(8,128)(2,1)S(1)}, u32[]{:S(2)}, u32[]{:S(2)}) collective-permute-start(bf16[2,2,16,32,128]{4,3,2,1,0:T(8,128)(2,1)} %collective-permute-done.11.refs_4_), channel_id=1, source_target_pairs={{0,1},{1,2},{2,3},{3,4},{4,5},{5,6},{6,7},{7,0},{8,9},{9,10},{10,1... | collective-permute-start | bytes 1572872 | tf_op jit(solution)/shard_map/ppermute | solution.py:33
  105.2 16.9 %collective-permute-start.14 = (bf16[2,2,16,32,128]{4,3,2,1,0:T(8,128)(2,1)}, bf16[2,2,16,32,128]{4,3,2,1,0:T(8,128)(2,1)}, u32[]{:S(2)}, u32[]{:S(2)}) collective-permute-start(bf16[2,2,16,32,128]{4,3,2,1,0:T(8,128)(2,1)} %collective-permute-done.12.refs_5_), channel_id=1, source_target_pairs={{0,7},{1,0},{2,1},{3,2},{4,3},{5,4},{6,5},{7,6},{8,15},{9,8},{10,9... | collective-permute-start | bytes 1572872 | tf_op jit(solution)/shard_map/ppermute | solution.py:33
  108.5 5.8 %collective-permute-start.6 = (bf16[2,1,16,32,128]{4,3,2,1,0:T(8,128)(2,1)}, bf16[2,1,16,32,128]{4,3,2,1,0:T(8,128)(2,1)}, u32[]{:S(2)}, u32[]{:S(2)}) collective-permute-start(bf16[2,1,16,32,128]{4,3,2,1,0:T(8,128)(2,1)} %slice.43), channel_id=1, source_target_pairs={{0,96},{1,97},{2,98},{3,99},{4,100},{5,101},{6,102},{7,103},{8,104... | collective-permute-start | bytes 786440 | tf_op jit(solution)/shard_map/ppermute | solution.py:33
  110.0 8.6 %collective-permute-start.18 = (bf16[2,1,16,32,128]{4,3,2,1,0:T(8,128)(2,1)}, bf16[2,1,16,32,128]{4,3,2,1,0:T(8,128)(2,1)}, u32[]{:S(2)}, u32[]{:S(2)}) collective-permute-start(bf16[2,1,16,32,128]{4,3,2,1,0:T(8,128)(2,1)} %slice.44), channel_id=1, source_target_pairs={{0,32},{1,33},{2,34},{3,35},{4,36},{5,37},{6,38},{7,39},{8,40},{9,... | collective-permute-start | bytes 786440 | tf_op jit(solution)/shard_map/ppermute | solution.py:33
  112.9 7.7 %collective-permute-start.19 = (bf16[2,1,16,32,128]{4,3,2,1,0:T(8,128)(2,1)}, bf16[2,1,16,32,128]{4,3,2,1,0:T(8,128)(2,1)}, u32[]{:S(2)}, u32[]{:S(2)}) collective-permute-start(bf16[2,1,16,32,128]{4,3,2,1,0:T(8,128)(2,1)} %slice.45), channel_id=1, source_target_pairs={{0,96},{1,97},{2,98},{3,99},{4,100},{5,101},{6,102},{7,103},{8,104... | collective-permute-start | bytes 786440 | tf_op jit(solution)/shard_map/ppermute | solution.py:33
  126.2 10.3 %collective-permute-start.21 = (f32[1,448,512]{2,1,0:T(8,128)S(1)}, f32[1,448,512]{2,1,0:T(8,128)S(1)}, u32[]{:S(2)}, u32[]{:S(2)}) collective-permute-start(f32[1,448,512]{2,1,0:T(8,128)S(1)} %get-tuple-element.22), channel_id=1, source_target_pairs={{0,16},{1,17},{2,18},{3,19},{4,20},{5,21},{6,22},{7,23},{8,24},{9,... | collective-permute-start | bytes 2752520 | tf_op jit(solution)/shard_map/ppermute | solution.py:33
  132.5 28.6 %collective-permute-start.20 = (f32[1,448,512]{2,1,0:T(8,128)S(1)}, f32[1,448,512]{2,1,0:T(8,128)S(1)}, u32[]{:S(2)}, u32[]{:S(2)}) collective-permute-start(f32[1,448,512]{2,1,0:T(8,128)S(1)} %get-tuple-element.20), channel_id=1, source_target_pairs={{0,16},{1,17},{2,18},{3,19},{4,20},{5,21},{6,22},{7,23},{8,24},{9,... | collective-permute-start | bytes 2752520 | tf_op jit(solution)/shard_map/ppermute | solution.py:33
  132.6 8.7 %collective-permute-start.23 = (bf16[1,2,16,32,128]{4,3,2,1,0:T(8,128)(2,1)S(1)}, bf16[1,2,16,32,128]{4,3,2,1,0:T(8,128)(2,1)S(1)}, u32[]{:S(2)}, u32[]{:S(2)}) collective-permute-start(bf16[1,2,16,32,128]{4,3,2,1,0:T(8,128)(2,1)S(1)} %slice.46), channel_id=1, source_target_pairs={{0,1},{1,2},{2,3},{3,4},{4,5},{5,6},{6,7},{7,0},{8,9},{9,10},{10,1... | collective-permute-start | bytes 786440 | tf_op jit(solution)/shard_map/ppermute | solution.py:33
  133.7 7.6 %collective-permute-start.24 = (bf16[1,2,16,32,128]{4,3,2,1,0:T(8,128)(2,1)S(1)}, bf16[1,2,16,32,128]{4,3,2,1,0:T(8,128)(2,1)S(1)}, u32[]{:S(2)}, u32[]{:S(2)}) collective-permute-start(bf16[1,2,16,32,128]{4,3,2,1,0:T(8,128)(2,1)S(1)} %slice.47), channel_id=1, source_target_pairs={{0,7},{1,0},{2,1},{3,2},{4,3},{5,4},{6,5},{7,6},{8,15},{9,8},{10,9... | collective-permute-start | bytes 786440 | tf_op jit(solution)/shard_map/ppermute | solution.py:33
  136.6 24.5 %collective-permute-start.22 = (f32[448,512]{1,0:T(8,128)S(1)}, f32[448,512]{1,0:T(8,128)S(1)}, u32[]{:S(2)}, u32[]{:S(2)}) collective-permute-start(f32[448,512]{1,0:T(8,128)S(1)} %add_bitcast_fusion), channel_id=1, source_target_pairs={{0,8},{1,9},{2,10},{3,11},{4,12},{5,13},{6,14},{7,15},{8,0},{9,1},... | collective-permute-start | bytes 2752520 | tf_op jit(solution)/shard_map/ppermute | solution.py:33
  144.0 2.8 %collective-permute-start.25 = (f32[2,64,512]{2,1,0:T(8,128)S(1)}, f32[2,64,512]{2,1,0:T(8,128)S(1)}, u32[]{:S(2)}, u32[]{:S(2)}) collective-permute-start(f32[2,64,512]{2,1,0:T(8,128)S(1)} %get-tuple-element.24), channel_id=1, source_target_pairs={{0,16},{1,17},{2,18},{3,19},{4,20},{5,21},{6,22},{7,23},{8,24},{9,... | collective-permute-start | bytes 786440 | tf_op jit(solution)/shard_map/ppermute | solution.py:33
  146.8 14.3 %collective-permute-start.26 = (f32[64,512]{1,0:T(8,128)S(1)}, f32[64,512]{1,0:T(8,128)S(1)}, u32[]{:S(2)}, u32[]{:S(2)}) collective-permute-start(f32[64,512]{1,0:T(8,128)S(1)} %fusion), channel_id=1, source_target_pairs={{0,8},{1,9},{2,10},{3,11},{4,12},{5,13},{6,14},{7,15},{8,0},{9,1},... | collective-permute-start | bytes 393224 | tf_op jit(solution)/shard_map/ppermute | solution.py:33
  (11 other events, 154.6 us)

commit v8 on v7

--- a/solution.py
+++ b/solution.py
@@ -298,9 +298,7 @@
         out_specs=[VMEM] * 2,
         out_shape=[tile, tile],
         compiler_params=pltpu.CompilerParams(vmem_limit_bytes=18 * MIB),
-        cost_estimate=pl.CostEstimate(
-            flops=2 * left.shape[0] * 512 * 2048, bytes_accessed=4 * 10**6, transcendentals=0
-        ),
+        cost_estimate=pl.CostEstimate(flops=10**6, bytes_accessed=10**4, transcendentals=0),
         name="gram_again",
     )(left, right)
 
@@ -314,11 +312,7 @@
         out_specs=[VMEM] * 3,
         out_shape=[tile, tile, jax.ShapeDtypeStruct((2 * rows, 2048), BF)],
         compiler_params=pltpu.CompilerParams(vmem_limit_bytes=18 * MIB),
-        cost_estimate=pl.CostEstimate(
-            flops=4 * rows * len(rights) * 512 * 2048,
-            bytes_accessed=4 * 10**6,
-            transcendentals=0,
-        ),
+        cost_estimate=pl.CostEstimate(flops=10**6, bytes_accessed=10**4, transcendentals=0),
         name="gram_part",
     )(where, *rights, *shards, *earlier)
 

time: 164 us -> 160 us (0.976)
  waiting for transfers between devices: 82.3 us -> 80.3 us
    ppermute x27, waiting for transfers between devices: 60.3 us -> 58.3 us  [move(): return lax.ppermute(array, MESH, pairs)]
  transfers between devices with their start and end apart: 28 -> 28, of which waited for: 11 -> 12; matrix products, arithmetic and copies ran while one was open for 3% -> 3% of each run, Pallas kernels for 5% -> 5%
where the time goes in v8:
time: 160 us; the launch traced here: 159 us
  waiting for transfers between devices  80.3 us (50%)
  starting transfers between devices  49.5 us (31%)
  Pallas kernels  24.1 us (15%)
  local copies, waits for them, and re-layouts  5.04 us (3%)
    ppermute x27, waiting for transfers between devices, move(): return lax.ppermute(array, MESH, pairs)  58.3 us
    ppermute x27, starting transfers between devices, move(): return lax.ppermute(array, MESH, pairs)  40.9 us
    all_to_all x1, waiting for transfers between devices, local(): lax.all_to_all(outgoing, 'seq', split_axis=0, concat_axis=0, tiled=True)  22 us
    all_to_all x1, starting transfers between devices, local(): lax.all_to_all(outgoing, 'seq', split_axis=0, concat_axis=0, tiled=True)  8.59 us
    pallas_call x2, Pallas kernels, gram_part(): pl.pallas_call(functools.partial(gram_kernel, steps, len(rights), len(ear...  6.77 us
    pallas_call x1, Pallas kernels, convolve(): pl.pallas_call(conv_kernel, in_specs=[SMEM, SMEM] + [VMEM] * 7, out_specs...  6.25 us
    pallas_call x1, Pallas kernels, prepare(): pl.pallas_call(prepare_kernel, grid=(4,), in_specs=[block] * 4, out_specs...  4.26 us
  transfers between devices with their start and end apart: 28, of which 12 were waited for; matrix products, arithmetic and copies ran while one was open for 3% of the time, Pallas kernels for 5%

profile of v8, /device:TPU:1, one launch (start us, length us, event | category | flops | bytes accessed | tf_op | source)
XLA Modules:
  0.0 159.5 jit_solution(4771046970177012540)
XLA Ops:
  0.0 4.3 %prepare.1 = bf16[16,96,512]{2,1,0:T(8,128)(2,1)} custom-call(bf16[512,512]{1,0:T(8,128)(2,1)} %gate.1, bf16[512,512]{1,0:T(8,128)(2,1)} %key.1, bf16[512,512]{1,0:T(8,128)(2,1)} %value.1, bf16[512,512]{1,0:T(8,128)(2,1)} %filt.1), custom_call_target="tpu_custom_call" | custom-call | tf_op jit(solution)/shard_map/prepare/pallas_call | solution.py:124
  4.3 8.6 %all-to-all-start = ((bf16[16,96,512]{2,1,0:T(8,128)(2,1)}), bf16[16,96,512]{2,1,0:T(8,128)(2,1)S(1)}, u32[]{:S(2)}, u32[]{:S(2)}) async-start(bf16[16,96,512]{2,1,0:T(8,128)(2,1)} %prepare.1), calls=%async_computation | async-start | bytes 3145728 | tf_op jit(solution)/shard_map/all_to_all | solution.py:365
  13.7 22.0 %all-to-all-done.data = bf16[16,96,512]{2,1,0:T(8,128)(2,1)S(1)} async-done(((bf16[16,96,512]{2,1,0:T(8,128)(2,1)}), bf16[16,96,512]{2,1,0:T(8,128)(2,1)S(1)}, u32[]{:S(2)}, u32[]{:S(2)}) %all-to-all-start) | async-done | bytes 1572896 | tf_op jit(solution)/shard_map/all_to_all | solution.py:365
  35.8 6.3 %convolve.1 = (bf16[16,32,128]{2,1,0:T(8,128)(2,1)S(1)}, bf16[16,32,128]{2,1,0:T(8,128)(2,1)S(1)}, bf16[2,16,32,128]{3,2,1,0:T(8,128)(2,1)S(1)}) custom-call(s32[6]{0:T(128)S(1)} %stack.57.where, f32[32]{0:T(128)S(1)} %dynamic_slice.3.skip, bf16[16,96,512]{2,1,0:T(8,128)(2,1)S(1)} %all-to-all-done.data, bf16[256,64]{1,0:T(8,128)(2,1)S(1)} %copy-done.11, ...), custom_call_target="tpu_custom_call" | custom-call | flops 4000000000 | bytes 3000000 | tf_op jit(solution)/shard_map/convolve/pallas_call | solution.py:211
  43.1 1.2 collective-permute-done
  45.0 1.7 %collective-permute-start.8 = (bf16[2,16,32,128]{3,2,1,0:T(8,128)(2,1)S(1)}, bf16[2,16,32,128]{3,2,1,0:T(8,128)(2,1)S(1)}, u32[]{:S(2)}, u32[]{:S(2)}) collective-permute-start(bf16[2,16,32,128]{3,2,1,0:T(8,128)(2,1)S(1)} %get-tuple-element.25), channel_id=1, source_target_pairs={{0,8},{1,9},{2,46},{3,47},{4,76},{5,77},{6,106},{7,107},{8,136},{9... | collective-permute-start | bytes 786440 | tf_op jit(solution)/shard_map/ppermute | solution.py:33
  46.7 3.0 %collective-permute-start.1 = (bf16[2,16,32,128]{3,2,1,0:T(8,128)(2,1)S(1)}, bf16[2,16,32,128]{3,2,1,0:T(8,128)(2,1)S(1)}, u32[]{:S(2)}, u32[]{:S(2)}) collective-permute-start(bf16[2,16,32,128]{3,2,1,0:T(8,128)(2,1)S(1)} %get-tuple-element.27), channel_id=1, source_target_pairs={{0,136},{1,137},{2,138},{3,139},{4,140},{5,141},{6,142},{7,143},{8... | collective-permute-start | bytes 786440 | tf_op jit(solution)/shard_map/ppermute | solution.py:33
  49.7 22.6 %collective-permute-done.8.refs_1_ = bf16[2,16,32,128]{3,2,1,0:T(8,128)(2,1)S(1)} collective-permute-done((bf16[2,16,32,128]{3,2,1,0:T(8,128)(2,1)S(1)}, bf16[2,16,32,128]{3,2,1,0:T(8,128)(2,1)S(1)}, u32[]{:S(2)}, u32[]{:S(2)}) %collective-permute-start.8) | collective-permute-done | bytes 262176 | tf_op jit(solution)/shard_map/ppermute | solution.py:33
  72.3 1.7 %collective-permute-start.9 = (bf16[2,2,16,32,128]{4,3,2,1,0:T(8,128)(2,1)S(1)}, bf16[2,2,16,32,128]{4,3,2,1,0:T(8,128)(2,1)S(1)}, u32[]{:S(2)}, u32[]{:S(2)}) collective-permute-start(bf16[2,2,16,32,128]{4,3,2,1,0:T(8,128)(2,1)S(1)} %after.4.refs_1_), channel_id=1, source_target_pairs={{0,1},{1,2},{2,3},{3,4},{4,5},{5,6},{6,7},{7,0},{8,9},{9,10},{10,1... | collective-permute-start | bytes 1572872 | tf_op jit(solution)/shard_map/ppermute | solution.py:33
  74.0 7.3 %collective-permute-start.10 = (bf16[2,2,16,32,128]{4,3,2,1,0:T(8,128)(2,1)S(1)}, bf16[2,2,16,32,128]{4,3,2,1,0:T(8,128)(2,1)S(1)}, u32[]{:S(2)}, u32[]{:S(2)}) collective-permute-start(bf16[2,2,16,32,128]{4,3,2,1,0:T(8,128)(2,1)S(1)} %after.4.refs_1_), channel_id=1, source_target_pairs={{0,7},{1,0},{2,1},{3,2},{4,3},{5,4},{6,5},{7,6},{8,15},{9,8},{10,9... | collective-permute-start | bytes 1572872 | tf_op jit(solution)/shard_map/ppermute | solution.py:33
  81.4 2.7 %collective-permute-start.4 = (bf16[2,2,16,32,128]{4,3,2,1,0:T(8,128)(2,1)S(1)}, bf16[2,2,16,32,128]{4,3,2,1,0:T(8,128)(2,1)S(1)}, u32[]{:S(2)}, u32[]{:S(2)}) collective-permute-start(bf16[2,2,16,32,128]{4,3,2,1,0:T(8,128)(2,1)S(1)} %after.3.own), channel_id=1, source_target_pairs={{0,96},{1,97},{2,98},{3,99},{4,100},{5,101},{6,102},{7,103},{8,104... | collective-permute-start | bytes 1572872 | tf_op jit(solution)/shard_map/ppermute | solution.py:33
  84.7 7.5 %collective-permute-done.9.refs_2_ = bf16[2,2,16,32,128]{4,3,2,1,0:T(8,128)(2,1)S(1)} collective-permute-done((bf16[2,2,16,32,128]{4,3,2,1,0:T(8,128)(2,1)S(1)}, bf16[2,2,16,32,128]{4,3,2,1,0:T(8,128)(2,1)S(1)}, u32[]{:S(2)}, u32[]{:S(2)}) %collective-permute-start.9) | collective-permute-done | bytes 524320 | tf_op jit(solution)/shard_map/ppermute | solution.py:33
  92.3 2.7 %collective-permute-start.12 = (bf16[2,2,16,32,128]{4,3,2,1,0:T(8,128)(2,1)S(1)}, bf16[2,2,16,32,128]{4,3,2,1,0:T(8,128)(2,1)}, u32[]{:S(2)}, u32[]{:S(2)}) collective-permute-start(bf16[2,2,16,32,128]{4,3,2,1,0:T(8,128)(2,1)S(1)} %collective-permute-done.10.refs_3_), channel_id=1, source_target_pairs={{0,7},{1,0},{2,1},{3,2},{4,3},{5,4},{6,5},{7,6},{8,15},{9,8},{10,9... | collective-permute-start | bytes 1572872 | tf_op jit(solution)/shard_map/ppermute | solution.py:33
  95.1 2.7 %collective-permute-start.17 = (bf16[2,2,16,32,128]{4,3,2,1,0:T(8,128)(2,1)S(1)}, bf16[2,2,16,32,128]{4,3,2,1,0:T(8,128)(2,1)S(1)}, u32[]{:S(2)}, u32[]{:S(2)}) collective-permute-start(bf16[2,2,16,32,128]{4,3,2,1,0:T(8,128)(2,1)S(1)} %after.5.own), channel_id=1, source_target_pairs={{0,96},{1,97},{2,98},{3,99},{4,100},{5,101},{6,102},{7,103},{8,104... | collective-permute-start | bytes 1572872 | tf_op jit(solution)/shard_map/ppermute | solution.py:33
  97.9 7.3 %collective-permute-done.11.refs_4_ = bf16[2,2,16,32,128]{4,3,2,1,0:T(8,128)(2,1)} collective-permute-done((bf16[2,2,16,32,128]{4,3,2,1,0:T(8,128)(2,1)S(1)}, bf16[2,2,16,32,128]{4,3,2,1,0:T(8,128)(2,1)}, u32[]{:S(2)}, u32[]{:S(2)}) %collective-permute-start.11) | collective-permute-done | bytes 524320 | tf_op jit(solution)/shard_map/ppermute | solution.py:33
  105.2 2.7 %collective-permute-start.14 = (bf16[2,2,16,32,128]{4,3,2,1,0:T(8,128)(2,1)}, bf16[2,2,16,32,128]{4,3,2,1,0:T(8,128)(2,1)}, u32[]{:S(2)}, u32[]{:S(2)}) collective-permute-start(bf16[2,2,16,32,128]{4,3,2,1,0:T(8,128)(2,1)} %collective-permute-done.12.refs_5_), channel_id=1, source_target_pairs={{0,7},{1,0},{2,1},{3,2},{4,3},{5,4},{6,5},{7,6},{8,15},{9,8},{10,9... | collective-permute-start | bytes 1572872 | tf_op jit(solution)/shard_map/ppermute | solution.py:33
  112.9 1.3 collective-permute-start.19
  114.4 1.4 columns.2.refs_0_.refs_1_
  115.8 2.8 %collective-permute-done.18.far_low = bf16[2,1,16,32,128]{4,3,2,1,0:T(8,128)(2,1)} collective-permute-done((bf16[2,1,16,32,128]{4,3,2,1,0:T(8,128)(2,1)}, bf16[2,1,16,32,128]{4,3,2,1,0:T(8,128)(2,1)}, u32[]{:S(2)}, u32[]{:S(2)}) %collective-permute-start.18) | collective-permute-done | bytes 262176 | tf_op jit(solution)/shard_map/ppermute | solution.py:33
  118.6 2.0 %collective-permute-done.19.far_high = bf16[2,1,16,32,128]{4,3,2,1,0:T(8,128)(2,1)} collective-permute-done((bf16[2,1,16,32,128]{4,3,2,1,0:T(8,128)(2,1)}, bf16[2,1,16,32,128]{4,3,2,1,0:T(8,128)(2,1)}, u32[]{:S(2)}, u32[]{:S(2)}) %collective-permute-start.19) | collective-permute-done | bytes 262176 | tf_op jit(solution)/shard_map/ppermute | solution.py:33
  120.6 1.4 columns.3.refs_8_.right.refs_0_
  122.1 4.1 %gram_part.2 = (f32[1,448,512]{2,1,0:T(8,128)S(1)}, f32[1,448,512]{2,1,0:T(8,128)S(1)}, bf16[896,2048]{1,0:T(8,128)(2,1)S(1)}) custom-call(s32[6]{0:T(128)S(1)} %stack.57.where, bf16[512,2048]{1,0:T(8,128)(2,1)S(1)} %columns.2.refs_0_.refs_1_, bf16[2,2,16,32,128]{4,3,2,1,0:T(8,128)(2,1)S(1)} %after.4.refs_1_, bf16[2,2,16,32,128]{4,3,2,1,0:T(8,128)(2,1)S(1)} %copy-done.6, ...), custom_call_target="tpu_custom_call" | custom-call | flops 1000000 | bytes 10000 | tf_op jit(solution)/shard_map/gram_part/pallas_call | solution.py:309
  126.2 4.2 %collective-permute-start.21 = (f32[1,448,512]{2,1,0:T(8,128)S(1)}, f32[1,448,512]{2,1,0:T(8,128)S(1)}, u32[]{:S(2)}, u32[]{:S(2)}) collective-permute-start(f32[1,448,512]{2,1,0:T(8,128)S(1)} %get-tuple-element.22), channel_id=1, source_target_pairs={{0,16},{1,17},{2,18},{3,19},{4,20},{5,21},{6,22},{7,23},{8,24},{9,... | collective-permute-start | bytes 2752520 | tf_op jit(solution)/shard_map/ppermute | solution.py:33
  130.4 2.1 %gram_again.1 = (f32[1,448,512]{2,1,0:T(8,128)S(1)}, f32[1,448,512]{2,1,0:T(8,128)S(1)}) custom-call(bf16[896,2048]{1,0:T(8,128)(2,1)S(1)} %get-tuple-element.18.left, bf16[512,2048]{1,0:T(8,128)(2,1)S(1)} %columns.3.refs_8_.right.refs_0_), custom_call_target="tpu_custom_call" | custom-call | flops 1000000 | bytes 10000 | tf_op jit(solution)/shard_map/gram_again/pallas_call | solution.py:295
  132.8 1.8 %collective-permute-start.22 = (f32[448,512]{1,0:T(8,128)S(1)}, f32[448,512]{1,0:T(8,128)S(1)}, u32[]{:S(2)}, u32[]{:S(2)}) collective-permute-start(f32[448,512]{1,0:T(8,128)S(1)} %add_bitcast_fusion), channel_id=1, source_target_pairs={{0,8},{1,9},{2,10},{3,11},{4,12},{5,13},{6,14},{7,15},{8,0},{9,1},... | collective-permute-start | bytes 2752520 | tf_op jit(solution)/shard_map/ppermute | solution.py:33
  135.7 3.0 %collective-permute-start.24 = (bf16[1,2,16,32,128]{4,3,2,1,0:T(8,128)(2,1)S(1)}, bf16[1,2,16,32,128]{4,3,2,1,0:T(8,128)(2,1)S(1)}, u32[]{:S(2)}, u32[]{:S(2)}) collective-permute-start(bf16[1,2,16,32,128]{4,3,2,1,0:T(8,128)(2,1)S(1)} %slice.47), channel_id=1, source_target_pairs={{0,7},{1,0},{2,1},{3,2},{4,3},{5,4},{6,5},{7,6},{8,15},{9,8},{10,9... | collective-permute-start | bytes 786440 | tf_op jit(solution)/shard_map/ppermute | solution.py:33
  138.7 4.3 %collective-permute-done.23.refs_2_ = bf16[1,2,16,32,128]{4,3,2,1,0:T(8,128)(2,1)S(1)} collective-permute-done((bf16[1,2,16,32,128]{4,3,2,1,0:T(8,128)(2,1)S(1)}, bf16[1,2,16,32,128]{4,3,2,1,0:T(8,128)(2,1)S(1)}, u32[]{:S(2)}, u32[]{:S(2)}) %collective-permute-start.23) | collective-permute-done | bytes 262176 | tf_op jit(solution)/shard_map/ppermute | solution.py:33
  143.2 2.7 %gram_part.3 = (f32[2,64,512]{2,1,0:T(8,128)S(1)}, f32[2,64,512]{2,1,0:T(8,128)S(1)}, bf16[128,2048]{1,0:T(8,128)(2,1)}) custom-call(s32[6]{0:T(128)S(1)} %stack.57.where, bf16[512,2048]{1,0:T(8,128)(2,1)S(1)} %columns.3.refs_8_.right.refs_0_, bf16[512,2048]{1,0:T(8,128)(2,1)S(1)} %columns.2.refs_0_.refs_1_, ...), custom_call_target="tpu_custom_call" | custom-call | flops 1000000 | bytes 10000 | tf_op jit(solution)/shard_map/gram_part/pallas_call | solution.py:309
  145.9 2.0 %collective-permute-start.25 = (f32[2,64,512]{2,1,0:T(8,128)S(1)}, f32[2,64,512]{2,1,0:T(8,128)S(1)}, u32[]{:S(2)}, u32[]{:S(2)}) collective-permute-start(f32[2,64,512]{2,1,0:T(8,128)S(1)} %get-tuple-element.24), channel_id=1, source_target_pairs={{0,16},{1,17},{2,18},{3,19},{4,20},{5,21},{6,22},{7,23},{8,24},{9,... | collective-permute-start | bytes 786440 | tf_op jit(solution)/shard_map/ppermute | solution.py:33
  147.9 1.2 collective-permute-done.25.refs_4_
  149.2 8.5 %collective-permute-done.26.refs_5_ = f32[64,512]{1,0:T(8,128)S(1)} collective-permute-done((f32[64,512]{1,0:T(8,128)S(1)}, f32[64,512]{1,0:T(8,128)S(1)}, u32[]{:S(2)}, u32[]{:S(2)}) %collective-permute-start.26) | collective-permute-done | bytes 131104 | tf_op jit(solution)/shard_map/ppermute | solution.py:33
  157.7 1.7 %finish.1 = f32[512,512]{1,0:T(8,128)} custom-call(s32[6]{0:T(128)S(1)} %stack.57.where, f32[512,512]{1,0:T(8,128)S(1)} %copy-done.4, f32[1,448,512]{2,1,0:T(8,128)S(1)} %get-tuple-element.19.refs_0_, f32[1,448,512]{2,1,0:T(8,128)S(1)} %collective-permute-done.20.refs_1_, f32[448,512]{1,0:T(8,128)S(1)} %collective-permute-done.22.refs_2_, ...), custom_call_target="tpu_custom_call" | custom-call | flops 1000000 | bytes 5000000 | tf_op jit(solution)/shard_map/finish/pallas_call | solution.py:340
  (79 shorter events, 10.7 us)
Async XLA Ops:
  4.3 31.5 %copy-start.9 = (bf16[256,256]{1,0:T(8,128)(2,1)S(1)}, bf16[256,256]{1,0:T(8,128)(2,1)}, u32[]{:S(2)}) copy-start(bf16[256,256]{1,0:T(8,128)(2,1)} %constant.116.fwd) | copy-start | bytes 393220
  4.3 31.5 %copy-start.10 = (bf16[256,256]{1,0:T(8,128)(2,1)S(1)}, bf16[256,256]{1,0:T(8,128)(2,1)}, u32[]{:S(2)}) copy-start(bf16[256,256]{1,0:T(8,128)(2,1)} %constant.117.bwd) | copy-start | bytes 393220
  4.3 31.5 %copy-start.11 = (bf16[256,64]{1,0:T(8,128)(2,1)S(1)}, bf16[256,64]{1,0:T(8,128)(2,1)}, u32[]{:S(2)}) copy-start(bf16[256,64]{1,0:T(8,128)(2,1)} %constant.114.first) | copy-start | bytes 98308
  4.3 31.5 %copy-start.12 = (f32[128,128]{1,0:T(8,128)S(1)}, f32[128,128]{1,0:T(8,128)}, u32[]{:S(2)}) copy-start(f32[128,128]{1,0:T(8,128)} %constant.112.clone.t_cos) | copy-start | bytes 196612
  4.3 31.4 %all-to-all-start = ((bf16[16,96,512]{2,1,0:T(8,128)(2,1)}), bf16[16,96,512]{2,1,0:T(8,128)(2,1)S(1)}, u32[]{:S(2)}, u32[]{:S(2)}) async-start(bf16[16,96,512]{2,1,0:T(8,128)(2,1)} %prepare.1), calls=%async_computation | async-start | bytes 3145728 | tf_op jit(solution)/shard_map/all_to_all | solution.py:365
  42.1 2.2 %collective-permute-start = (bf16[2,16,32,128]{3,2,1,0:T(8,128)(2,1)S(1)}, bf16[2,16,32,128]{3,2,1,0:T(8,128)(2,1)S(1)}, u32[]{:S(2)}, u32[]{:S(2)}) collective-permute-start(bf16[2,16,32,128]{3,2,1,0:T(8,128)(2,1)S(1)} %get-tuple-element.16), channel_id=1, source_target_pairs={{0,16},{1,17},{2,18},{3,19},{4,20},{5,21},{6,22},{7,23},{8,24},{9,... | collective-permute-start | bytes 786440 | tf_op jit(solution)/shard_map/ppermute | solution.py:33
  44.4 5.3 %collective-permute-start.7 = (bf16[2,16,32,128]{3,2,1,0:T(8,128)(2,1)S(1)}, bf16[2,16,32,128]{3,2,1,0:T(8,128)(2,1)S(1)}, u32[]{:S(2)}, u32[]{:S(2)}) collective-permute-start(bf16[2,16,32,128]{3,2,1,0:T(8,128)(2,1)S(1)} %get-tuple-element.26), channel_id=1, source_target_pairs={{0,0},{1,1},{2,38},{3,39},{4,68},{5,69},{6,98},{7,99},{8,128},{9,1... | collective-permute-start | bytes 786440 | tf_op jit(solution)/shard_map/ppermute | solution.py:33
  45.0 27.2 %collective-permute-start.8 = (bf16[2,16,32,128]{3,2,1,0:T(8,128)(2,1)S(1)}, bf16[2,16,32,128]{3,2,1,0:T(8,128)(2,1)S(1)}, u32[]{:S(2)}, u32[]{:S(2)}) collective-permute-start(bf16[2,16,32,128]{3,2,1,0:T(8,128)(2,1)S(1)} %get-tuple-element.25), channel_id=1, source_target_pairs={{0,8},{1,9},{2,46},{3,47},{4,76},{5,77},{6,106},{7,107},{8,136},{9... | collective-permute-start | bytes 786440 | tf_op jit(solution)/shard_map/ppermute | solution.py:33
  46.7 34.6 %collective-permute-start.1 = (bf16[2,16,32,128]{3,2,1,0:T(8,128)(2,1)S(1)}, bf16[2,16,32,128]{3,2,1,0:T(8,128)(2,1)S(1)}, u32[]{:S(2)}, u32[]{:S(2)}) collective-permute-start(bf16[2,16,32,128]{3,2,1,0:T(8,128)(2,1)S(1)} %get-tuple-element.27), channel_id=1, source_target_pairs={{0,136},{1,137},{2,138},{3,139},{4,140},{5,141},{6,142},{7,143},{8... | collective-permute-start | bytes 786440 | tf_op jit(solution)/shard_map/ppermute | solution.py:33
  49.6 31.6 %collective-permute-start.2 = (bf16[2,16,32,128]{3,2,1,0:T(8,128)(2,1)S(1)}, bf16[2,16,32,128]{3,2,1,0:T(8,128)(2,1)S(1)}, u32[]{:S(2)}, u32[]{:S(2)}) collective-permute-start(bf16[2,16,32,128]{3,2,1,0:T(8,128)(2,1)S(1)} %get-tuple-element.27), channel_id=1, source_target_pairs={{0,8},{1,9},{2,10},{3,11},{4,12},{5,13},{6,14},{7,15},{8,128},{9,1... | collective-permute-start | bytes 786440 | tf_op jit(solution)/shard_map/ppermute | solution.py:33
  72.3 20.0 %collective-permute-start.9 = (bf16[2,2,16,32,128]{4,3,2,1,0:T(8,128)(2,1)S(1)}, bf16[2,2,16,32,128]{4,3,2,1,0:T(8,128)(2,1)S(1)}, u32[]{:S(2)}, u32[]{:S(2)}) collective-permute-start(bf16[2,2,16,32,128]{4,3,2,1,0:T(8,128)(2,1)S(1)} %after.4.refs_1_), channel_id=1, source_target_pairs={{0,1},{1,2},{2,3},{3,4},{4,5},{5,6},{6,7},{7,0},{8,9},{9,10},{10,1... | collective-permute-start | bytes 1572872 | tf_op jit(solution)/shard_map/ppermute | solution.py:33
  74.0 18.3 %collective-permute-start.10 = (bf16[2,2,16,32,128]{4,3,2,1,0:T(8,128)(2,1)S(1)}, bf16[2,2,16,32,128]{4,3,2,1,0:T(8,128)(2,1)S(1)}, u32[]{:S(2)}, u32[]{:S(2)}) collective-permute-start(bf16[2,2,16,32,128]{4,3,2,1,0:T(8,128)(2,1)S(1)} %after.4.refs_1_), channel_id=1, source_target_pairs={{0,7},{1,0},{2,1},{3,2},{4,3},{5,4},{6,5},{7,6},{8,15},{9,8},{10,9... | collective-permute-start | bytes 1572872 | tf_op jit(solution)/shard_map/ppermute | solution.py:33
  81.3 13.6 %collective-permute-start.3 = (bf16[2,2,16,32,128]{4,3,2,1,0:T(8,128)(2,1)S(1)}, bf16[2,2,16,32,128]{4,3,2,1,0:T(8,128)(2,1)S(1)}, u32[]{:S(2)}, u32[]{:S(2)}) collective-permute-start(bf16[2,2,16,32,128]{4,3,2,1,0:T(8,128)(2,1)S(1)} %after.3.own), channel_id=1, source_target_pairs={{0,32},{1,33},{2,34},{3,35},{4,36},{5,37},{6,38},{7,39},{8,40},{9,... | collective-permute-start | bytes 1572872 | tf_op jit(solution)/shard_map/ppermute | solution.py:33
  81.4 13.5 %collective-permute-start.4 = (bf16[2,2,16,32,128]{4,3,2,1,0:T(8,128)(2,1)S(1)}, bf16[2,2,16,32,128]{4,3,2,1,0:T(8,128)(2,1)S(1)}, u32[]{:S(2)}, u32[]{:S(2)}) collective-permute-start(bf16[2,2,16,32,128]{4,3,2,1,0:T(8,128)(2,1)S(1)} %after.3.own), channel_id=1, source_target_pairs={{0,96},{1,97},{2,98},{3,99},{4,100},{5,101},{6,102},{7,103},{8,104... | collective-permute-start | bytes 1572872 | tf_op jit(solution)/shard_map/ppermute | solution.py:33
  84.1 10.8 %collective-permute-start.15 = (bf16[2,16,32,128]{3,2,1,0:T(8,128)(2,1)S(1)}, bf16[2,16,32,128]{3,2,1,0:T(8,128)(2,1)S(1)}, u32[]{:S(2)}, u32[]{:S(2)}) collective-permute-start(bf16[2,16,32,128]{3,2,1,0:T(8,128)(2,1)S(1)} %get-tuple-element.28.refs_2_.refs_0_), channel_id=1, source_target_pairs={{0,128},{1,129},{2,130},{3,131},{4,132},{5,133},{6,134},{7,135},{8... | collective-permute-start | bytes 786440 | tf_op jit(solution)/shard_map/ppermute | solution.py:33
  92.2 12.9 %collective-permute-start.11 = (bf16[2,2,16,32,128]{4,3,2,1,0:T(8,128)(2,1)S(1)}, bf16[2,2,16,32,128]{4,3,2,1,0:T(8,128)(2,1)}, u32[]{:S(2)}, u32[]{:S(2)}) collective-permute-start(bf16[2,2,16,32,128]{4,3,2,1,0:T(8,128)(2,1)S(1)} %collective-permute-done.9.refs_2_), channel_id=1, source_target_pairs={{0,1},{1,2},{2,3},{3,4},{4,5},{5,6},{6,7},{7,0},{8,9},{9,10},{10,1... | collective-permute-start | bytes 1572872 | tf_op jit(solution)/shard_map/ppermute | solution.py:33
  92.3 12.9 %collective-permute-start.12 = (bf16[2,2,16,32,128]{4,3,2,1,0:T(8,128)(2,1)S(1)}, bf16[2,2,16,32,128]{4,3,2,1,0:T(8,128)(2,1)}, u32[]{:S(2)}, u32[]{:S(2)}) collective-permute-start(bf16[2,2,16,32,128]{4,3,2,1,0:T(8,128)(2,1)S(1)} %collective-permute-done.10.refs_3_), channel_id=1, source_target_pairs={{0,7},{1,0},{2,1},{3,2},{4,3},{5,4},{6,5},{7,6},{8,15},{9,8},{10,9... | collective-permute-start | bytes 1572872 | tf_op jit(solution)/shard_map/ppermute | solution.py:33
  95.0 13.6 %collective-permute-start.16 = (bf16[2,2,16,32,128]{4,3,2,1,0:T(8,128)(2,1)S(1)}, bf16[2,2,16,32,128]{4,3,2,1,0:T(8,128)(2,1)S(1)}, u32[]{:S(2)}, u32[]{:S(2)}) collective-permute-start(bf16[2,2,16,32,128]{4,3,2,1,0:T(8,128)(2,1)S(1)} %after.5.own), channel_id=1, source_target_pairs={{0,32},{1,33},{2,34},{3,35},{4,36},{5,37},{6,38},{7,39},{8,40},{9,... | collective-permute-start | bytes 1572872 | tf_op jit(solution)/shard_map/ppermute | solution.py:33
  95.1 14.9 %collective-permute-start.17 = (bf16[2,2,16,32,128]{4,3,2,1,0:T(8,128)(2,1)S(1)}, bf16[2,2,16,32,128]{4,3,2,1,0:T(8,128)(2,1)S(1)}, u32[]{:S(2)}, u32[]{:S(2)}) collective-permute-start(bf16[2,2,16,32,128]{4,3,2,1,0:T(8,128)(2,1)S(1)} %after.5.own), channel_id=1, source_target_pairs={{0,96},{1,97},{2,98},{3,99},{4,100},{5,101},{6,102},{7,103},{8,104... | collective-permute-start | bytes 1572872 | tf_op jit(solution)/shard_map/ppermute | solution.py:33
  97.8 15.2 %collective-permute-start.5 = (bf16[2,1,16,32,128]{4,3,2,1,0:T(8,128)(2,1)S(1)}, bf16[2,1,16,32,128]{4,3,2,1,0:T(8,128)(2,1)S(1)}, u32[]{:S(2)}, u32[]{:S(2)}) collective-permute-start(bf16[2,1,16,32,128]{4,3,2,1,0:T(8,128)(2,1)S(1)} %slice.42), channel_id=1, source_target_pairs={{0,32},{1,33},{2,34},{3,35},{4,36},{5,37},{6,38},{7,39},{8,40},{9,... | collective-permute-start | bytes 786440 | tf_op jit(solution)/shard_map/ppermute | solution.py:33
  105.2 16.9 %collective-permute-start.13 = (bf16[2,2,16,32,128]{4,3,2,1,0:T(8,128)(2,1)}, bf16[2,2,16,32,128]{4,3,2,1,0:T(8,128)(2,1)S(1)}, u32[]{:S(2)}, u32[]{:S(2)}) collective-permute-start(bf16[2,2,16,32,128]{4,3,2,1,0:T(8,128)(2,1)} %collective-permute-done.11.refs_4_), channel_id=1, source_target_pairs={{0,1},{1,2},{2,3},{3,4},{4,5},{5,6},{6,7},{7,0},{8,9},{9,10},{10,1... | collective-permute-start | bytes 1572872 | tf_op jit(solution)/shard_map/ppermute | solution.py:33
  105.2 16.9 %collective-permute-start.14 = (bf16[2,2,16,32,128]{4,3,2,1,0:T(8,128)(2,1)}, bf16[2,2,16,32,128]{4,3,2,1,0:T(8,128)(2,1)}, u32[]{:S(2)}, u32[]{:S(2)}) collective-permute-start(bf16[2,2,16,32,128]{4,3,2,1,0:T(8,128)(2,1)} %collective-permute-done.12.refs_5_), channel_id=1, source_target_pairs={{0,7},{1,0},{2,1},{3,2},{4,3},{5,4},{6,5},{7,6},{8,15},{9,8},{10,9... | collective-permute-start | bytes 1572872 | tf_op jit(solution)/shard_map/ppermute | solution.py:33
  108.5 5.8 %collective-permute-start.6 = (bf16[2,1,16,32,128]{4,3,2,1,0:T(8,128)(2,1)}, bf16[2,1,16,32,128]{4,3,2,1,0:T(8,128)(2,1)}, u32[]{:S(2)}, u32[]{:S(2)}) collective-permute-start(bf16[2,1,16,32,128]{4,3,2,1,0:T(8,128)(2,1)} %slice.43), channel_id=1, source_target_pairs={{0,96},{1,97},{2,98},{3,99},{4,100},{5,101},{6,102},{7,103},{8,104... | collective-permute-start | bytes 786440 | tf_op jit(solution)/shard_map/ppermute | solution.py:33
  110.0 8.6 %collective-permute-start.18 = (bf16[2,1,16,32,128]{4,3,2,1,0:T(8,128)(2,1)}, bf16[2,1,16,32,128]{4,3,2,1,0:T(8,128)(2,1)}, u32[]{:S(2)}, u32[]{:S(2)}) collective-permute-start(bf16[2,1,16,32,128]{4,3,2,1,0:T(8,128)(2,1)} %slice.44), channel_id=1, source_target_pairs={{0,32},{1,33},{2,34},{3,35},{4,36},{5,37},{6,38},{7,39},{8,40},{9,... | collective-permute-start | bytes 786440 | tf_op jit(solution)/shard_map/ppermute | solution.py:33
  112.9 7.7 %collective-permute-start.19 = (bf16[2,1,16,32,128]{4,3,2,1,0:T(8,128)(2,1)}, bf16[2,1,16,32,128]{4,3,2,1,0:T(8,128)(2,1)}, u32[]{:S(2)}, u32[]{:S(2)}) collective-permute-start(bf16[2,1,16,32,128]{4,3,2,1,0:T(8,128)(2,1)} %slice.45), channel_id=1, source_target_pairs={{0,96},{1,97},{2,98},{3,99},{4,100},{5,101},{6,102},{7,103},{8,104... | collective-permute-start | bytes 786440 | tf_op jit(solution)/shard_map/ppermute | solution.py:33
  126.2 6.4 %collective-permute-start.21 = (f32[1,448,512]{2,1,0:T(8,128)S(1)}, f32[1,448,512]{2,1,0:T(8,128)S(1)}, u32[]{:S(2)}, u32[]{:S(2)}) collective-permute-start(f32[1,448,512]{2,1,0:T(8,128)S(1)} %get-tuple-element.22), channel_id=1, source_target_pairs={{0,16},{1,17},{2,18},{3,19},{4,20},{5,21},{6,22},{7,23},{8,24},{9,... | collective-permute-start | bytes 2752520 | tf_op jit(solution)/shard_map/ppermute | solution.py:33
  132.5 25.2 %collective-permute-start.20 = (f32[1,448,512]{2,1,0:T(8,128)S(1)}, f32[1,448,512]{2,1,0:T(8,128)S(1)}, u32[]{:S(2)}, u32[]{:S(2)}) collective-permute-start(f32[1,448,512]{2,1,0:T(8,128)S(1)} %get-tuple-element.20), channel_id=1, source_target_pairs={{0,16},{1,17},{2,18},{3,19},{4,20},{5,21},{6,22},{7,23},{8,24},{9,... | collective-permute-start | bytes 2752520 | tf_op jit(solution)/shard_map/ppermute | solution.py:33
  132.8 24.9 %collective-permute-start.22 = (f32[448,512]{1,0:T(8,128)S(1)}, f32[448,512]{1,0:T(8,128)S(1)}, u32[]{:S(2)}, u32[]{:S(2)}) collective-permute-start(f32[448,512]{1,0:T(8,128)S(1)} %add_bitcast_fusion), channel_id=1, source_target_pairs={{0,8},{1,9},{2,10},{3,11},{4,12},{5,13},{6,14},{7,15},{8,0},{9,1},... | collective-permute-start | bytes 2752520 | tf_op jit(solution)/shard_map/ppermute | solution.py:33
  134.6 8.4 %collective-permute-start.23 = (bf16[1,2,16,32,128]{4,3,2,1,0:T(8,128)(2,1)S(1)}, bf16[1,2,16,32,128]{4,3,2,1,0:T(8,128)(2,1)S(1)}, u32[]{:S(2)}, u32[]{:S(2)}) collective-permute-start(bf16[1,2,16,32,128]{4,3,2,1,0:T(8,128)(2,1)S(1)} %slice.46), channel_id=1, source_target_pairs={{0,1},{1,2},{2,3},{3,4},{4,5},{5,6},{6,7},{7,0},{8,9},{9,10},{10,1... | collective-permute-start | bytes 786440 | tf_op jit(solution)/shard_map/ppermute | solution.py:33
  135.7 7.5 %collective-permute-start.24 = (bf16[1,2,16,32,128]{4,3,2,1,0:T(8,128)(2,1)S(1)}, bf16[1,2,16,32,128]{4,3,2,1,0:T(8,128)(2,1)S(1)}, u32[]{:S(2)}, u32[]{:S(2)}) collective-permute-start(bf16[1,2,16,32,128]{4,3,2,1,0:T(8,128)(2,1)S(1)} %slice.47), channel_id=1, source_target_pairs={{0,7},{1,0},{2,1},{3,2},{4,3},{5,4},{6,5},{7,6},{8,15},{9,8},{10,9... | collective-permute-start | bytes 786440 | tf_op jit(solution)/shard_map/ppermute | solution.py:33
  145.9 3.1 %collective-permute-start.25 = (f32[2,64,512]{2,1,0:T(8,128)S(1)}, f32[2,64,512]{2,1,0:T(8,128)S(1)}, u32[]{:S(2)}, u32[]{:S(2)}) collective-permute-start(f32[2,64,512]{2,1,0:T(8,128)S(1)} %get-tuple-element.24), channel_id=1, source_target_pairs={{0,16},{1,17},{2,18},{3,19},{4,20},{5,21},{6,22},{7,23},{8,24},{9,... | collective-permute-start | bytes 786440 | tf_op jit(solution)/shard_map/ppermute | solution.py:33
  149.1 8.6 %collective-permute-start.26 = (f32[64,512]{1,0:T(8,128)S(1)}, f32[64,512]{1,0:T(8,128)S(1)}, u32[]{:S(2)}, u32[]{:S(2)}) collective-permute-start(f32[64,512]{1,0:T(8,128)S(1)} %fusion), channel_id=1, source_target_pairs={{0,8},{1,9},{2,10},{3,11},{4,12},{5,13},{6,14},{7,15},{8,0},{9,1},... | collective-permute-start | bytes 393224 | tf_op jit(solution)/shard_map/ppermute | solution.py:33
  (11 other events, 152.1 us)
